TPU v7x, 32 devices: a whole 2x2x4 slice. The times are simulated.
32 devices in a mesh: replica: 2 (over core), fsdp: 4 (over y, x), tensor: 4 (over z).
Axes of the slice: x: 2, y: 2, z: 4, core: 2. Of those that a mesh axis runs over, the one named last changes fastest.
Arguments:
- layer_input: bfloat16 [2, 2048, 2048], P('replica', 'fsdp'), may hold values from -6 to 6
- block_order: int32 [2, 4], P('replica'), may hold values from 0 to 3, each once within a row
- first_gain: bfloat16 [2048], replicated, may hold values from 0.099609375 to 1.8984375
- first_bias: bfloat16 [2048], replicated, may hold values from -1.75 to 1.75
- second_gain: bfloat16 [2048], replicated, may hold values from 0.099609375 to 1.8984375
- second_bias: bfloat16 [2048], replicated, may hold values from -1.75 to 1.75
- heads_weight: bfloat16 [2048, 8, 768], P('fsdp', 'tensor'), may hold values from -0.125 to 0.125
- heads_bias: bfloat16 [8, 768], P('tensor'), may hold values from -1.75 to 1.75
- output_weight: bfloat16 [8, 256, 2048], P('tensor', None, 'fsdp'), may hold values from -1 to 1
- output_bias: bfloat16 [2048], replicated, may hold values from -1.75 to 1.75
- expand_weight: bfloat16 [2048, 8192], P('fsdp', 'tensor'), may hold values from -0.125 to 0.125
- expand_bias: bfloat16 [8192], P('tensor'), may hold values from -1.75 to 1.75
- shrink_weight: bfloat16 [8192, 2048], P('tensor', 'fsdp'), may hold values from -0.0625 to 0.0625
- shrink_bias: bfloat16 [2048], replicated, may hold values from -1.75 to 1.75
- cotangent: bfloat16 [2, 2048, 2048], P('replica', 'fsdp'), may hold values from -8 to 8
Outputs:
- layer_output: bfloat16 [2, 2048, 2048], P('replica', 'fsdp')
- input_grad: float32 [2, 2048, 2048], P('replica', 'fsdp')
- first_gain_grad: float32 [2048], replicated
- first_bias_grad: float32 [2048], replicated
- second_gain_grad: float32 [2048], replicated
- second_bias_grad: float32 [2048], replicated
- heads_weight_grad: float32 [2048, 8, 768], P('fsdp', 'tensor')
- heads_bias_grad: float32 [8, 768], P('tensor')
- output_weight_grad: float32 [8, 256, 2048], P('tensor', None, 'fsdp')
- output_bias_grad: float32 [2048], replicated
- expand_weight_grad: float32 [2048, 8192], P('fsdp', 'tensor')
- expand_bias_grad: float32 [8192], P('tensor')
- shrink_weight_grad: float32 [8192, 2048], P('tensor', 'fsdp')
- shrink_bias_grad: float32 [2048], replicated
Inputs may be any that keep to these rules, and one draw needn't show every extreme that they name: `block_order`: row s lists, for each of the 4 devices of sequence s's group in order, which block of 512 consecutive positions that device holds; every row is a permutation.
All inputs are finite; a program needn't handle non-finite values.
Results may differ from a plain program's by a relative error of at most 0.01.
Values may be sent and summed in bfloat16 or wider, within the bound.
A program may use at most 256 MiB of HBM per device.

v0:
```python
import jax
import jax.numpy as jnp
from jax import lax
from jax.sharding import PartitionSpec as P

ROT = 64


NORM_EPS = 1e-05
MASKED = -1e30


def layer_norm(values_in, gain_vec, shift_vec):
    average = jnp.mean(values_in, -1, keepdims=True)
    centred = values_in - average
    spread_sq = jnp.mean(centred * centred, -1, keepdims=True)
    return centred * lax.rsqrt(spread_sq + NORM_EPS) * gain_vec + shift_vec


def rotate(values_in, cosine, sine_part):
    rot_width = cosine.shape[-1]
    half_width = rot_width // 2
    turning = values_in[..., :rot_width]
    swapped = jnp.concatenate([-turning[..., half_width:], turning[..., :half_width]], -1)
    return jnp.concatenate([turning * cosine + swapped * sine_part, values_in[..., rot_width:]], -1)


def rotary_tables(positions, rot_width):
    frequency = jnp.power(10000.0, -jnp.arange(0, rot_width, 2, dtype=jnp.float32) / rot_width)
    angle_half = positions.astype(jnp.float32)[:, None] * frequency[None, :]
    angles = jnp.concatenate([angle_half, angle_half], -1)
    return (jnp.cos(angles), jnp.sin(angles))


def contract_last(left_op, right_op):
    return lax.dot_general(
        left_op, right_op, (((1,), (1,)), ((), ())), preferred_element_type=jnp.float32
    )


def contract_first(left_op, right_op):
    return lax.dot_general(
        left_op, right_op, (((0,), (0,)), ((), ())), preferred_element_type=jnp.float32
    )


def softmax_rows(scores, allowed):
    masked_scores = jnp.where(allowed, scores, MASKED)
    row_top = jnp.max(masked_scores, -1, keepdims=True)
    exponent = jnp.exp(masked_scores - row_top)
    return exponent / jnp.sum(exponent, -1, keepdims=True)


def local(
    layer_input,
    block_order,
    first_gain,
    first_bias,
    second_gain,
    second_bias,
    heads_weight,
    heads_bias,
    output_weight,
    output_bias,
    expand_weight,
    expand_bias,
    shrink_weight,
    shrink_bias,
    cotangent,
):
    tokens_here = layer_input.shape[1]
    fsdp_count = lax.axis_size("fsdp")
    head_dim = output_weight.shape[1]
    score_scale = head_dim ** (-0.5)
    order_row = block_order[0]
    device_slot = lax.axis_index("fsdp")
    own_block = jnp.sum(
        jnp.where(jnp.arange(fsdp_count, dtype=jnp.int32) == device_slot, order_row, 0)
    )
    offsets = jnp.arange(tokens_here, dtype=jnp.int32)
    query_pos = own_block * tokens_here + offsets
    key_pos = jnp.repeat(order_row, tokens_here) * tokens_here + jnp.tile(offsets, fsdp_count)
    allowed = key_pos[None, :] <= query_pos[:, None]
    cosine, sine_part = rotary_tables(query_pos, ROT)
    hidden_in = layer_input[0].astype(jnp.float32)
    gain_one = first_gain.astype(jnp.float32)
    shift_one = first_bias.astype(jnp.float32)
    gain_two = second_gain.astype(jnp.float32)
    shift_two = second_bias.astype(jnp.float32)
    norm_one_low = layer_norm(hidden_in, gain_one, shift_one).astype(jnp.bfloat16)
    norm_two_low = layer_norm(hidden_in, gain_two, shift_two).astype(jnp.bfloat16)
    heads_full, output_full, expand_full, shrink_full = (
        lax.all_gather(heads_weight, "fsdp", axis=0, tiled=True),
        lax.all_gather(output_weight, "fsdp", axis=2, tiled=True),
        lax.all_gather(expand_weight, "fsdp", axis=0, tiled=True),
        lax.all_gather(shrink_weight, "fsdp", axis=1, tiled=True),
    )
    projected = jnp.einsum(
        "td,dhe->hte", norm_one_low, heads_full, preferred_element_type=jnp.float32
    )
    projected = projected + heads_bias.astype(jnp.float32)[:, None, :]
    query_pre = projected[..., :head_dim]
    key_pre = projected[..., head_dim : 2 * head_dim]
    query_low = rotate(query_pre, cosine, sine_part).astype(jnp.bfloat16)
    key_low = rotate(key_pre, cosine, sine_part).astype(jnp.bfloat16)
    value_low = projected[..., 2 * head_dim :].astype(jnp.bfloat16)
    key_all, value_all = (
        lax.all_gather(key_low, "fsdp", axis=1, tiled=True),
        lax.all_gather(value_low, "fsdp", axis=1, tiled=True),
    )

    def attend_head(operands):
        query_head, key_head, value_head = operands
        probability = softmax_rows(contract_last(query_head, key_head) * score_scale, allowed)
        return jnp.dot(
            probability.astype(jnp.bfloat16), value_head, preferred_element_type=jnp.float32
        )

    context = lax.map(attend_head, (query_low, key_all, value_all))
    context_low = context.astype(jnp.bfloat16)
    expand_in = jnp.dot(
        norm_two_low, expand_full, preferred_element_type=jnp.float32
    ) + expand_bias.astype(jnp.float32)
    activation_low = jax.nn.gelu(expand_in, approximate=False).astype(jnp.bfloat16)
    branch_part = jnp.einsum(
        "hte,hed->td", context_low, output_full, preferred_element_type=jnp.float32
    )
    branch_part = branch_part + jnp.dot(
        activation_low, shrink_full, preferred_element_type=jnp.float32
    )
    branch = lax.psum(branch_part, "tensor")
    layer_output = (
        hidden_in + branch + output_bias.astype(jnp.float32) + shrink_bias.astype(jnp.float32)
    ).astype(jnp.bfloat16)[None]
    heads_back, output_back, expand_back, shrink_back = (
        lax.all_gather(heads_weight, "fsdp", axis=0, tiled=True),
        lax.all_gather(output_weight, "fsdp", axis=2, tiled=True),
        lax.all_gather(expand_weight, "fsdp", axis=0, tiled=True),
        lax.all_gather(shrink_weight, "fsdp", axis=1, tiled=True),
    )
    key_back, value_back = (
        lax.all_gather(key_low, "fsdp", axis=1, tiled=True),
        lax.all_gather(value_low, "fsdp", axis=1, tiled=True),
    )
    grad_out = cotangent[0]
    grad_float = grad_out.astype(jnp.float32)
    output_weight_grad = jnp.einsum(
        "hte,td->hed", context_low, grad_out, preferred_element_type=jnp.float32
    )
    shrink_weight_grad = contract_first(activation_low, grad_out)
    bias_total = jnp.sum(grad_float, 0)
    context_grad = jnp.einsum(
        "td,hed->hte", grad_out, output_back, preferred_element_type=jnp.float32
    ).astype(jnp.bfloat16)
    activation_grad = contract_last(grad_out, shrink_back)
    _, gelu_back = jax.vjp(lambda inner_val: jax.nn.gelu(inner_val, approximate=False), expand_in)
    expand_grad = gelu_back(activation_grad)[0].astype(jnp.bfloat16)
    expand_weight_grad = contract_first(norm_two_low, expand_grad)
    expand_bias_grad = jnp.sum(expand_grad.astype(jnp.float32), 0)
    norm_two_grad = contract_last(expand_grad, expand_back)

    def attend_back(operands):
        query_head, key_head, value_head, context_head = operands
        probability = softmax_rows(contract_last(query_head, key_head) * score_scale, allowed)
        prob_low = probability.astype(jnp.bfloat16)
        weight_grad = contract_last(context_head, value_head)
        row_inner = jnp.sum(probability * weight_grad, -1, keepdims=True)
        score_grad = (probability * (weight_grad - row_inner)).astype(jnp.bfloat16)
        query_grad = jnp.dot(score_grad, key_head, preferred_element_type=jnp.float32) * score_scale
        key_grad = contract_first(score_grad, query_head) * score_scale
        value_grad = contract_first(prob_low, context_head)
        return (query_grad, key_grad, value_grad)

    query_grad, key_grad_all, value_grad_all = lax.map(
        attend_back, (query_low, key_back, value_back, context_grad)
    )
    key_grad, value_grad = (
        lax.psum_scatter(key_grad_all, "fsdp", scatter_dimension=1, tiled=True),
        lax.psum_scatter(value_grad_all, "fsdp", scatter_dimension=1, tiled=True),
    )
    _, rotate_back = jax.vjp(lambda inner_val: rotate(inner_val, cosine, sine_part), query_pre)
    projected_grad = jnp.concatenate(
        [rotate_back(query_grad)[0], rotate_back(key_grad)[0], value_grad], -1
    ).astype(jnp.bfloat16)
    heads_weight_grad = jnp.einsum(
        "td,hte->dhe", norm_one_low, projected_grad, preferred_element_type=jnp.float32
    )
    heads_bias_grad = jnp.sum(projected_grad.astype(jnp.float32), 1)
    norm_one_grad = jnp.einsum(
        "hte,dhe->td", projected_grad, heads_back, preferred_element_type=jnp.float32
    )
    norm_one_grad, norm_two_grad = lax.psum((norm_one_grad, norm_two_grad), "tensor")
    _, first_back = jax.vjp(layer_norm, hidden_in, gain_one, shift_one)
    input_first, first_gain_grad, first_bias_grad = first_back(norm_one_grad)
    _, second_back = jax.vjp(layer_norm, hidden_in, gain_two, shift_two)
    input_second, second_gain_grad, second_bias_grad = second_back(norm_two_grad)
    input_grad = (grad_float + input_first + input_second)[None]
    small_sums = lax.psum(
        (
            first_gain_grad,
            first_bias_grad,
            second_gain_grad,
            second_bias_grad,
            bias_total,
            expand_bias_grad,
            heads_bias_grad,
        ),
        ("replica", "fsdp"),
    )
    shard_parts = (
        lax.psum_scatter(heads_weight_grad, "fsdp", scatter_dimension=0, tiled=True),
        lax.psum_scatter(output_weight_grad, "fsdp", scatter_dimension=2, tiled=True),
        lax.psum_scatter(expand_weight_grad, "fsdp", scatter_dimension=0, tiled=True),
        lax.psum_scatter(shrink_weight_grad, "fsdp", scatter_dimension=1, tiled=True),
    )
    reduced = lax.psum((shard_parts[0], shard_parts[1], shard_parts[2], shard_parts[3]), "replica")
    return (
        layer_output,
        input_grad,
        small_sums[0],
        small_sums[1],
        small_sums[2],
        small_sums[3],
        reduced[0],
        small_sums[6],
        reduced[1],
        small_sums[4],
        reduced[2],
        small_sums[5],
        reduced[3],
        small_sums[4],
    )


def solution(mesh):
    placed = (
        P("replica", "fsdp", None),
        P("replica", None),
        P(),
        P(),
        P(),
        P(),
        P("fsdp", "tensor", None),
        P("tensor", None),
        P("tensor", None, "fsdp"),
        P(),
        P("fsdp", "tensor"),
        P("tensor"),
        P("tensor", "fsdp"),
        P(),
        P("replica", "fsdp", None),
    )
    return jax.shard_map(
        local,
        mesh=mesh,
        in_specs=placed,
        out_specs=(
            P("replica", "fsdp", None),
            P("replica", "fsdp", None),
            P(),
            P(),
            P(),
            P(),
            P("fsdp", "tensor", None),
            P("tensor", None),
            P("tensor", None, "fsdp"),
            P(),
            P("fsdp", "tensor"),
            P("tensor"),
            P("tensor", "fsdp"),
            P(),
        ),
        check_vma=False,
    )
```

profile of v0, /device:TPU:0, one launch (start us, length us, event | category | flops | bytes accessed | tf_op | source)
XLA Modules:
  0.0 1483.9 jit_solution(10723808795782699004)
XLA Ops:
  7.3 2.9 copy.29
  12.5 1.1 fusion.102
  15.4 68.0 %all-gather.7.cloned.1.call-done = bf16[2048,2,768]{2,0,1:T(8,128)(2,1)} async-done(((bf16[512,2,768]{2,0,1:T(8,128)(2,1)}), bf16[2048,2,768]{2,0,1:T(8,128)(2,1)}) %all-gather.7.cloned.1.call-update) | async-done | bytes 6291472 | tf_op jit(solution)/shard_map/all_gather | solution.py:93
  83.4 6.3 fusion.123
  89.8 1.3 fusion.120
  91.9 1.1 pad_maximum_fusion.2
  93.0 1.9 slice.57
  96.8 23.6 %all-gather.13.cloned.1.call-done = bf16[2,256,2048]{2,1,0:T(8,128)(2,1)} async-done(((bf16[2,256,512]{2,1,0:T(8,128)(2,1)}), bf16[2,256,2048]{2,1,0:T(8,128)(2,1)}) %all-gather.13.cloned.1.call-update) | async-done | bytes 2097168 | tf_op jit(solution)/shard_map/all_gather | solution.py:94
  120.4 3.7 fusion.92
  124.4 33.7 %all-gather.9.cloned.1.call-done = bf16[2,2048,256]{2,1,0:T(8,128)(2,1)} async-done(((bf16[2,512,256]{2,1,0:T(8,128)(2,1)}), bf16[2,2048,256]{2,1,0:T(8,128)(2,1)}) %all-gather.9.cloned.1.call-update) | async-done | bytes 2097168 | tf_op jit(solution)/shard_map/all_gather | solution.py:108
  158.2 37.6 %all-gather.11.cloned.1.call-done = bf16[2,2048,256]{2,1,0:T(8,128)(2,1)} async-done(((bf16[2,512,256]{2,1,0:T(8,128)(2,1)}), bf16[2,2048,256]{2,1,0:T(8,128)(2,1)}) %all-gather.11.cloned.1.call-update) | async-done | bytes 2097168 | tf_op jit(solution)/shard_map/all_gather | solution.py:109
  195.8 28.5 %while.29 = (s32[]{:T(128)}, f32[2,512,256]{2,1,0:T(8,128)S(1)}, f32[2,2048,256]{2,1,0:T(8,128)}, f32[2,2048,256]{2,1,0:T(8,128)}, bf16[2,512,256]{2,1,0:T(8,128...) while((s32[]{:T(128)}, f32[2,512,256]{2,1,0:T(8,128)S(1)}, ...), condition=%wide.region_12.13_spmd.clone.clone, body=%wide.region_8.12_spmd.clone.sunk.clone | while | flops 2703882752 | bytes 130585904 | solution.py:174
  195.8 2.1 fusion.182
  199.6 1.5 multiply_reduce_fusion.3
  201.2 1.4 multiply_convert_fusion.4
  204.8 2.5 copy-done.10
  207.3 1.4 fusion.186
  208.8 2.1 copy-done.11
  210.8 2.1 fusion.182
  214.6 1.5 multiply_reduce_fusion.3
  216.2 1.4 multiply_convert_fusion.4
  219.8 1.0 copy-done.10
  220.8 1.4 fusion.186
  222.3 2.1 copy-done.11
  225.3 9.3 while.28
  225.3 2.1 fusion.173
  228.2 0.9 copy-done.52
  230.0 2.1 fusion.173
  234.7 5.5 fusion.79
  240.5 44.7 %all-gather.15.cloned.1.call-done = bf16[2048,2048]{1,0:T(8,128)(2,1)} async-done(((bf16[512,2048]{1,0:T(8,128)(2,1)}), bf16[2048,2048]{1,0:T(8,128)(2,1)}) %all-gather.15.cloned.1.call-update) | async-done | bytes 8388624 | tf_op jit(solution)/shard_map/all_gather | solution.py:95
  285.1 17.9 %multiply_convert_fusion.1 = (bf16[512,2048]{1,0:T(8,128)(2,1)}, f32[512,2048]{1,0:T(8,128)}, f32[512,2048]{1,0:T(8,128)}) fusion(f32[2048]{0:T(1024)S(1)} %convert_element_type.94, bf16[2048,2048]{1,0:T(8,128)(2,1)} %all-gather.15.cloned.1.call-done, bf16[1,512,2048]{2,1,0:T(8,128)(2,1)S(1)} %copy-done.1, f32[2048]{0:T(1024)S(1)} %convert_element_type.92, ...), kind=kOutput, calls=%fused_computation.89 | convolution fusion | flops 4370464768 | bytes 21000192 | tf_op jit(solution)/shard_map/dot_general | solution.py:121
  303.0 71.3 %all-gather.17.cloned.1.call-done = bf16[2048,2048]{1,0:T(8,128)(2,1)} async-done(((bf16[2048,512]{1,0:T(8,128)(2,1)}), bf16[2048,2048]{1,0:T(8,128)(2,1)}) %all-gather.17.cloned.1.call-update) | async-done | bytes 8388624 | tf_op jit(solution)/shard_map/all_gather | solution.py:96
  374.3 12.2 convert_reduce_fusion.2
  386.5 1.3 copy-done.54
  387.9 8.8 fusion.109
  396.7 12.6 fusion.85
  409.4 2.6 split.24
  412.0 18.1 %reduce-scatter.9.cloned.1.call-done = f32[2,512,256]{2,1,0:T(8,128)} async-done(((f32[2,2048,256]{2,1,0:T(8,128)}), f32[2,512,256]{2,1,0:T(8,128)}) %reduce-scatter.9.cloned.1.call-update) | async-done | bytes 1048592 | tf_op jit(solution)/shard_map/reduce_scatter | solution.py:179
  430.1 2.1 convert.27
  432.1 54.4 %reduce-scatter.7.cloned.1.call-done = f32[2,512,256]{2,1,0:T(8,128)} async-done(((f32[2,2048,256]{2,1,0:T(8,128)}), f32[2,512,256]{2,1,0:T(8,128)}) %reduce-scatter.7.cloned.1.call-update) | async-done | bytes 1048592 | tf_op jit(solution)/shard_map/reduce_scatter | solution.py:178
  486.6 1.7 split.34
  488.3 1.3 slice_multiply_fusion.3
  492.3 6.7 fusion.106
  499.1 8.2 fusion.124
  507.3 3.4 bitcast_add_fusion
  510.7 9.9 fusion.125
  520.6 5.0 convolution_bitcast_fusion.1
  525.7 16.5 %reduce-scatter.13.cloned.1.call-done = f32[2,256,512]{2,1,0:T(8,128)} async-done(((f32[2,256,2048]{2,1,0:T(8,128)}), f32[2,256,512]{2,1,0:T(8,128)}) %reduce-scatter.13.cloned.1.call-update) | async-done | bytes 1048592 | tf_op jit(solution)/shard_map/reduce_scatter | solution.py:212
  542.3 157.0 %reduce-scatter.15.cloned.1.call-done = f32[512,2048]{1,0:T(8,128)} async-done(((f32[2048,2048]{1,0:T(8,128)}), f32[512,2048]{1,0:T(8,128)}) %reduce-scatter.15.cloned.1.call-update) | async-done | bytes 4194320 | tf_op jit(solution)/shard_map/reduce_scatter | solution.py:213
  699.3 157.2 %reduce-scatter.17.cloned.1.call-done = f32[2048,512]{1,0:T(8,128)} async-done(((f32[2048,2048]{1,0:T(8,128)}), f32[2048,512]{1,0:T(8,128)}) %reduce-scatter.17.cloned.1.call-update) | async-done | bytes 4194320 | tf_op jit(solution)/shard_map/reduce_scatter | solution.py:214
  856.5 124.0 %reduce-scatter.11.cloned.1.call-done = f32[512,2,768]{2,0,1:T(8,128)} async-done(((f32[2048,2,768]{2,0,1:T(8,128)}), f32[512,2,768]{2,0,1:T(8,128)}) %reduce-scatter.11.cloned.1.call-update) | async-done | bytes 3145744 | tf_op jit(solution)/shard_map/reduce_scatter | solution.py:211
  981.2 1.3 convert_reduce_fusion.3
  982.5 429.7 %all-reduce.14.cloned.1.call-done = (f32[512,2048]{1,0:T(8,128)}, f32[512,2048]{1,0:T(8,128)}, f32[512,2048]{1,0:T(8,128)}) async-done(((f32[512,2048]{1,0:T(8,128)}, f32[512,2048]{1,0:T(8,128)}, f32[512,2048]{1,0:T(8,128)}), (f32[512,2048]{1,0:T(8,128)}, f32[512,2048]{1,0:T(8,128)}, f32[512,2048]{1,0:T(8,128)})) %all-reduce.14.cloned.1.call-update) | async-done | bytes 12582928 | tf_op jit(solution)/shard_map/psum | solution.py:131
  1412.2 4.6 fusion.116
  1416.9 1.3 copy-done.3
  1418.1 3.6 fusion.62
  1422.0 6.3 convert_reduce_fusion
  1428.3 28.7 %all-reduce.8 = (f32[2048]{0:T(1024)}, f32[2048]{0:T(1024)}, f32[2048]{0:T(1024)}, f32[2048]{0:T(1024)}, f32[2,768]{1,0:T(2,128)}, /*index=5*/f32[2048]{0:T(1024)S(1)}, f32[2048]{0:T(1024)}) all-reduce(f32[2048]{0:T(1024)S(1)} %get-tuple-element.174, ...), channel_id=1, replica_groups=mesh['replica'=2,'fsdp'=4,'tensor'=4] {'replica','fsdp'}, use_global_device_ids=true, to_apply=%region_22.23 | all-reduce | flops 13824 | bytes 110592 | tf_op jit(solution)/shard_map/psum | solution.py:198
  1457.0 6.8 all-reduce.16.cloned.1.call-done
  1463.8 6.1 copy.33
  1470.5 1.0 copy.71
  1471.5 2.1 copy.72
  1473.6 1.6 copy-done.6
  1475.2 2.0 copy.73
  (197 shorter events, 23.8 us)
Async XLA Ops:
  7.2 3.8 copy-start.48
  7.2 3.8 copy-start.41
  7.2 3.9 copy-start.42
  7.2 3.9 copy-start.49
  7.2 6.5 copy-start
  7.2 76.1 %all-gather.7.cloned.1.call-start = ((), (), s32[]{:S(2)}) async-start(), calls=%async_computation.6 | async-start | bytes 7864320 | tf_op jit(solution)/shard_map/all_gather | solution.py:93
  10.2 110.2 %all-gather.13.cloned.1.call-start = ((), (), s32[]{:S(2)}) async-start(), calls=%async_computation.9 | async-start | bytes 2621440 | tf_op jit(solution)/shard_map/all_gather | solution.py:94
  10.9 147.2 %all-gather.9.cloned.1.call-start = ((), (), s32[]{:S(2)}) async-start(), calls=%async_computation.7 | async-start | bytes 2621440 | tf_op jit(solution)/shard_map/all_gather | solution.py:108
  11.1 78.6 %copy-start.38 = (f32[2048]{0:T(1024)}, f32[2048]{0:T(1024)S(1)}, u32[]{:S(2)}) copy-start(f32[2048]{0:T(1024)S(1)} %convert_element_type.86) | copy-start | bytes 24580
  11.1 78.6 %copy-start.30 = (f32[2048]{0:T(1024)}, f32[2048]{0:T(1024)S(1)}, u32[]{:S(2)}) copy-start(f32[2048]{0:T(1024)S(1)} %convert_element_type.85) | copy-start | bytes 24580
  13.7 77.7 %copy-start.17 = (f32[512,64]{1,0:T(8,128)}, f32[512,64]{1,0:T(8,128)S(1)}, u32[]{:S(2)}) copy-start(f32[512,64]{1,0:T(8,128)S(1)} %get-tuple-element.252) | copy-start | bytes 393220
  13.7 77.7 %copy-start.19 = (f32[512,64]{1,0:T(8,128)}, f32[512,64]{1,0:T(8,128)S(1)}, u32[]{:S(2)}) copy-start(f32[512,64]{1,0:T(8,128)S(1)} %get-tuple-element.253) | copy-start | bytes 393220
  14.1 75.7 %copy-start.32 = (f32[512]{0:T(512)}, f32[512]{0:T(512)S(1)}, u32[]{:S(2)}) copy-start(f32[512]{0:T(512)S(1)} %broadcast_multiply_fusion.1) | copy-start | bytes 6148
  15.4 74.4 %copy-start.36 = (f32[512]{0:T(512)}, f32[512]{0:T(512)S(1)}, u32[]{:S(2)}) copy-start(f32[512]{0:T(512)S(1)} %fusion.103) | copy-start | bytes 6148
  89.7 2.1 copy-start.28
  91.9 28.5 %copy-start.4 = (bf16[1,512,2048]{2,1,0:T(8,128)(2,1)S(1)}, bf16[1,512,2048]{2,1,0:T(8,128)(2,1)}, u32[]{:S(2)}) copy-start(bf16[1,512,2048]{2,1,0:T(8,128)(2,1)} %param.33) | copy-start | bytes 6291460
  93.0 102.8 %all-gather.11.cloned.1.call-start = ((), (), s32[]{:S(2)}) async-start(), calls=%async_computation.8 | async-start | bytes 2621440 | tf_op jit(solution)/shard_map/all_gather | solution.py:109
  94.9 190.2 %all-gather.15.cloned.1.call-start = ((), (), s32[]{:S(2)}) async-start(), calls=%async_computation.10 | async-start | bytes 10485760 | tf_op jit(solution)/shard_map/all_gather | solution.py:95
  95.5 278.8 %all-gather.17.cloned.1.call-start = ((), (), s32[]{:S(2)}) async-start(), calls=%async_computation.11 | async-start | bytes 10485760 | tf_op jit(solution)/shard_map/all_gather | solution.py:96
  96.1 333.9 %reduce-scatter.9.cloned.1.call-start = ((), (), s32[]{:S(2)}) async-start(), calls=%async_computation.13 | async-start | bytes 5242880 | tf_op jit(solution)/shard_map/reduce_scatter | solution.py:179
  120.4 3.7 copy-start.22
  201.1 2.9 copy-start.8
  203.5 3.9 copy-start.10
  204.8 4.0 copy-start.9
  208.8 2.1 copy-start.11
  216.2 2.8 copy-start.8
  218.5 2.3 copy-start.10
  219.8 2.5 copy-start.9
  222.2 2.1 copy-start.11
  224.3 262.2 %reduce-scatter.7.cloned.1.call-start = ((), (), s32[]{:S(2)}) async-start(), calls=%async_computation.12 | async-start | bytes 5242880 | tf_op jit(solution)/shard_map/reduce_scatter | solution.py:178
  225.3 317.0 %reduce-scatter.13.cloned.1.call-start = ((), (), s32[]{:S(2)}) async-start(), calls=%async_computation.15 | async-start | bytes 5242880 | tf_op jit(solution)/shard_map/reduce_scatter | solution.py:212
  234.6 5.8 copy-start.43
  234.6 5.8 copy-start.44
  234.6 5.8 copy-start.45
  234.6 50.5 %copy-start.1 = (bf16[1,512,2048]{2,1,0:T(8,128)(2,1)S(1)}, bf16[1,512,2048]{2,1,0:T(8,128)(2,1)}, u32[]{:S(2)}) copy-start(bf16[1,512,2048]{2,1,0:T(8,128)(2,1)} %param.19) | copy-start | bytes 6291460
  234.7 50.5 %copy-start.33 = (f32[512]{0:T(512)S(1)}, f32[512]{0:T(512)}, u32[]{:S(2)}) copy-start(f32[512]{0:T(512)} %copy-done.32) | copy-start | bytes 6148
  234.7 50.5 %copy-start.37 = (f32[512]{0:T(512)S(1)}, f32[512]{0:T(512)}, u32[]{:S(2)}) copy-start(f32[512]{0:T(512)} %copy-done.36) | copy-start | bytes 6148
  240.2 459.1 %reduce-scatter.15.cloned.1.call-start = ((), (), s32[]{:S(2)}) async-start(), calls=%async_computation.16 | async-start | bytes 20971520 | tf_op jit(solution)/shard_map/reduce_scatter | solution.py:213
  396.6 459.8 %reduce-scatter.17.cloned.1.call-start = ((), (), s32[]{:S(2)}) async-start(), calls=%async_computation.17 | async-start | bytes 20971520 | tf_op jit(solution)/shard_map/reduce_scatter | solution.py:214
  409.3 79.0 %copy-start.20 = (f32[512,64]{1,0:T(8,128)S(1)}, f32[512,64]{1,0:T(8,128)}, u32[]{:S(2)}) copy-start(f32[512,64]{1,0:T(8,128)} %copy-done.19) | copy-start | bytes 393220
  409.3 571.2 %reduce-scatter.11.cloned.1.call-start = ((), (), s32[]{:S(2)}) async-start(), calls=%async_computation.14 | async-start | bytes 15728640 | tf_op jit(solution)/shard_map/reduce_scatter | solution.py:211
  432.1 57.8 %copy-start.18 = (f32[512,64]{1,0:T(8,128)S(1)}, f32[512,64]{1,0:T(8,128)}, u32[]{:S(2)}) copy-start(f32[512,64]{1,0:T(8,128)} %copy-done.17) | copy-start | bytes 393220
  486.6 3.4 copy-start.12
  486.6 3.4 copy-start.15
  490.0 2.3 copy-start.21
  490.0 2.3 copy-start.31
  490.0 2.3 copy-start.39
  499.0 913.2 %all-reduce.14.cloned.1.call-start = ((), (), s32[]{:S(2)}) async-start(), calls=%async_computation.18 | async-start | bytes 25165824 | tf_op jit(solution)/shard_map/psum | solution.py:131
  499.1 8.2 copy-start.27
  507.3 3.5 copy-start.55
  507.3 13.3 slice-start
  510.7 9.9 copy-start.24
  510.7 9.9 copy-start.26
  510.7 9.9 slice-start.1
  525.7 938.1 %all-reduce.16.cloned.1.call-start = ((), (), s32[]{:S(2)}) async-start(), calls=%async_computation.19 | async-start | bytes 25165824 | tf_op jit(solution)/shard_map/psum | solution.py:216
  1412.2 4.6 copy-start.35
  1412.2 4.7 copy-start.2
  1412.2 5.9 copy-start.3
  1418.1 3.6 copy-start.5
  1418.1 3.8 copy-start.16
  1457.0 14.5 copy-start.40
  1463.8 6.7 copy-start.29
  1463.8 7.7 copy-start.7
  1471.5 3.7 copy-start.6
  (16 other events, 20.0 us)
Sparse Core Ops, SparseCore 0:
  10.5 72.8 all-gather.6
  85.2 35.1 all-gather.12
  122.8 35.3 all-gather.8
  160.5 35.2 all-gather.10
  197.5 87.5 all-gather.14
  286.8 87.4 all-gather.16
  377.3 52.7 reduce-scatter.8
  433.9 52.6 reduce-scatter.6
  489.5 52.6 reduce-scatter.12
  545.5 153.7 reduce-scatter.14
  702.7 153.7 reduce-scatter.16
  859.7 120.6 reduce-scatter.10
  984.7 427.4 all-reduce.13
  1415.1 48.6 all-reduce.15
where the time goes:
time: 1490 us; the launch traced here: 1480 us
  waiting for transfers between devices  1250 us (84%)
  matrix products  119 us (8%)
  local copies, waits for them, and re-layouts  42.4 us (3%)
  other arithmetic  31.3 us (2%)
  blocking collectives  28.7 us (2%)
  between operations  15.4 us (1%)
    psum x1, waiting for transfers between devices, local(): branch = lax.psum(branch_part, 'tensor')  430 us
    reduce_scatter x1, waiting for transfers between devices, local(): lax.psum_scatter(shrink_weight_grad, 'fsdp', scatter_dimension=1, tiled=T...  157 us
    reduce_scatter x1, waiting for transfers between devices, local(): lax.psum_scatter(expand_weight_grad, 'fsdp', scatter_dimension=0, tiled=T...  157 us
    reduce_scatter x1, waiting for transfers between devices, local(): lax.psum_scatter(heads_weight_grad, 'fsdp', scatter_dimension=0, tiled=True)  124 us
    all_gather x1, waiting for transfers between devices, local(): lax.all_gather(shrink_weight, 'fsdp', axis=1, tiled=True)  71.3 us
    all_gather x1, waiting for transfers between devices, local(): lax.all_gather(heads_weight, 'fsdp', axis=0, tiled=True)  68 us
    reduce_scatter x1, waiting for transfers between devices, local(): lax.psum_scatter(key_grad_all, 'fsdp', scatter_dimension=1, tiled=True)  54.4 us
    all_gather x1, waiting for transfers between devices, local(): lax.all_gather(expand_weight, 'fsdp', axis=0, tiled=True)  44.7 us
  transfers between devices with their start and end apart: 14, of which 14 were waited for; matrix products, arithmetic and copies ran while one was open for 11% of the time, Pallas kernels for 0%

commit v1 on v0

--- a/solution.py
+++ b/solution.py
@@ -51,7 +51,254 @@
     return exponent / jnp.sum(exponent, -1, keepdims=True)
 
 
-def local(
+SWAP_X = ((0, 1), (1, 0), (2, 3), (3, 2))
+SWAP_Y = ((0, 2), (2, 0), (1, 3), (3, 1))
+SWAP_CORE = ((0, 1), (1, 0))
+LOW = jnp.bfloat16
+FULL = jnp.float32
+
+
+def to_x(part):
+    return lax.ppermute(part, "fsdp", SWAP_X)
+
+
+def to_y(part):
+    return lax.ppermute(part, "fsdp", SWAP_Y)
+
+
+def to_core(part):
+    return lax.ppermute(part, "replica", SWAP_CORE)
+
+
+def swap_if(flag, pair):
+    return jnp.where(flag, pair[::-1], pair)
+
+
+def turn(array, axis, r_bit, x_bit, y_bit):
+    shape = array.shape
+    cut = array.reshape(shape[:axis] + (2, 2, 2, shape[axis] // 8) + shape[axis + 1 :])
+    for at, bit in ((axis, y_bit), (axis + 1, x_bit), (axis + 2, r_bit)):
+        cut = jnp.where(bit, jnp.flip(cut, at), cut)
+    return cut.reshape(shape)
+
+
+def gather_blocks(own_half, other_half, axis):
+    from_x, from_y = to_x(own_half), to_y(own_half)
+    cut = own_half.shape[axis] // 2
+    far_one = to_y(lax.slice_in_dim(from_x, 0, cut, axis=axis))
+    far_two = to_x(lax.slice_in_dim(from_y, cut, 2 * cut, axis=axis))
+    far = jnp.concatenate([far_one, far_two], axis)
+    return jnp.concatenate(
+        [own_half, other_half, from_x, to_core(from_x), from_y, to_core(from_y), far, to_core(far)],
+        axis,
+    )
+
+
+def scatter_blocks(blocks, axis):
+    own, for_x, for_y, for_far = jnp.split(blocks, 4, axis)
+    cut = own.shape[axis] // 2
+    far_low = for_far.astype(LOW)
+    via_x = to_x(lax.slice_in_dim(far_low, 0, cut, axis=axis))
+    via_y = to_y(lax.slice_in_dim(far_low, cut, 2 * cut, axis=axis))
+    y_top = lax.slice_in_dim(for_y, 0, cut, axis=axis) + via_x.astype(FULL)
+    y_end = lax.slice_in_dim(for_y, cut, 2 * cut, axis=axis)
+    x_top = lax.slice_in_dim(for_x, 0, cut, axis=axis)
+    x_end = lax.slice_in_dim(for_x, cut, 2 * cut, axis=axis) + via_y.astype(FULL)
+    got_x = to_x(jnp.concatenate([x_top, x_end], axis).astype(LOW))
+    got_y = to_y(jnp.concatenate([y_top, y_end], axis).astype(LOW))
+    return own + got_x.astype(FULL) + got_y.astype(FULL)
+
+
+def halves_of(array, axis):
+    shape = array.shape
+    cut = array.reshape(shape[:axis] + (4, 2, shape[axis] // 8) + shape[axis + 1 :])
+    flat = shape[:axis] + (shape[axis] // 2,) + shape[axis + 1 :]
+    return [lax.index_in_dim(cut, h, axis + 1, keepdims=False).reshape(flat) for h in (0, 1)]
+
+
+def weight_grad(product, wide, axis, r_bit):
+    own_part, other_part = halves_of(wide, 1)
+    sent = product(other_part).astype(LOW)
+    blocks = product(own_part) + to_core(sent).astype(FULL)
+    half = scatter_blocks(blocks, axis)
+    pair = swap_if(r_bit, jnp.stack([half, to_core(half)]))
+    return jnp.concatenate([pair[0], pair[1]], axis)
+
+
+def square_local(
+    layer_input,
+    block_order,
+    first_gain,
+    first_bias,
+    second_gain,
+    second_bias,
+    heads_weight,
+    heads_bias,
+    output_weight,
+    output_bias,
+    expand_weight,
+    expand_bias,
+    shrink_weight,
+    shrink_bias,
+    cotangent,
+):
+    tokens = layer_input.shape[1]
+    width = layer_input.shape[2]
+    head_dim = output_weight.shape[1]
+    score_scale = head_dim ** (-0.5)
+    replica, fsdp = lax.axis_index("replica"), lax.axis_index("fsdp")
+    r_bit, x_bit, y_bit = replica == 1, fsdp % 2 == 1, fsdp // 2 == 1
+
+    def turned(array, axis):
+        return turn(array, axis, r_bit, x_bit, y_bit)
+
+    def chosen(pair):
+        swapped = swap_if(y_bit, pair)
+        return swapped[0], swapped[1]
+
+    heads_rows = heads_weight.reshape(heads_weight.shape[0], -1)
+    output_rows = output_weight.reshape(-1, output_weight.shape[2])
+
+    def halves(shard, axis):
+        pair = jnp.stack(jnp.split(shard, 2, axis))
+        swapped = swap_if(r_bit, pair)
+        return swapped[0], swapped[1]
+
+    heads_full = gather_blocks(*halves(heads_rows, 0), 0)
+    output_full = gather_blocks(*halves(output_rows, 1), 1)
+    expand_full = gather_blocks(*halves(expand_weight, 0), 0)
+    shrink_full = gather_blocks(*halves(shrink_weight, 1), 1)
+
+    hidden = turned(layer_input[0], 1).astype(FULL)
+    grad_out = turned(cotangent[0], 1)
+    gain_one, shift_one, gain_two, shift_two = (
+        turned(vec.astype(FULL), 0) for vec in (first_gain, first_bias, second_gain, second_bias)
+    )
+    average = jnp.mean(hidden, -1, keepdims=True)
+    centred = hidden - average
+    inverse = lax.rsqrt(jnp.mean(centred * centred, -1, keepdims=True) + NORM_EPS)
+    normal = centred * inverse
+    norm_one = (normal * gain_one + shift_one).astype(LOW)
+    norm_two = (normal * gain_two + shift_two).astype(LOW)
+
+    order_row = block_order[0]
+    slots = fsdp ^ jnp.array([0, 2, 1, 3], jnp.int32)
+    order_here = order_row[slots]
+    offsets = jnp.arange(tokens, dtype=jnp.int32)
+    key_pos = (order_here[:, None] * tokens + offsets[None]).reshape(-1)
+    query_pos = key_pos[: 2 * tokens]
+    cosine, sine_part = rotary_tables(query_pos, ROT)
+
+    projected = jnp.dot(norm_one, heads_full, preferred_element_type=FULL)
+    projected = projected + heads_bias.reshape(-1).astype(FULL)
+    projected = projected.reshape(tokens, 2, 3, head_dim).transpose(1, 2, 0, 3)
+    spun = rotate(projected[:, :2], cosine[:tokens], sine_part[:tokens])
+    qkv = jnp.concatenate([spun, projected[:, 2:]], 1).astype(LOW)
+    qkv_own, qkv_away = chosen(qkv)
+    qkv_y = to_y(qkv_away)
+    kv_x, kv_far = to_x(qkv_own[1:]), to_x(qkv_y[1:])
+    query = jnp.concatenate([qkv_own[0], qkv_y[0]], 0)
+    key, value = (
+        jnp.concatenate([qkv_own[i], qkv_y[i], kv_x[i - 1], kv_far[i - 1]], 0) for i in (1, 2)
+    )
+    context_grad = contract_last(grad_out, output_full).astype(LOW)
+    away_own = chosen(context_grad.reshape(tokens, 2, head_dim).transpose(1, 0, 2))
+    context_grad_here = jnp.concatenate([away_own[0], to_y(away_own[1])], 0)
+
+    allowed = key_pos[None, :] <= query_pos[:, None]
+    probability = softmax_rows(contract_last(query, key) * score_scale, allowed)
+    prob_low = probability.astype(LOW)
+    context_here = jnp.dot(prob_low, value, preferred_element_type=FULL).astype(LOW)
+    weight_part = contract_last(context_grad_here, value)
+    row_inner = jnp.sum(probability * weight_part, -1, keepdims=True)
+    score_grad = (probability * (weight_part - row_inner)).astype(LOW)
+    query_grad = jnp.dot(score_grad, key, preferred_element_type=FULL) * score_scale
+    key_grad = contract_first(score_grad, query) * score_scale
+    value_grad = contract_first(prob_low, context_grad_here)
+
+    context_back = to_y(context_here[tokens:])
+    context_low = swap_if(y_bit, jnp.stack([context_here[:tokens], context_back]))
+    context_rows = context_low.transpose(1, 0, 2).reshape(tokens, -1)
+
+    kv_grad = jnp.stack([key_grad, value_grad]).reshape(2, 2, 2 * tokens, head_dim)
+    kv_grad = kv_grad[:, 0] + to_x(kv_grad[:, 1].astype(LOW)).astype(FULL)
+    spun_grad = jnp.stack([query_grad, kv_grad[0]])
+    _, rotate_back = jax.vjp(
+        lambda inner: rotate(inner, cosine[None], sine_part[None]), jnp.zeros_like(spun_grad)
+    )
+    projected_grad = jnp.concatenate([rotate_back(spun_grad)[0], kv_grad[1:]], 0).astype(LOW)
+    projected_back = to_y(projected_grad[:, tokens:])
+    projected_grad = swap_if(y_bit, jnp.stack([projected_grad[:, :tokens], projected_back]))
+    projected_rows = projected_grad.transpose(2, 0, 1, 3).reshape(tokens, -1)
+    heads_bias_grad = jnp.sum(projected_rows.astype(FULL), 0)
+    norm_one_grad = contract_last(projected_rows, heads_full)
+
+    expand_in = jnp.dot(norm_two, expand_full, preferred_element_type=FULL) + expand_bias.astype(FULL)
+    activation = jax.nn.gelu(expand_in, approximate=False).astype(LOW)
+    _, gelu_back = jax.vjp(lambda inner: jax.nn.gelu(inner, approximate=False), expand_in)
+    branch = jnp.dot(context_rows, output_full, preferred_element_type=FULL) + jnp.dot(
+        activation, shrink_full, preferred_element_type=FULL
+    )
+    branch = lax.psum(branch.astype(LOW), "tensor").astype(FULL)
+    both_biases = turned(output_bias.astype(FULL) + shrink_bias.astype(FULL), 0)
+    layer_output = turned((hidden + branch + both_biases).astype(LOW), 1)[None]
+    expand_grad = gelu_back(contract_last(grad_out, shrink_full))[0].astype(LOW)
+    expand_bias_grad = jnp.sum(expand_grad.astype(FULL), 0)
+    norm_two_grad = contract_last(expand_grad, expand_full)
+
+    upstream = norm_one_grad * gain_one + norm_two_grad * gain_two
+    upstream = lax.psum(upstream.astype(LOW), "tensor").astype(FULL)
+    input_part = inverse * (
+        upstream
+        - jnp.mean(upstream, -1, keepdims=True)
+        - normal * jnp.mean(upstream * normal, -1, keepdims=True)
+    )
+    input_grad = turned(grad_out.astype(FULL) + input_part, 1)[None]
+
+    gains = jnp.stack(
+        [
+            jnp.sum(norm_one_grad * normal, 0),
+            jnp.sum(norm_one_grad, 0),
+            jnp.sum(norm_two_grad * normal, 0),
+            jnp.sum(norm_two_grad, 0),
+        ]
+    )
+    gains = lax.psum(turned(gains, 1), ("replica", "fsdp", "tensor"))
+    bias_total, expand_bias_grad, heads_bias_grad = lax.psum(
+        (jnp.sum(cotangent[0].astype(FULL), 0), expand_bias_grad, heads_bias_grad),
+        ("replica", "fsdp"),
+    )
+
+    def by_rows(left, right, axis_out, r_flag):
+        return weight_grad(lambda part: contract_first(part, right), left, axis_out, r_flag)
+
+    heads_weight_grad = by_rows(norm_one, projected_rows, 0, r_bit)
+    expand_weight_grad = by_rows(norm_two, expand_grad, 0, r_bit)
+    output_weight_grad = weight_grad(
+        lambda part: contract_first(context_rows, part), grad_out, 1, r_bit
+    )
+    shrink_weight_grad = weight_grad(
+        lambda part: contract_first(activation, part), grad_out, 1, r_bit
+    )
+    return (
+        layer_output,
+        input_grad,
+        gains[0],
+        gains[1],
+        gains[2],
+        gains[3],
+        heads_weight_grad.reshape(heads_weight.shape),
+        heads_bias_grad.reshape(heads_bias.shape),
+        output_weight_grad.reshape(output_weight.shape),
+        bias_total,
+        expand_weight_grad,
+        expand_bias_grad,
+        shrink_weight_grad,
+        bias_total,
+    )
+
+
+def ring_local(
     layer_input,
     block_order,
     first_gain,
@@ -250,6 +497,7 @@
         P(),
         P("replica", "fsdp", None),
     )
+    local = square_local if mesh.shape["fsdp"] == 4 and mesh.shape["replica"] == 2 else ring_local
     return jax.shard_map(
         local,
         mesh=mesh,

time: 1490 us -> 862 us (0.58)
  waiting for transfers between devices: 1250 us -> 240 us
  local copies, waits for them, and re-layouts: 42.4 us -> 242 us
  other arithmetic: 31.3 us -> 138 us
  blocking collectives: 28.7 us -> 67.2 us
  starting transfers between devices: 1.23 us -> 37.4 us
    reduce_scatter x6 -> x0, waiting for transfers between devices: 527 us -> none  [the longest x1 157 us: local(): lax.psum_scatter(shrink_weight_grad, 'fsdp', scatter_dimension=1, tiled=T...]
    psum x2 -> x1, waiting for transfers between devices: 437 us -> 66 us  [square_local(): branch = lax.psum(branch.astype(LOW), 'tensor').astype(FULL)]
    all_gather x6 -> x0, waiting for transfers between devices: 279 us -> none  [the longest x1 71.3 us: local(): lax.all_gather(shrink_weight, 'fsdp', axis=1, tiled=True)]
    ppermute x0 -> x59, waiting for transfers between devices: none -> 174 us  [the longest x20 112 us: to_y(): return lax.ppermute(part, 'fsdp', SWAP_Y)]
    rev x0 -> x10, local copies, waits for them, and re-layouts: none -> 75.5 us  [turn(): cut = jnp.where(bit, jnp.flip(cut, at), cut)]
    select_n x0 -> x39, other arithmetic: none -> 60 us  [the longest x27 51.9 us: turn(): cut = jnp.where(bit, jnp.flip(cut, at), cut)]
    unnamed x107 -> x241, local copies, waits for them, and re-layouts: 22 us -> 67.8 us
    psum x1 -> x2, blocking collectives: 28.7 us -> 67.2 us  [the longest x1 40.8 us: square_local(): gains = lax.psum(turned(gains, 1), ('replica', 'fsdp', 'tensor'))]
  transfers between devices with their start and end apart: 14 -> 60, of which waited for: 14 -> 24; matrix products, arithmetic and copies ran while one was open for 11% -> 53% of each run, Pallas kernels for 0% -> 0%
where the time goes in v1:
time: 862 us; the launch traced here: 847 us
  local copies, waits for them, and re-layouts  242 us (28%)
  waiting for transfers between devices  240 us (28%)
  other arithmetic  138 us (16%)
  matrix products  106 us (12%)
  blocking collectives  67.2 us (8%)
  starting transfers between devices  37.4 us (4%)
  between operations  16.5 us (2%)
    ppermute x20, waiting for transfers between devices, to_y(): return lax.ppermute(part, 'fsdp', SWAP_Y)  112 us
    rev x10, local copies, waits for them, and re-layouts, turn(): cut = jnp.where(bit, jnp.flip(cut, at), cut)  75.5 us
    unnamed x241, local copies, waits for them, and re-layouts  67.8 us
    psum x1, waiting for transfers between devices, square_local(): branch = lax.psum(branch.astype(LOW), 'tensor').astype(FULL)  66 us
    ppermute x19, waiting for transfers between devices, to_x(): return lax.ppermute(part, 'fsdp', SWAP_X)  57.8 us
    select_n x27, other arithmetic, turn(): cut = jnp.where(bit, jnp.flip(cut, at), cut)  51.9 us
    dot_general x6, matrix products, contract_last(): lax.dot_general(left_op, right_op, (((1,), (1,)), ((), ())), preferred_el...  42.1 us
    psum x1, blocking collectives, square_local(): gains = lax.psum(turned(gains, 1), ('replica', 'fsdp', 'tensor'))  40.8 us
  transfers between devices with their start and end apart: 60, of which 24 were waited for; matrix products, arithmetic and copies ran while one was open for 53% of the time, Pallas kernels for 0%

profile of v1, /device:TPU:0, one launch (start us, length us, event | category | flops | bytes accessed | tf_op | source)
XLA Modules:
  0.0 847.0 jit_solution(1181576492630502129)
XLA Ops:
  10.4 3.1 reverse_select_fusion.6
  49.7 4.5 reshape_squeeze.26
  54.1 4.4 broadcast_select_fusion.2
  58.5 3.5 broadcast_select_fusion.5
  62.0 19.7 %rev.140 = bf16[512,2,2,2,256]{4,3,2,1,0:T(2,128)(2,1)} reverse(bf16[512,2,2,2,256]{4,3,2,1,0:T(2,128)(2,1)} %broadcast_select_fusion.5), dimensions={3} | reverse | bytes 4194304 | tf_op jit(solution)/shard_map/jit(_flip)/rev | solution.py:81
  81.7 5.7 fusion.70
  87.5 7.2 copy.49
  94.7 8.8 %multiply_reduce_fusion.3 = f32[512]{0:T(512)S(1)} fusion(f32[512,2,2,2,256]{4,3,2,1,0:T(2,128)} %get-tuple-element.85, f32[512]{0:T(512)S(1)} %broadcast_multiply_fusion.4), kind=kLoop, calls=%fused_computation.57 | loop fusion | flops 3145216 | bytes 4198400 | tf_op jit(solution)/shard_map/reduce_sum | solution.py:179
  106.3 4.4 broadcast_select_fusion
  114.2 15.1 %rev.167 = bf16[512,2,2,2,256]{4,3,2,1,0:T(2,128)(2,1)} reverse(bf16[512,2,2,2,256]{4,3,2,1,0:T(2,128)(2,1)S(1)} %broadcast_select_fusion.3), dimensions={3} | reverse | bytes 4194304 | tf_op jit(solution)/shard_map/jit(_flip)/rev | solution.py:81
  129.4 5.6 broadcast_select_fusion.7
  139.5 3.8 add_convert_fusion
  144.9 4.6 copy.52
  149.5 3.1 fusion.77
  162.9 6.6 reshape.324
  187.9 12.3 %collective-permute-done = bf16[256,1536]{1,0:T(8,128)(2,1)S(1)} collective-permute-done((bf16[256,1536]{1,0:T(8,128)(2,1)}, bf16[256,1536]{1,0:T(8,128)(2,1)S(1)}, u32[]{:S(2)}, u32[]{:S(2)}) %collective-permute-start) | collective-permute-done | bytes 786464 | tf_op jit(solution)/shard_map/ppermute | solution.py:62
  204.5 24.5 %collective-permute-done.2 = bf16[256,1536]{1,0:T(8,128)(2,1)S(1)} collective-permute-done((bf16[256,1536]{1,0:T(8,128)(2,1)}, bf16[256,1536]{1,0:T(8,128)(2,1)S(1)}, u32[]{:S(2)}, u32[]{:S(2)}) %collective-permute-start.2) | collective-permute-done | bytes 786464 | tf_op jit(solution)/shard_map/ppermute | solution.py:66
  244.5 7.8 collective-permute-done.22
  254.1 9.5 %collective-permute-done.29 = bf16[2048,128]{0,1:T(8,128)(2,1)S(1)} collective-permute-done((bf16[2048,128]{0,1:T(8,128)(2,1)S(1)}, bf16[2048,128]{0,1:T(8,128)(2,1)S(1)}, u32[]{:S(2)}, u32[]{:S(2)}) %collective-permute-start.29) | collective-permute-done | bytes 524320 | tf_op jit(solution)/shard_map/ppermute | solution.py:66
  266.1 3.8 collective-permute-done.6
  272.8 5.2 convolution_add_fusion
  301.8 7.7 collective-permute-done.8
  310.7 7.2 fusion.14
  319.0 16.0 %convert_reduce_fusion.1 = (f32[2048]{0:T(1024)S(1)}, bf16[512,2048]{1,0:T(8,128)(2,1)S(1)}, f32[512,2048]{1,0:T(8,128)S(1)}) fusion(f32[512,2048]{1,0:T(8,128)S(1)} %fusion.14, f32[2048]{0:T(1024)S(1)} %copy-done.72, bf16[512,2048]{1,0:T(8,128)(2,1)S(1)} %copy-done.17, bf16[2048,2048]{0,1:T(8,128)(2,1)} %constant_dynamic-update-slice_fusion.26), kind=kOutput, calls=%fused_computation.31 | convolution fusion | flops 4373608448 | bytes 20987904 | tf_op jit(solution)/shard_map/dot_general | solution.py:36
  337.0 4.3 convolution_convert_fusion.1
  341.4 9.5 %fusion.85 = f32[512,2048]{1,0:T(8,128)} fusion(bf16[512,2048]{1,0:T(8,128)(2,1)S(1)} %multiply_convert_fusion.1, bf16[2048,2048]{0,1:T(8,128)(2,1)} %constant_dynamic-update-slice_fusion.26), kind=kOutput, calls=%fused_computation.309 | convolution fusion | flops 4294967296 | bytes 14680064 | tf_op jit(solution)/shard_map/dot_general | solution.py:239
  351.4 4.3 convolution_convert_fusion
  356.0 9.3 %collective-permute-done.9 = bf16[2,512,256]{1,2,0:T(8,128)(2,1)S(1)} collective-permute-done((bf16[2,512,256]{1,2,0:T(8,128)(2,1)S(1)}, bf16[2,512,256]{1,2,0:T(8,128)(2,1)S(1)}, u32[]{:S(2)}, u32[]{:S(2)}) %collective-permute-start.9) | collective-permute-done | bytes 524320 | tf_op jit(solution)/shard_map/ppermute | solution.py:62
  369.8 5.7 multiply_reduce_fusion
  381.1 6.9 multiply_convert_fusion
  388.0 4.1 convolution_multiply_fusion
  394.1 6.1 fusion.23
  400.2 3.1 copy.48
  409.3 20.1 %collective-permute-done.33 = bf16[2,1024,256]{1,2,0:T(8,128)(2,1)S(1)} collective-permute-done((bf16[2,1024,256]{1,2,0:T(8,128)(2,1)S(1)}, bf16[2,1024,256]{1,2,0:T(8,128)(2,1)S(1)}, u32[]{:S(2)}, u32[]{:S(2)}) %collective-permute-start.33) | collective-permute-done | bytes 1048608 | tf_op jit(solution)/shard_map/ppermute | solution.py:62
  435.6 3.7 collective-permute-done.42
  443.4 15.8 %collective-permute-done.45 = bf16[512,256]{1,0:T(8,128)(2,1)S(1)} collective-permute-done((bf16[512,256]{1,0:T(8,128)(2,1)S(1)}, bf16[512,256]{1,0:T(8,128)(2,1)S(1)}, u32[]{:S(2)}, u32[]{:S(2)}) %collective-permute-start.45) | collective-permute-done | bytes 262176 | tf_op jit(solution)/shard_map/ppermute | solution.py:66
  460.1 3.5 fusion.86
  463.7 12.1 %add_convert_fusion.2 = (bf16[512,2048]{1,0:T(8,128)(2,1)}, f32[512,2048]{1,0:T(8,128)}) fusion(f32[512,2048]{1,0:T(8,128)S(1)} %fusion.86, f32[2048]{0:T(1024)S(1)} %bitcast.241, f32[2048]{0:T(1024)S(1)} %bitcast.243, bf16[512,2048]{1,0:T(8,128)(2,1)S(1)} %copy-done.34, bf16[2048,2048]{1,0:T(8,128)(2,1)} %constant_dynamic-update-slice_fusion.18), kind=kOutput, calls=%fused_computation.38 | convolution fusion | flops 4299161600 | bytes 20987904 | tf_op jit(solution)/shard_map/dot_general | solution.py:36
  475.8 3.5 convolution_convert_fusion.2
  479.8 26.3 %all-reduce.4 = (f32[2,768]{1,0:T(2,128)}, f32[2048]{0:T(1024)S(1)}, f32[2048]{0:T(1024)}) all-reduce(f32[2,768]{1,0:T(2,128)S(1)} %bitcast.239, f32[2048]{0:T(1024)S(1)} %copy-done.70, f32[2048]{0:T(1024)S(1)} %get-tuple-element.73), channel_id=1, replica_groups=mesh['replica'=2,'fsdp'=4,'tensor'=4] {'replica','fsdp'}, use_global_device_ids=true, to_apply=%region_15.16 | all-reduce | flops 5632 | bytes 45056 | tf_op jit(solution)/shard_map/psum | solution.py:267
  508.8 4.5 fusion.65
  516.0 4.6 fusion.64
  523.0 5.7 collective-permute-done.48
  531.7 8.2 collective-permute-done.54
  543.3 3.7 fusion.68
  548.7 13.7 %collective-permute-done.51 = bf16[256,2048]{1,0:T(8,128)(2,1)S(1)} collective-permute-done((bf16[256,2048]{1,0:T(8,128)(2,1)S(1)}, bf16[256,2048]{1,0:T(8,128)(2,1)S(1)}, u32[]{:S(2)}, u32[]{:S(2)}) %collective-permute-start.51) | collective-permute-done | bytes 1048608 | tf_op jit(solution)/shard_map/ppermute | solution.py:66
  566.3 18.6 %collective-permute-done.57 = bf16[2048,256]{0,1:T(8,128)(2,1)S(1)} collective-permute-done((bf16[2048,256]{0,1:T(8,128)(2,1)S(1)}, bf16[2048,256]{0,1:T(8,128)(2,1)S(1)}, u32[]{:S(2)}, u32[]{:S(2)}) %collective-permute-start.57) | collective-permute-done | bytes 1048608 | tf_op jit(solution)/shard_map/ppermute | solution.py:66
  588.8 3.9 collective-permute-done.36
  596.8 66.0 %all-reduce.8.cloned.1.call-done = (bf16[512,2048]{1,0:T(8,128)(2,1)}, bf16[512,2048]{1,0:T(8,128)(2,1)}) async-done(((bf16[512,2048]{1,0:T(8,128)(2,1)}, bf16[512,2048]{1,0:T(8,128)(2,1)}), (bf16[512,2048]{1,0:T(8,128)(2,1)}, bf16[512,2048]{1,0:T(8,128)(2,1)})) %all-reduce.8.cloned.1.call-update) | async-done | bytes 4194320 | tf_op jit(solution)/shard_map/psum | solution.py:242
  662.8 6.8 multiply_reduce_fusion.1
  671.1 3.5 fusion.6
  677.6 4.4 broadcast_select_fusion.1
  681.9 3.5 broadcast_select_fusion.4
  685.4 19.3 %rev.164 = bf16[512,2,2,2,256]{4,3,2,1,0:T(2,128)(2,1)} reverse(bf16[512,2,2,2,256]{4,3,2,1,0:T(2,128)(2,1)} %broadcast_select_fusion.4), dimensions={3} | reverse | bytes 4194304 | tf_op jit(solution)/shard_map/jit(_flip)/rev | solution.py:81
  704.7 5.6 broadcast_select_fusion.8
  710.3 6.8 reshape.320
  717.1 5.6 reverse_select_fusion.3
  724.7 4.2 reverse_select_fusion.2
  728.9 20.8 %rev.172 = f32[512,2,2,2,256]{4,3,2,1,0:T(2,128)} reverse(f32[512,2,2,2,256]{4,3,2,1,0:T(2,128)} %reverse_select_fusion.2), dimensions={3} | reverse | bytes 8388608 | tf_op jit(solution)/shard_map/jit(_flip)/rev | solution.py:81
  749.7 8.5 %broadcast_select_fusion.6 = f32[512,2,2,2,256]{4,3,2,1,0:T(2,128)} fusion(f32[512,2,2,2,256]{4,3,2,1,0:T(2,128)} %rev.172, pred[]{:T(512)S(6)} %eq.11, f32[512,2,2,2,256]{4,3,2,1,0:T(2,128)} %copy-done.6, pred[]{:T(512)S(6)} %eq.12), kind=kLoop, calls=%fused_computation.66 | loop fusion | flops 2097152 | bytes 12582914 | tf_op jit(solution)/shard_map/jit(_where)/select_n | solution.py:81
  761.2 6.4 broadcast_in_dim_reshape.5
  767.8 40.8 %psum.44 = f32[4,2048]{1,0:T(4,128)S(1)} all-reduce(f32[4,2048]{1,0:T(4,128)S(1)} %reshape.321), channel_id=1, replica_groups=mesh['replica'=2,'fsdp'=4,'tensor'=4] {'replica','fsdp','tensor'}, use_global_device_ids=true, to_apply=%region_13.14 | all-reduce | flops 8192 | bytes 65536 | tf_op jit(solution)/shard_map/psum | solution.py:266
  817.1 5.3 copy.56
  834.7 4.4 pad_maximum_fusion.5
  (523 shorter events, 223.0 us)
Async XLA Ops:
  7.2 128.9 %copy-start = (s32[1,4]{1,0:T(1,128)S(1)}, s32[1,4]{1,0:T(1,128)}, u32[]{:S(2)}) copy-start(s32[1,4]{1,0:T(1,128)} %param.17) | copy-start | bytes 52
  7.2 655.6 %all-reduce.8.cloned.1.call-start = ((), (), s32[]{:S(2)}) async-start(), calls=%async_computation | async-start | bytes 8388608 | tf_op jit(solution)/shard_map/psum | solution.py:242
  14.6 215.0 %collective-permute-start.18 = (bf16[256,2048]{1,0:T(8,128)(2,1)}, bf16[256,2048]{1,0:T(8,128)(2,1)}, u32[]{:S(2)}, u32[]{:S(2)}) collective-permute-start(bf16[256,2048]{1,0:T(8,128)(2,1)} %slice_bitcast_fusion.7), channel_id=1, source_target_pairs={{0,4},{4,0},{8,12},{12,8},{1,5},{5,1},{9,13},{13,9},{2,6},{6,2},{1... | collective-permute-start | bytes 3145736 | tf_op jit(solution)/shard_map/ppermute | solution.py:62
  17.5 213.7 %collective-permute-start.20 = (bf16[256,2048]{1,0:T(8,128)(2,1)}, bf16[256,2048]{1,0:T(8,128)(2,1)}, u32[]{:S(2)}, u32[]{:S(2)}) collective-permute-start(bf16[256,2048]{1,0:T(8,128)(2,1)} %slice_bitcast_fusion.7), channel_id=1, source_target_pairs={{0,8},{8,0},{4,12},{12,4},{1,9},{9,1},{5,13},{13,5},{2,10},{10,2},... | collective-permute-start | bytes 3145736 | tf_op jit(solution)/shard_map/ppermute | solution.py:66
  20.7 135.3 %collective-permute-start.11 = (bf16[512,256]{1,0:T(8,128)(2,1)}, bf16[512,256]{1,0:T(8,128)(2,1)}, u32[]{:S(2)}, u32[]{:S(2)}) collective-permute-start(bf16[512,256]{1,0:T(8,128)(2,1)} %slice_bitcast_fusion.17), channel_id=1, source_target_pairs={{0,4},{4,0},{8,12},{12,8},{1,5},{5,1},{9,13},{13,9},{2,6},{6,2},{1... | collective-permute-start | bytes 786440 | tf_op jit(solution)/shard_map/ppermute | solution.py:62
  21.3 137.7 %collective-permute-start.13 = (bf16[512,256]{1,0:T(8,128)(2,1)}, bf16[512,256]{1,0:T(8,128)(2,1)}, u32[]{:S(2)}, u32[]{:S(2)}) collective-permute-start(bf16[512,256]{1,0:T(8,128)(2,1)} %slice_bitcast_fusion.17), channel_id=1, source_target_pairs={{0,8},{8,0},{4,12},{12,4},{1,9},{9,1},{5,13},{13,5},{2,10},{10,2},... | collective-permute-start | bytes 786440 | tf_op jit(solution)/shard_map/ppermute | solution.py:66
  87.5 223.2 %copy-start.67 = (f32[512]{0:T(512)}, f32[512]{0:T(512)S(1)}, u32[]{:S(2)}) copy-start(f32[512]{0:T(512)S(1)} %broadcast_multiply_fusion.4) | copy-start | bytes 6148
  156.9 22.7 %collective-permute-start.15 = (bf16[512,128]{1,0:T(8,128)(2,1)S(1)}, bf16[512,128]{1,0:T(8,128)(2,1)S(1)}, u32[]{:S(2)}, u32[]{:S(2)}) collective-permute-start(bf16[512,128]{1,0:T(8,128)(2,1)S(1)} %slice.445), channel_id=1, source_target_pairs={{0,8},{8,0},{4,12},{12,4},{1,9},{9,1},{5,13},{13,5},{2,10},{10,2},... | collective-permute-start | bytes 393224 | tf_op jit(solution)/shard_map/ppermute | solution.py:66
  159.9 20.3 %collective-permute-start.16 = (bf16[512,128]{1,0:T(8,128)(2,1)S(1)}, bf16[512,128]{1,0:T(8,128)(2,1)S(1)}, u32[]{:S(2)}, u32[]{:S(2)}) collective-permute-start(bf16[512,128]{1,0:T(8,128)(2,1)S(1)} %slice.446), channel_id=1, source_target_pairs={{0,4},{4,0},{8,12},{12,8},{1,5},{5,1},{9,13},{13,9},{2,6},{6,2},{1... | collective-permute-start | bytes 393224 | tf_op jit(solution)/shard_map/ppermute | solution.py:62
  161.5 18.7 %collective-permute-start.12 = (bf16[512,256]{1,0:T(8,128)(2,1)}, bf16[512,256]{1,0:T(8,128)(2,1)S(1)}, u32[]{:S(2)}, u32[]{:S(2)}) collective-permute-start(bf16[512,256]{1,0:T(8,128)(2,1)} %collective-permute-done.11), channel_id=1, source_target_pairs={{0,16},{16,0},{1,17},{17,1},{2,18},{18,2},{3,19},{19,3},{4,20},{20... | collective-permute-start | bytes 786440 | tf_op jit(solution)/shard_map/ppermute | solution.py:70
  179.7 20.6 %collective-permute-start = (bf16[256,1536]{1,0:T(8,128)(2,1)}, bf16[256,1536]{1,0:T(8,128)(2,1)S(1)}, u32[]{:S(2)}, u32[]{:S(2)}) collective-permute-start(bf16[256,1536]{1,0:T(8,128)(2,1)} %slice_bitcast_fusion.12), channel_id=1, source_target_pairs={{0,4},{4,0},{8,12},{12,8},{1,5},{5,1},{9,13},{13,9},{2,6},{6,2},{1... | collective-permute-start | bytes 2359304 | tf_op jit(solution)/shard_map/ppermute | solution.py:62
  180.2 4.1 collective-permute-start.14
  180.3 53.8 %collective-permute-start.25 = (bf16[2048,256]{0,1:T(8,128)(2,1)}, bf16[2048,256]{0,1:T(8,128)(2,1)}, u32[]{:S(2)}, u32[]{:S(2)}) collective-permute-start(bf16[2048,256]{0,1:T(8,128)(2,1)} %slice_bitcast_fusion.5), channel_id=1, source_target_pairs={{0,4},{4,0},{8,12},{12,8},{1,5},{5,1},{9,13},{13,9},{2,6},{6,2},{1... | collective-permute-start | bytes 3145736 | tf_op jit(solution)/shard_map/ppermute | solution.py:62
  184.3 2.4 collective-permute-start.17
  186.6 52.4 %collective-permute-start.27 = (bf16[2048,256]{0,1:T(8,128)(2,1)}, bf16[2048,256]{0,1:T(8,128)(2,1)}, u32[]{:S(2)}, u32[]{:S(2)}) collective-permute-start(bf16[2048,256]{0,1:T(8,128)(2,1)} %slice_bitcast_fusion.5), channel_id=1, source_target_pairs={{0,8},{8,0},{4,12},{12,4},{1,9},{9,1},{5,13},{13,5},{2,10},{10,2},... | collective-permute-start | bytes 3145736 | tf_op jit(solution)/shard_map/ppermute | solution.py:66
  200.3 28.8 %collective-permute-start.2 = (bf16[256,1536]{1,0:T(8,128)(2,1)}, bf16[256,1536]{1,0:T(8,128)(2,1)S(1)}, u32[]{:S(2)}, u32[]{:S(2)}) collective-permute-start(bf16[256,1536]{1,0:T(8,128)(2,1)} %slice_bitcast_fusion.12), channel_id=1, source_target_pairs={{0,8},{8,0},{4,12},{12,4},{1,9},{9,1},{5,13},{13,5},{2,10},{10,2},... | collective-permute-start | bytes 2359304 | tf_op jit(solution)/shard_map/ppermute | solution.py:66
  229.1 12.1 %collective-permute-start.4 = (bf16[128,1536]{1,0:T(8,128)(2,1)S(1)}, bf16[128,1536]{1,0:T(8,128)(2,1)S(1)}, u32[]{:S(2)}, u32[]{:S(2)}) collective-permute-start(bf16[128,1536]{1,0:T(8,128)(2,1)S(1)} %slice.419), channel_id=1, source_target_pairs={{0,8},{8,0},{4,12},{12,4},{1,9},{9,1},{5,13},{13,5},{2,10},{10,2},... | collective-permute-start | bytes 1179656 | tf_op jit(solution)/shard_map/ppermute | solution.py:66
  229.6 12.1 %collective-permute-start.5 = (bf16[128,1536]{1,0:T(8,128)(2,1)S(1)}, bf16[128,1536]{1,0:T(8,128)(2,1)S(1)}, u32[]{:S(2)}, u32[]{:S(2)}) collective-permute-start(bf16[128,1536]{1,0:T(8,128)(2,1)S(1)} %slice.420), channel_id=1, source_target_pairs={{0,4},{4,0},{8,12},{12,8},{1,5},{5,1},{9,13},{13,9},{2,6},{6,2},{1... | collective-permute-start | bytes 1179656 | tf_op jit(solution)/shard_map/ppermute | solution.py:62
  231.2 21.2 %collective-permute-start.22 = (bf16[128,2048]{1,0:T(8,128)(2,1)S(1)}, bf16[128,2048]{1,0:T(8,128)(2,1)S(1)}, u32[]{:S(2)}, u32[]{:S(2)}) collective-permute-start(bf16[128,2048]{1,0:T(8,128)(2,1)S(1)} %slice.449), channel_id=1, source_target_pairs={{0,8},{8,0},{4,12},{12,4},{1,9},{9,1},{5,13},{13,5},{2,10},{10,2},... | collective-permute-start | bytes 1572872 | tf_op jit(solution)/shard_map/ppermute | solution.py:66
  234.0 18.9 %collective-permute-start.23 = (bf16[128,2048]{1,0:T(8,128)(2,1)S(1)}, bf16[128,2048]{1,0:T(8,128)(2,1)S(1)}, u32[]{:S(2)}, u32[]{:S(2)}) collective-permute-start(bf16[128,2048]{1,0:T(8,128)(2,1)S(1)} %slice.450), channel_id=1, source_target_pairs={{0,4},{4,0},{8,12},{12,8},{1,5},{5,1},{9,13},{13,9},{2,6},{6,2},{1... | collective-permute-start | bytes 1572872 | tf_op jit(solution)/shard_map/ppermute | solution.py:62
  239.0 26.2 %collective-permute-start.1 = (bf16[256,1536]{1,0:T(8,128)(2,1)S(1)}, bf16[256,1536]{1,0:T(8,128)(2,1)S(1)}, u32[]{:S(2)}, u32[]{:S(2)}) collective-permute-start(bf16[256,1536]{1,0:T(8,128)(2,1)S(1)} %collective-permute-done), channel_id=1, source_target_pairs={{0,16},{16,0},{1,17},{17,1},{2,18},{18,2},{3,19},{19,3},{4,20},{20... | collective-permute-start | bytes 2359304 | tf_op jit(solution)/shard_map/ppermute | solution.py:70
  241.1 22.5 %collective-permute-start.29 = (bf16[2048,128]{0,1:T(8,128)(2,1)S(1)}, bf16[2048,128]{0,1:T(8,128)(2,1)S(1)}, u32[]{:S(2)}, u32[]{:S(2)}) collective-permute-start(bf16[2048,128]{0,1:T(8,128)(2,1)S(1)} %slice.453), channel_id=1, source_target_pairs={{0,8},{8,0},{4,12},{12,4},{1,9},{9,1},{5,13},{13,5},{2,10},{10,2},... | collective-permute-start | bytes 1572872 | tf_op jit(solution)/shard_map/ppermute | solution.py:66
  241.7 21.9 %collective-permute-start.30 = (bf16[2048,128]{0,1:T(8,128)(2,1)S(1)}, bf16[2048,128]{0,1:T(8,128)(2,1)S(1)}, u32[]{:S(2)}, u32[]{:S(2)}) collective-permute-start(bf16[2048,128]{0,1:T(8,128)(2,1)S(1)} %slice.454), channel_id=1, source_target_pairs={{0,4},{4,0},{8,12},{12,8},{1,5},{5,1},{9,13},{13,9},{2,6},{6,2},{1... | collective-permute-start | bytes 1572872 | tf_op jit(solution)/shard_map/ppermute | solution.py:62
  252.3 117.4 %collective-permute-start.32 = (bf16[512,256]{0,1:T(8,128)(2,1)}, bf16[512,256]{0,1:T(8,128)(2,1)}, u32[]{:S(2)}, u32[]{:S(2)}) collective-permute-start(bf16[512,256]{0,1:T(8,128)(2,1)} %get-tuple-element.153), channel_id=1, source_target_pairs={{0,8},{8,0},{4,12},{12,4},{1,9},{9,1},{5,13},{13,5},{2,10},{10,2},... | collective-permute-start | bytes 786440 | tf_op jit(solution)/shard_map/ppermute | solution.py:66
  253.0 12.5 %collective-permute-start.3 = (bf16[256,1536]{1,0:T(8,128)(2,1)S(1)}, bf16[256,1536]{1,0:T(8,128)(2,1)S(1)}, u32[]{:S(2)}, u32[]{:S(2)}) collective-permute-start(bf16[256,1536]{1,0:T(8,128)(2,1)S(1)} %collective-permute-done.2), channel_id=1, source_target_pairs={{0,16},{16,0},{1,17},{17,1},{2,18},{18,2},{3,19},{19,3},{4,20},{20... | collective-permute-start | bytes 2359304 | tf_op jit(solution)/shard_map/ppermute | solution.py:70
  263.6 18.5 %collective-permute-start.19 = (bf16[256,2048]{1,0:T(8,128)(2,1)}, bf16[256,2048]{1,0:T(8,128)(2,1)}, u32[]{:S(2)}, u32[]{:S(2)}) collective-permute-start(bf16[256,2048]{1,0:T(8,128)(2,1)} %collective-permute-done.18), channel_id=1, source_target_pairs={{0,16},{16,0},{1,17},{17,1},{2,18},{18,2},{3,19},{19,3},{4,20},{20... | collective-permute-start | bytes 3145736 | tf_op jit(solution)/shard_map/ppermute | solution.py:70
  263.6 29.2 %collective-permute-start.21 = (bf16[256,2048]{1,0:T(8,128)(2,1)}, bf16[256,2048]{1,0:T(8,128)(2,1)}, u32[]{:S(2)}, u32[]{:S(2)}) collective-permute-start(bf16[256,2048]{1,0:T(8,128)(2,1)} %collective-permute-done.20), channel_id=1, source_target_pairs={{0,16},{16,0},{1,17},{17,1},{2,18},{18,2},{3,19},{19,3},{4,20},{20... | collective-permute-start | bytes 3145736 | tf_op jit(solution)/shard_map/ppermute | solution.py:70
  265.2 4.8 collective-permute-start.6
  265.5 22.4 %collective-permute-start.26 = (bf16[2048,256]{0,1:T(8,128)(2,1)}, bf16[2048,256]{0,1:T(8,128)(2,1)}, u32[]{:S(2)}, u32[]{:S(2)}) collective-permute-start(bf16[2048,256]{0,1:T(8,128)(2,1)} %collective-permute-done.25), channel_id=1, source_target_pairs={{0,16},{16,0},{1,17},{17,1},{2,18},{18,2},{3,19},{19,3},{4,20},{20... | collective-permute-start | bytes 3145736 | tf_op jit(solution)/shard_map/ppermute | solution.py:70
  270.0 25.6 %collective-permute-start.28 = (bf16[2048,256]{0,1:T(8,128)(2,1)}, bf16[2048,256]{0,1:T(8,128)(2,1)}, u32[]{:S(2)}, u32[]{:S(2)}) collective-permute-start(bf16[2048,256]{0,1:T(8,128)(2,1)} %collective-permute-done.27), channel_id=1, source_target_pairs={{0,16},{16,0},{1,17},{17,1},{2,18},{18,2},{3,19},{19,3},{4,20},{20... | collective-permute-start | bytes 3145736 | tf_op jit(solution)/shard_map/ppermute | solution.py:70
  282.1 83.2 %copy-start.58 = (bf16[512,256]{0,1:T(8,128)(2,1)}, bf16[512,256]{0,1:T(8,128)(2,1)S(1)}, u32[]{:S(2)}) copy-start(bf16[512,256]{0,1:T(8,128)(2,1)S(1)} %get-tuple-element.132) | copy-start | bytes 786436
  282.8 26.8 %collective-permute-start.24 = (bf16[256,2048]{1,0:T(8,128)(2,1)S(1)}, bf16[256,2048]{1,0:T(8,128)(2,1)S(1)}, u32[]{:S(2)}, u32[]{:S(2)}) collective-permute-start(bf16[256,2048]{1,0:T(8,128)(2,1)S(1)} %copy-done.50), channel_id=1, source_target_pairs={{0,16},{16,0},{1,17},{17,1},{2,18},{18,2},{3,19},{19,3},{4,20},{20... | collective-permute-start | bytes 3145736 | tf_op jit(solution)/shard_map/ppermute | solution.py:70
  287.8 30.0 %collective-permute-start.31 = (bf16[2048,256]{0,1:T(8,128)(2,1)S(1)}, bf16[2048,256]{0,1:T(8,128)(2,1)S(1)}, u32[]{:S(2)}, u32[]{:S(2)}) collective-permute-start(bf16[2048,256]{0,1:T(8,128)(2,1)S(1)} %copy-done.51), channel_id=1, source_target_pairs={{0,16},{16,0},{1,17},{17,1},{2,18},{18,2},{3,19},{19,3},{4,20},{20... | collective-permute-start | bytes 3145736 | tf_op jit(solution)/shard_map/ppermute | solution.py:70
  292.8 58.1 %collective-permute-start.7 = (bf16[3,512,256]{1,2,0:T(8,128)(2,1)S(1)}, bf16[3,512,256]{1,2,0:T(8,128)(2,1)S(1)}, u32[]{:S(2)}, u32[]{:S(2)}) collective-permute-start(bf16[3,512,256]{1,2,0:T(8,128)(2,1)S(1)} %slice_bitcast_fusion.10), channel_id=1, source_target_pairs={{0,8},{8,0},{4,12},{12,4},{1,9},{9,1},{5,13},{13,5},{2,10},{10,2},... | collective-permute-start | bytes 2359304 | tf_op jit(solution)/shard_map/ppermute | solution.py:66
  295.6 13.9 %collective-permute-start.8 = (bf16[2,512,256]{1,2,0:T(8,128)(2,1)S(1)}, bf16[2,512,256]{1,2,0:T(8,128)(2,1)S(1)}, u32[]{:S(2)}, u32[]{:S(2)}) collective-permute-start(bf16[2,512,256]{1,2,0:T(8,128)(2,1)S(1)} %slice_bitcast_fusion.13), channel_id=1, source_target_pairs={{0,4},{4,0},{8,12},{12,8},{1,5},{5,1},{9,13},{13,9},{2,6},{6,2},{1... | collective-permute-start | bytes 1572872 | tf_op jit(solution)/shard_map/ppermute | solution.py:62
  341.4 167.4 %collective-permute-start.47 = (bf16[1024,2048]{1,0:T(8,128)(2,1)}, bf16[1024,2048]{1,0:T(8,128)(2,1)}, u32[]{:S(2)}, u32[]{:S(2)}) collective-permute-start(bf16[1024,2048]{1,0:T(8,128)(2,1)} %convolution_convert_fusion.1), channel_id=1, source_target_pairs={{0,16},{16,0},{1,17},{17,1},{2,18},{18,2},{3,19},{19,3},{4,20},{20... | collective-permute-start | bytes 12582920 | tf_op jit(solution)/shard_map/ppermute | solution.py:70
  350.9 14.3 %collective-permute-start.9 = (bf16[2,512,256]{1,2,0:T(8,128)(2,1)S(1)}, bf16[2,512,256]{1,2,0:T(8,128)(2,1)S(1)}, u32[]{:S(2)}, u32[]{:S(2)}) collective-permute-start(bf16[2,512,256]{1,2,0:T(8,128)(2,1)S(1)} %slice.435), channel_id=1, source_target_pairs={{0,4},{4,0},{8,12},{12,8},{1,5},{5,1},{9,13},{13,9},{2,6},{6,2},{1... | collective-permute-start | bytes 1572872 | tf_op jit(solution)/shard_map/ppermute | solution.py:62
  355.7 160.2 %collective-permute-start.53 = (bf16[2048,1024]{0,1:T(8,128)(2,1)}, bf16[2048,1024]{0,1:T(8,128)(2,1)}, u32[]{:S(2)}, u32[]{:S(2)}) collective-permute-start(bf16[2048,1024]{0,1:T(8,128)(2,1)} %convolution_convert_fusion), channel_id=1, source_target_pairs={{0,16},{16,0},{1,17},{17,1},{2,18},{18,2},{3,19},{19,3},{4,20},{20... | collective-permute-start | bytes 12582920 | tf_op jit(solution)/shard_map/ppermute | solution.py:70
  379.6 27.5 %collective-permute-start.10 = (bf16[512,256]{0,1:T(8,128)(2,1)}, bf16[512,256]{0,1:T(8,128)(2,1)}, u32[]{:S(2)}, u32[]{:S(2)}) collective-permute-start(bf16[512,256]{0,1:T(8,128)(2,1)} %get-tuple-element.147), channel_id=1, source_target_pairs={{0,8},{8,0},{4,12},{12,4},{1,9},{9,1},{5,13},{13,5},{2,10},{10,2},... | collective-permute-start | bytes 786440 | tf_op jit(solution)/shard_map/ppermute | solution.py:66
  404.9 24.5 %collective-permute-start.33 = (bf16[2,1024,256]{1,2,0:T(8,128)(2,1)S(1)}, bf16[2,1024,256]{1,2,0:T(8,128)(2,1)S(1)}, u32[]{:S(2)}, u32[]{:S(2)}) collective-permute-start(bf16[2,1024,256]{1,2,0:T(8,128)(2,1)S(1)} %fusion.35), channel_id=1, source_target_pairs={{0,4},{4,0},{8,12},{12,8},{1,5},{5,1},{9,13},{13,9},{2,6},{6,2},{1... | collective-permute-start | bytes 3145736 | tf_op jit(solution)/shard_map/ppermute | solution.py:62
  409.2 21.9 %collective-permute-start.41 = (bf16[512,1024]{1,0:T(8,128)(2,1)S(1)}, bf16[512,1024]{1,0:T(8,128)(2,1)S(1)}, u32[]{:S(2)}, u32[]{:S(2)}) collective-permute-start(bf16[512,1024]{1,0:T(8,128)(2,1)S(1)} %convolution_convert_fusion.3), channel_id=1, source_target_pairs={{0,16},{16,0},{1,17},{17,1},{2,18},{18,2},{3,19},{19,3},{4,20},{20... | collective-permute-start | bytes 3145736 | tf_op jit(solution)/shard_map/ppermute | solution.py:70
  432.8 6.5 collective-permute-start.42
  433.4 5.9 collective-permute-start.44
  433.9 25.5 %collective-permute-start.34 = (bf16[3,512,256]{1,2,0:T(8,128)(2,1)S(1)}, bf16[3,512,256]{1,2,0:T(8,128)(2,1)S(1)}, u32[]{:S(2)}, u32[]{:S(2)}) collective-permute-start(bf16[3,512,256]{1,2,0:T(8,128)(2,1)S(1)} %get-tuple-element.129), channel_id=1, source_target_pairs={{0,8},{8,0},{4,12},{12,4},{1,9},{9,1},{5,13},{13,5},{2,10},{10,2},... | collective-permute-start | bytes 2359304 | tf_op jit(solution)/shard_map/ppermute | solution.py:66
  439.4 19.8 %collective-permute-start.45 = (bf16[512,256]{1,0:T(8,128)(2,1)S(1)}, bf16[512,256]{1,0:T(8,128)(2,1)S(1)}, u32[]{:S(2)}, u32[]{:S(2)}) collective-permute-start(bf16[512,256]{1,0:T(8,128)(2,1)S(1)} %pad_maximum_fusion.37), channel_id=1, source_target_pairs={{0,8},{8,0},{4,12},{12,4},{1,9},{9,1},{5,13},{13,5},{2,10},{10,2},... | collective-permute-start | bytes 786440 | tf_op jit(solution)/shard_map/ppermute | solution.py:66
  440.1 19.1 %collective-permute-start.43 = (bf16[512,256]{1,0:T(8,128)(2,1)S(1)}, bf16[512,256]{1,0:T(8,128)(2,1)S(1)}, u32[]{:S(2)}, u32[]{:S(2)}) collective-permute-start(bf16[512,256]{1,0:T(8,128)(2,1)S(1)} %pad_maximum_fusion.36), channel_id=1, source_target_pairs={{0,4},{4,0},{8,12},{12,8},{1,5},{5,1},{9,13},{13,9},{2,6},{6,2},{1... | collective-permute-start | bytes 786440 | tf_op jit(solution)/shard_map/ppermute | solution.py:62
  459.3 46.9 %collective-permute-start.46 = (f32[512,256]{1,0:T(8,128)S(1)}, f32[512,256]{1,0:T(8,128)}, u32[]{:S(2)}, u32[]{:S(2)}) collective-permute-start(f32[512,256]{1,0:T(8,128)S(1)} %fusion.47), channel_id=1, source_target_pairs={{0,16},{16,0},{1,17},{17,1},{2,18},{18,2},{3,19},{19,3},{4,20},{20... | collective-permute-start | bytes 1572872 | tf_op jit(solution)/shard_map/ppermute | solution.py:70
  479.4 63.6 %collective-permute-start.35 = (bf16[1024,1536]{1,0:T(8,128)(2,1)}, bf16[1024,1536]{1,0:T(8,128)(2,1)}, u32[]{:S(2)}, u32[]{:S(2)}) collective-permute-start(bf16[1024,1536]{1,0:T(8,128)(2,1)} %convolution_convert_fusion.2), channel_id=1, source_target_pairs={{0,16},{16,0},{1,17},{17,1},{2,18},{18,2},{3,19},{19,3},{4,20},{20... | collective-permute-start | bytes 9437192 | tf_op jit(solution)/shard_map/ppermute | solution.py:70
  506.2 333.0 %copy-start.79 = (f32[2048]{0:T(1024)}, f32[2048]{0:T(1024)S(1)}, u32[]{:S(2)}) copy-start(f32[2048]{0:T(1024)S(1)} %get-tuple-element.200) | copy-start | bytes 24580
  513.6 15.1 %collective-permute-start.48 = (bf16[128,2048]{1,0:T(8,128)(2,1)S(1)}, bf16[128,2048]{1,0:T(8,128)(2,1)S(1)}, u32[]{:S(2)}, u32[]{:S(2)}) collective-permute-start(bf16[128,2048]{1,0:T(8,128)(2,1)S(1)} %get-tuple-element.105), channel_id=1, source_target_pairs={{0,8},{8,0},{4,12},{12,4},{1,9},{9,1},{5,13},{13,5},{2,10},{10,2},... | collective-permute-start | bytes 1572872 | tf_op jit(solution)/shard_map/ppermute | solution.py:66
  516.0 14.9 %collective-permute-start.50 = (bf16[128,2048]{1,0:T(8,128)(2,1)S(1)}, bf16[128,2048]{1,0:T(8,128)(2,1)S(1)}, u32[]{:S(2)}, u32[]{:S(2)}) collective-permute-start(bf16[128,2048]{1,0:T(8,128)(2,1)S(1)} %get-tuple-element.104), channel_id=1, source_target_pairs={{0,4},{4,0},{8,12},{12,8},{1,5},{5,1},{9,13},{13,9},{2,6},{6,2},{1... | collective-permute-start | bytes 1572872 | tf_op jit(solution)/shard_map/ppermute | solution.py:62
  520.8 19.1 %collective-permute-start.54 = (bf16[2048,128]{0,1:T(8,128)(2,1)S(1)}, bf16[2048,128]{0,1:T(8,128)(2,1)S(1)}, u32[]{:S(2)}, u32[]{:S(2)}) collective-permute-start(bf16[2048,128]{0,1:T(8,128)(2,1)S(1)} %get-tuple-element.99), channel_id=1, source_target_pairs={{0,8},{8,0},{4,12},{12,4},{1,9},{9,1},{5,13},{13,5},{2,10},{10,2},... | collective-permute-start | bytes 1572872 | tf_op jit(solution)/shard_map/ppermute | solution.py:66
  522.1 19.9 %collective-permute-start.56 = (bf16[2048,128]{0,1:T(8,128)(2,1)S(1)}, bf16[2048,128]{0,1:T(8,128)(2,1)S(1)}, u32[]{:S(2)}, u32[]{:S(2)}) collective-permute-start(bf16[2048,128]{0,1:T(8,128)(2,1)S(1)} %get-tuple-element.98), channel_id=1, source_target_pairs={{0,4},{4,0},{8,12},{12,8},{1,5},{5,1},{9,13},{13,9},{2,6},{6,2},{1... | collective-permute-start | bytes 1572872 | tf_op jit(solution)/shard_map/ppermute | solution.py:62
  531.2 31.2 %collective-permute-start.51 = (bf16[256,2048]{1,0:T(8,128)(2,1)S(1)}, bf16[256,2048]{1,0:T(8,128)(2,1)S(1)}, u32[]{:S(2)}, u32[]{:S(2)}) collective-permute-start(bf16[256,2048]{1,0:T(8,128)(2,1)S(1)} %pad_maximum_fusion.18), channel_id=1, source_target_pairs={{0,8},{8,0},{4,12},{12,4},{1,9},{9,1},{5,13},{13,5},{2,10},{10,2},... | collective-permute-start | bytes 3145736 | tf_op jit(solution)/shard_map/ppermute | solution.py:66
  531.4 33.1 %collective-permute-start.49 = (bf16[256,2048]{1,0:T(8,128)(2,1)S(1)}, bf16[256,2048]{1,0:T(8,128)(2,1)S(1)}, u32[]{:S(2)}, u32[]{:S(2)}) collective-permute-start(bf16[256,2048]{1,0:T(8,128)(2,1)S(1)} %pad_maximum_fusion.17), channel_id=1, source_target_pairs={{0,4},{4,0},{8,12},{12,8},{1,5},{5,1},{9,13},{13,9},{2,6},{6,2},{1... | collective-permute-start | bytes 3145736 | tf_op jit(solution)/shard_map/ppermute | solution.py:62
  542.5 42.4 %collective-permute-start.57 = (bf16[2048,256]{0,1:T(8,128)(2,1)S(1)}, bf16[2048,256]{0,1:T(8,128)(2,1)S(1)}, u32[]{:S(2)}, u32[]{:S(2)}) collective-permute-start(bf16[2048,256]{0,1:T(8,128)(2,1)S(1)} %pad_maximum_fusion.20), channel_id=1, source_target_pairs={{0,8},{8,0},{4,12},{12,4},{1,9},{9,1},{5,13},{13,5},{2,10},{10,2},... | collective-permute-start | bytes 3145736 | tf_op jit(solution)/shard_map/ppermute | solution.py:66
  542.6 44.4 %collective-permute-start.55 = (bf16[2048,256]{0,1:T(8,128)(2,1)S(1)}, bf16[2048,256]{0,1:T(8,128)(2,1)S(1)}, u32[]{:S(2)}, u32[]{:S(2)}) collective-permute-start(bf16[2048,256]{0,1:T(8,128)(2,1)S(1)} %pad_maximum_fusion.19), channel_id=1, source_target_pairs={{0,4},{4,0},{8,12},{12,8},{1,5},{5,1},{9,13},{13,9},{2,6},{6,2},{1... | collective-permute-start | bytes 3145736 | tf_op jit(solution)/shard_map/ppermute | solution.py:62
  547.1 45.6 %collective-permute-start.36 = (bf16[128,1536]{1,0:T(8,128)(2,1)S(1)}, bf16[128,1536]{1,0:T(8,128)(2,1)S(1)}, u32[]{:S(2)}, u32[]{:S(2)}) collective-permute-start(bf16[128,1536]{1,0:T(8,128)(2,1)S(1)} %get-tuple-element.113), channel_id=1, source_target_pairs={{0,8},{8,0},{4,12},{12,4},{1,9},{9,1},{5,13},{13,5},{2,10},{10,2},... | collective-permute-start | bytes 1179656 | tf_op jit(solution)/shard_map/ppermute | solution.py:66
  562.4 30.4 %collective-permute-start.38 = (bf16[128,1536]{1,0:T(8,128)(2,1)S(1)}, bf16[128,1536]{1,0:T(8,128)(2,1)S(1)}, u32[]{:S(2)}, u32[]{:S(2)}) collective-permute-start(bf16[128,1536]{1,0:T(8,128)(2,1)S(1)} %get-tuple-element.112), channel_id=1, source_target_pairs={{0,4},{4,0},{8,12},{12,8},{1,5},{5,1},{9,13},{13,9},{2,6},{6,2},{1... | collective-permute-start | bytes 1179656 | tf_op jit(solution)/shard_map/ppermute | solution.py:62
  566.3 256.2 %collective-permute-start.52 = (f32[256,2048]{1,0:T(8,128)}, f32[256,2048]{1,0:T(8,128)}, u32[]{:S(2)}, u32[]{:S(2)}) collective-permute-start(f32[256,2048]{1,0:T(8,128)} %fusion.19), channel_id=1, source_target_pairs={{0,16},{16,0},{1,17},{17,1},{2,18},{18,2},{3,19},{19,3},{4,20},{20... | collective-permute-start | bytes 6291464 | tf_op jit(solution)/shard_map/ppermute | solution.py:70
  588.8 222.4 %collective-permute-start.58 = (f32[2048,256]{0,1:T(8,128)}, f32[2048,256]{0,1:T(8,128)}, u32[]{:S(2)}, u32[]{:S(2)}) collective-permute-start(f32[2048,256]{0,1:T(8,128)} %fusion.18), channel_id=1, source_target_pairs={{0,16},{16,0},{1,17},{17,1},{2,18},{18,2},{3,19},{19,3},{4,20},{20... | collective-permute-start | bytes 6291464 | tf_op jit(solution)/shard_map/ppermute | solution.py:70
  593.9 215.3 %collective-permute-start.39 = (bf16[256,1536]{1,0:T(8,128)(2,1)}, bf16[256,1536]{1,0:T(8,128)(2,1)S(1)}, u32[]{:S(2)}, u32[]{:S(2)}) collective-permute-start(bf16[256,1536]{1,0:T(8,128)(2,1)} %pad_maximum_fusion.24), channel_id=1, source_target_pairs={{0,8},{8,0},{4,12},{12,4},{1,9},{9,1},{5,13},{13,5},{2,10},{10,2},... | collective-permute-start | bytes 2359304 | tf_op jit(solution)/shard_map/ppermute | solution.py:66
  596.5 212.7 %collective-permute-start.37 = (bf16[256,1536]{1,0:T(8,128)(2,1)}, bf16[256,1536]{1,0:T(8,128)(2,1)}, u32[]{:S(2)}, u32[]{:S(2)}) collective-permute-start(bf16[256,1536]{1,0:T(8,128)(2,1)} %pad_maximum_fusion.23), channel_id=1, source_target_pairs={{0,4},{4,0},{8,12},{12,8},{1,5},{5,1},{9,13},{13,9},{2,6},{6,2},{1... | collective-permute-start | bytes 2359304 | tf_op jit(solution)/shard_map/ppermute | solution.py:62
  811.2 17.2 %collective-permute-start.40 = (f32[256,1536]{1,0:T(8,128)S(1)}, f32[256,1536]{1,0:T(8,128)S(1)}, u32[]{:S(2)}, u32[]{:S(2)}) collective-permute-start(f32[256,1536]{1,0:T(8,128)S(1)} %fusion.30), channel_id=1, source_target_pairs={{0,16},{16,0},{1,17},{17,1},{2,18},{18,2},{3,19},{19,3},{4,20},{20... | collective-permute-start | bytes 4718600 | tf_op jit(solution)/shard_map/ppermute | solution.py:70
  (92 other events, 989.0 us)
Sparse Core Ops, SparseCore 0:
  506.3 156.4 all-reduce.7

commit v2 on v0

--- a/solution.py
+++ b/solution.py
@@ -1,6 +1,10 @@
+import functools
+
 import jax
 import jax.numpy as jnp
 from jax import lax
+from jax.experimental import pallas as pl
+from jax.experimental.pallas import tpu as pltpu
 from jax.sharding import PartitionSpec as P
 
 ROT = 64
@@ -51,7 +55,1014 @@
     return exponent / jnp.sum(exponent, -1, keepdims=True)
 
 
-def local(
+LOW = jnp.bfloat16
+FULL = jnp.float32
+
+
+def turn(array, axis, r_bit, x_bit, y_bit):
+    shape = array.shape
+    cut = array.reshape(shape[:axis] + (2, 2, 2, shape[axis] // 8) + shape[axis + 1 :])
+    for at, bit in ((axis, y_bit), (axis + 1, x_bit), (axis + 2, r_bit)):
+        cut = jnp.where(bit, jnp.flip(cut, at), cut)
+    return cut.reshape(shape)
+
+
+MESH = pl.DeviceIdType.MESH
+ANY = pl.BlockSpec(memory_space=pl.ANY)
+IN_VMEM = pl.BlockSpec(memory_space=pltpu.VMEM)
+VMEM_BYTES = 62 * 2**20
+COPIES = 96
+
+
+class Links:
+    def __init__(self, send_sem, recv_sem, line=0):
+        self.send_sem, self.recv_sem, self.sent, self.count = send_sem, recv_sem, [], 0
+        self.r, self.f, self.t = (lax.axis_index(name) for name in ("replica", "fsdp", "tensor"))
+        self.xb, self.yb = lax.rem(self.f, 2), lax.div(self.f, 2)
+        self.x = (self.r, self.f + 1 - 2 * self.xb, self.t)
+        self.y = (self.r, lax.rem(self.f + 2, 4), self.t)
+        self.core = (1 - self.r, self.f, self.t)
+        self.peers = [self.x, self.y, self.core]
+        if line:
+            self.line = line
+            self.left, self.right, self.across = (
+                (self.r, self.f, lax.rem(self.t + step, line)) for step in (line - 1, 1, 2)
+            )
+            self.pair = (self.r, self.f, self.t + 1 - 2 * lax.rem(self.t, 2))
+            self.peers += [self.left, self.right, self.across]
+
+    def meet(self):
+        barrier = pltpu.get_barrier_semaphore()
+        for peer in self.peers:
+            pl.semaphore_signal(barrier, inc=1, device_id=peer, device_id_type=MESH)
+        pl.semaphore_wait(barrier, len(self.peers))
+
+    def prepare(self, source, target, peer):
+        k = self.count
+        self.count += 1
+        return pltpu.make_async_remote_copy(
+            src_ref=source,
+            dst_ref=target,
+            send_sem=self.send_sem.at[k],
+            recv_sem=self.recv_sem.at[k],
+            device_id=peer,
+            device_id_type=MESH,
+        )
+
+    def send(self, source, target, peer):
+        copy = self.prepare(source, target, peer)
+        copy.start()
+        self.sent.append(copy)
+        return copy
+
+    def end(self):
+        for copy in self.sent:
+            copy.wait_send()
+
+    def block(self, i):
+        bits = [(1 - bit) if i >> at & 1 else bit for at, bit in ((2, self.yb), (1, self.xb), (0, self.r))]
+        return (bits[0] * 2 + bits[1]) * 2 + bits[2]
+
+
+class Local:
+    def __init__(self, sem):
+        self.sem, self.count, self.open = sem, 0, []
+
+    def start(self, source, target):
+        copy = pltpu.make_async_copy(source, target, self.sem.at[self.count])
+        self.count += 1
+        copy.start()
+        self.open.append(copy)
+        return copy
+
+    def wait(self, *copies):
+        for copy in copies:
+            copy.wait()
+            self.open = [other for other in self.open if other is not copy]
+
+    def end(self):
+        self.wait(*list(self.open))
+
+
+def at_rows(ref, start, size):
+    return ref.at[pl.ds(start, size), :]
+
+
+def at_columns(ref, start, size):
+    return ref.at[:, pl.ds(start, size)]
+
+
+class Gathered:
+    def __init__(self, links, local, shard, full, cut, unit):
+        self.links, self.local, self.full, self.cut, self.unit = links, local, full, cut, unit
+        mine = cut(shard, pl.multiple_of(links.r * unit, unit), unit)
+        self.copies = [
+            local.start(mine, self.at(0)),
+            local.start(cut(shard, pl.multiple_of((1 - links.r) * unit, unit), unit), self.at(1)),
+        ]
+        self.mine = mine
+
+    def at(self, block, start=0, size=None):
+        return self.cut(self.full, block * self.unit + start, self.unit if size is None else size)
+
+    def first(self):
+        self.from_x = self.links.send(self.mine, self.at(2), self.links.x)
+        self.from_y = self.links.send(self.mine, self.at(4), self.links.y)
+
+    def relay_x(self):
+        half = self.unit // 2
+        self.from_x.wait_recv()
+        self.far_top = self.links.send(self.at(2, 0, half), self.at(6, 0, half), self.links.y)
+        self.core_x = self.links.send(self.at(2), self.at(3), self.links.core)
+
+    def relay_y(self):
+        half = self.unit // 2
+        self.from_y.wait_recv()
+        self.far_end = self.links.send(self.at(4, half, half), self.at(6, half, half), self.links.x)
+        self.core_y = self.links.send(self.at(4), self.at(5), self.links.core)
+
+    def relay_far(self):
+        self.far_top.wait_recv()
+        self.far_end.wait_recv()
+        self.core_far = self.links.send(self.at(6), self.at(7), self.links.core)
+
+    def whole(self):
+        self.local.wait(*self.copies)
+        for copy in (self.core_x, self.core_y, self.core_far):
+            copy.wait_recv()
+
+
+def tile_of(j, size):
+    return pl.ds(pl.multiple_of(j * size, size), size)
+
+
+def dot(left, right):
+    return jnp.dot(left, right, preferred_element_type=FULL)
+
+
+def spin(values_in, cosine, sine_one, sine_two):
+    head = values_in[:, :128]
+    turned_head = (
+        head * cosine + pltpu.roll(head, 96, 1) * sine_one + pltpu.roll(head, 32, 1) * sine_two
+    )
+    return jnp.concatenate([turned_head, values_in[:, 128:]], -1)
+
+
+def gather_kernel(
+    score_scale,
+    x_hbm, g_hbm, wh_hbm, wo_hbm, we_hbm, ws_hbm, vecs, key_pos, query_pos, cosine, sine_one, sine_two,
+    we, ws, wo_out, act_out, slope_out, n2t_out, up_out, ctx_out, red_heads, red_out, red_shrink, sums,
+    wh, wo, xr, g, n1, n2, n1t, n2t, stat, qkv_away, qkv, dctx_away, dctx, ctxt, ctxt_away,
+    pg, pg_away, kvg, kvg_away, kvg_got, got_heads, got_out, got_shrink, local_sem, tile_sem, send_sem, recv_sem,
+):
+    links, local = Links(send_sem, recv_sem), Local(local_sem)
+    tokens, width = xr.shape
+    hd = dctx.shape[1]
+    unit = width // 8
+    blocks = range(8)
+    x_in, g_in = [], []
+    for i in blocks:
+        cols = pl.ds(pl.multiple_of(links.block(i) * unit, unit), unit)
+        x_in.append(local.start(x_hbm.at[:, cols], xr.at[:, pl.ds(i * unit, unit)]))
+        g_in.append(local.start(g_hbm.at[:, cols], g.at[:, pl.ds(i * unit, unit)]))
+    links.meet()
+    heads = Gathered(links, local, wh_hbm, wh, at_rows, unit)
+    output = Gathered(links, local, wo_hbm, wo, at_columns, unit)
+    expand = Gathered(links, local, we_hbm, we, at_rows, unit)
+    shrink = Gathered(links, local, ws_hbm, ws, at_columns, unit)
+    heads.first()
+    output.first()
+
+    local.wait(*x_in)
+
+    def norm_rows(c, carry):
+        rows = tile_of(c, 64)
+        value = xr[rows, :].astype(FULL)
+        average = jnp.mean(value, -1, keepdims=True)
+        centred = value - average
+        inverse = lax.rsqrt(jnp.mean(centred * centred, -1, keepdims=True) + NORM_EPS)
+        normal = centred * inverse
+        stat[rows, :] = jnp.concatenate(
+            [jnp.broadcast_to(average, (64, 128)), jnp.broadcast_to(inverse, (64, 128))], -1
+        )
+        n1[rows, :] = (normal * vecs[0:1, :] + vecs[1:2, :]).astype(LOW)
+        n2[rows, :] = (normal * vecs[2:3, :] + vecs[3:4, :]).astype(LOW)
+        return carry
+
+    lax.fori_loop(0, tokens // 64, norm_rows, 0)
+
+    def turn_tiles(j, carry):
+        cols = tile_of(j, unit)
+        n1t[cols, :] = n1[:, cols].T
+        n2t[cols, :] = n2[:, cols].T
+        return carry
+
+    lax.fori_loop(0, 8, turn_tiles, 0)
+    local.start(n2t, n2t_out)
+    sums[...] = jnp.zeros_like(sums)
+    local.wait(*g_in)
+    for i in blocks:
+        cols = pl.ds(pl.multiple_of(links.block(i) * unit, unit), unit)
+        sums[4:5, cols] = jnp.sum(g[:, i * unit : (i + 1) * unit].astype(FULL), 0, keepdims=True)
+
+    heads.relay_x()
+    heads.relay_y()
+    output.relay_x()
+    output.relay_y()
+    heads.relay_far()
+    expand.first()
+    output.relay_far()
+    heads.whole()
+
+    own, away = links.yb * 3 * hd, (1 - links.yb) * 3 * hd
+
+    def project(start, target):
+        def one(c, carry):
+            cols = pl.ds(pl.multiple_of(start + c * hd, hd), hd)
+            value = dot(n1[...], wh[:, cols]) + vecs[5:6, cols]
+            spun = spin(value, cosine[:tokens, :], sine_one[:tokens, :], sine_two[:tokens, :])
+            target[c, :tokens, :] = jnp.where(c < 2, spun, value).astype(LOW)
+            return carry
+
+        lax.fori_loop(0, 3, one, 0)
+
+    project(away, qkv_away)
+    qkv_from_y = links.send(qkv_away, qkv.at[:, pl.ds(tokens, tokens), :], links.y)
+    project(own, qkv)
+    kv_from_x = links.send(
+        qkv.at[pl.ds(1, 2), pl.ds(0, tokens), :], qkv.at[pl.ds(1, 2), pl.ds(2 * tokens, tokens), :], links.x
+    )
+    output.whole()
+    local.start(wo, wo_out)
+    rows_own = pl.ds(pl.multiple_of(links.yb * hd, hd), hd)
+    rows_away = pl.ds(pl.multiple_of((1 - links.yb) * hd, hd), hd)
+    dctx_away[...] = contract_last(g[...], wo[rows_away, :]).astype(LOW)
+    dctx_from_y = links.send(dctx_away, dctx.at[pl.ds(tokens, tokens), :], links.y)
+    dctx[:tokens, :] = contract_last(g[...], wo[rows_own, :]).astype(LOW)
+
+    qkv_from_y.wait_recv()
+    kv_from_far = links.send(
+        qkv.at[pl.ds(1, 2), pl.ds(tokens, tokens), :],
+        qkv.at[pl.ds(1, 2), pl.ds(3 * tokens, tokens), :],
+        links.x,
+    )
+    expand.relay_x()
+    expand.relay_y()
+    shrink.first()
+    dctx_from_y.wait_recv()
+    kv_from_x.wait_recv()
+    kv_from_far.wait_recv()
+
+    def attention(kt, vt, dk, dv, prob, wgt, prob_low, grad_low):
+        keys = qkv.shape[1]
+        step = 512
+        parts = [pl.ds(i * step, step) for i in range(keys // step)]
+        for part in parts:
+            kt[:, part] = qkv[1, part, :].T
+            vt[:, part] = qkv[2, part, :].T
+        dk[...] = jnp.zeros_like(dk)
+        dv[...] = jnp.zeros_like(dv)
+
+        def one(b, carry):
+            rows = tile_of(b, hd)
+            query, grad = qkv[0, rows, :], dctx[rows, :]
+            spot = query_pos[:, rows]
+            top = jnp.full((1, hd), MASKED, FULL)
+            for part in parts:
+                scores = contract_last(qkv[1, part, :], query) * score_scale
+                scores = jnp.where(key_pos[part, :] <= spot, scores, MASKED)
+                prob[part, :] = scores
+                top = jnp.maximum(top, jnp.max(scores, 0, keepdims=True))
+            total = jnp.zeros((1, hd), FULL)
+            for part in parts:
+                exponent = jnp.exp(prob[part, :] - top)
+                prob[part, :] = exponent
+                total = total + jnp.sum(exponent, 0, keepdims=True)
+            share = 1.0 / total
+            inner = jnp.zeros((1, hd), FULL)
+            for part in parts:
+                weight = contract_last(qkv[2, part, :], grad)
+                chance = prob[part, :] * share
+                prob[part, :] = chance
+                prob_low[part, :] = chance.astype(LOW)
+                wgt[part, :] = weight
+                inner = inner + jnp.sum(chance * weight, 0, keepdims=True)
+            for part in parts:
+                grad_low[part, :] = (prob[part, :] * (wgt[part, :] - inner)).astype(LOW)
+            context = dot(vt[...], prob_low[...]).astype(LOW)
+            query_grad = dot(kt[...], grad_low[...]) * score_scale
+            for part in parts:
+                dv[part, :] += dot(prob_low[part, :], grad)
+                dk[part, :] += dot(grad_low[part, :], query)
+            turned_grad = spin(query_grad.T, cosine[rows, :], -sine_one[rows, :], -sine_two[rows, :]).astype(LOW)
+            return context, turned_grad
+
+        def here(b, carry):
+            context, turned_grad = one(b, carry)
+            rows = tile_of(b, hd)
+            ctxt[rows_own, rows] = context
+            pg[rows, pl.ds(pl.multiple_of(own, hd), hd)] = turned_grad
+            return carry
+
+        def there(b, carry):
+            context, turned_grad = one(b + tokens // hd, carry)
+            rows = tile_of(b, hd)
+            ctxt_away[:, rows] = context
+            pg_away[rows, :hd] = turned_grad
+            return carry
+
+        lax.fori_loop(0, tokens // hd, there, 0)
+        lax.fori_loop(0, tokens // hd, here, 0)
+        for i, total in enumerate((dk, dv)):
+            kvg_away[i, :, :] = total[2 * tokens :, :].astype(LOW)
+            kvg[i, :, :] = total[: 2 * tokens, :]
+
+    keys = qkv.shape[1]
+    pl.run_scoped(
+        attention,
+        pltpu.VMEM((hd, keys), LOW),
+        pltpu.VMEM((hd, keys), LOW),
+        pltpu.VMEM((keys, hd), FULL),
+        pltpu.VMEM((keys, hd), FULL),
+        pltpu.VMEM((keys, hd), FULL),
+        pltpu.VMEM((keys, hd), FULL),
+        pltpu.VMEM((keys, hd), LOW),
+        pltpu.VMEM((keys, hd), LOW),
+    )
+    ctx_from_y = links.send(ctxt_away, ctxt.at[rows_own, :], links.y)
+    kvg_from_x = links.send(kvg_away, kvg_got, links.x)
+    expand.relay_far()
+    expand.whole()
+
+    def rest(tiles, slope, actt, send_heads, send_out, send_shrink):
+        act = n1
+
+        def load(j):
+            return pltpu.make_async_copy(
+                we.at[:, tile_of(j, unit)], tiles.at[lax.rem(j, 2)], tile_sem.at[lax.rem(j, 2)]
+            )
+
+        load(0).start()
+
+        def forward(j, carry):
+            @pl.when(j < 7)
+            def _():
+                load(j + 1).start()
+
+            load(j).wait()
+            cols = tile_of(j, unit)
+            value = dot(n2[...], tiles[lax.rem(j, 2)]) + vecs[4:5, cols]
+            normal_share = 0.5 * (1.0 + lax.erf(value * (0.5**0.5)))
+            low_act = (value * normal_share).astype(LOW)
+            act[:, cols] = low_act
+            actt[cols, :] = low_act.T
+            density = jnp.exp(value * value * -0.5) * 0.3989422804014327
+            slope[:, cols] = (normal_share + value * density).astype(LOW)
+            return carry
+
+        lax.fori_loop(0, 4, forward, 0)
+        shrink.relay_x()
+        shrink.relay_y()
+        lax.fori_loop(4, 8, forward, 0)
+        local.start(act, act_out)
+        local.start(slope, slope_out)
+
+        kvg_from_x.wait_recv()
+        for i in range(2):
+            for away_rows, target in ((False, pg), (True, pg_away)):
+                rows = pl.ds(tokens if away_rows else 0, tokens)
+                total = kvg[i, rows, :] + kvg_got[i, rows, :].astype(FULL)
+                if i == 0:
+                    total = spin(total * score_scale, cosine[rows, :], -sine_one[rows, :], -sine_two[rows, :])
+                start = (0 if away_rows else own) + (1 + i) * hd
+                target[:, pl.ds(pl.multiple_of(start, hd), hd)] = total.astype(LOW)
+        pg_from_y = links.send(pg_away, pg.at[:, pl.ds(pl.multiple_of(own, 3 * hd), 3 * hd)], links.y)
+
+        def shrink_block(i, target, extra):
+            def one(c, carry):
+                rows = tile_of(c, 512)
+                part = dot(actt[rows, :], g[:, i * unit : (i + 1) * unit])
+                if extra is not None:
+                    part = part + extra[rows, :].astype(FULL)
+                target[rows, :] = part.astype(LOW)
+                return carry
+
+            lax.fori_loop(0, actt.shape[0] // 512, one, 0)
+
+        shrink_got, out_got, heads_got = [], [], []
+        for k in range(4):
+            shrink_block(2 * k + 1, send_shrink.at[k], None)
+            shrink_got.append(links.send(send_shrink.at[k], got_shrink.at[k], links.core))
+        ctx_from_y.wait_recv()
+        local.start(ctxt, ctx_out)
+        for k in range(4):
+            i = 2 * k + 1
+            send_out[k, :, :] = dot(ctxt[...], g[:, i * unit : (i + 1) * unit]).astype(LOW)
+            out_got.append(links.send(send_out.at[k], got_out.at[k], links.core))
+        for k in range(4):
+            shrink_got[k].wait_recv()
+            shrink_block(2 * k, got_shrink.at[k], got_shrink.at[k])
+            local.start(got_shrink.at[k], red_shrink.at[k])
+        for k in range(4):
+            out_got[k].wait_recv()
+            total = dot(ctxt[...], g[:, 2 * k * unit : (2 * k + 1) * unit])
+            got_out[k, :, :] = (total + got_out[k, :, :].astype(FULL)).astype(LOW)
+            local.start(got_out.at[k], red_out.at[k])
+        shrink.relay_far()
+        pg_from_y.wait_recv()
+        for k in range(4):
+            rows = pl.ds((2 * k + 1) * unit, unit)
+            send_heads[k, :, :] = dot(n1t[rows, :], pg[...]).astype(LOW)
+            heads_got.append(links.send(send_heads.at[k], got_heads.at[k], links.core))
+
+        up = n2
+        for i in blocks:
+            cols = slice(i * unit, (i + 1) * unit)
+            grad = contract_last(pg[...], wh[cols, :])
+            normal = (xr[:, cols].astype(FULL) - stat[:, 0:1]) * stat[:, 128:129]
+            place = pl.ds(pl.multiple_of(links.block(i) * unit, unit), unit)
+            sums[0:1, place] = jnp.sum(grad * normal, 0, keepdims=True)
+            sums[1:2, place] = jnp.sum(grad, 0, keepdims=True)
+            up[:, cols] = (grad * vecs[0:1, cols]).astype(LOW)
+        local.start(up, up_out)
+        sums[6:7, : pg.shape[1]] = jnp.sum(pg[...].astype(FULL), 0, keepdims=True)
+        for k in range(4):
+            heads_got[k].wait_recv()
+            total = dot(n1t[2 * k * unit : (2 * k + 1) * unit, :], pg[...])
+            got_heads[k, :, :] = (total + got_heads[k, :, :].astype(FULL)).astype(LOW)
+            local.start(got_heads.at[k], red_heads.at[k])
+        shrink.whole()
+        links.end()
+        local.end()
+
+    pl.run_scoped(
+        rest,
+        pltpu.VMEM((2, width, unit), LOW),
+        pltpu.VMEM(n2.shape, LOW),
+        pltpu.VMEM((we.shape[1], tokens), LOW),
+        pltpu.VMEM(got_heads.shape, LOW),
+        pltpu.VMEM(got_out.shape, LOW),
+        pltpu.VMEM(got_shrink.shape, LOW),
+    )
+
+
+def gather_call(x, g, heads_rows, output_rows, expand_weight, shrink_weight, vecs, key_pos, query_pos, tables):
+    tokens, width = x.shape
+    heads_wide, out_wide, units = heads_rows.shape[1], output_rows.shape[0], expand_weight.shape[1]
+    hd = heads_wide // 6
+    keys = key_pos.shape[0]
+    unit = width // 8
+    low = lambda *shape: jax.ShapeDtypeStruct(shape, LOW)
+    outs = [
+        low(width, units),
+        low(units, width),
+        low(out_wide, width),
+        low(tokens, units),
+        low(tokens, units),
+        low(width, tokens),
+        low(tokens, width),
+        low(out_wide, tokens),
+        low(4, unit, heads_wide),
+        low(4, out_wide, unit),
+        low(4, units, unit),
+        jax.ShapeDtypeStruct((8, width), FULL),
+    ]
+    vm = lambda *shape: pltpu.VMEM(shape, LOW)
+    scratch = [
+        vm(width, heads_wide),
+        vm(out_wide, width),
+        vm(tokens, width),
+        vm(tokens, width),
+        vm(tokens, width),
+        vm(tokens, width),
+        vm(width, tokens),
+        vm(width, tokens),
+        pltpu.VMEM((tokens, 256), FULL),
+        vm(3, tokens, hd),
+        vm(3, keys, hd),
+        vm(tokens, hd),
+        vm(2 * tokens, hd),
+        vm(out_wide, tokens),
+        vm(hd, tokens),
+        vm(tokens, heads_wide),
+        vm(tokens, 3 * hd),
+        pltpu.VMEM((2, 2 * tokens, hd), FULL),
+        vm(2, 2 * tokens, hd),
+        vm(2, 2 * tokens, hd),
+        vm(4, unit, heads_wide),
+        vm(4, out_wide, unit),
+        vm(4, units, unit),
+        pltpu.SemaphoreType.DMA((64,)),
+        pltpu.SemaphoreType.DMA((2,)),
+        pltpu.SemaphoreType.DMA((COPIES,)),
+        pltpu.SemaphoreType.DMA((COPIES,)),
+    ]
+    return pl.pallas_call(
+        functools.partial(gather_kernel, hd**-0.5),
+        out_shape=outs,
+        in_specs=[ANY] * 6 + [IN_VMEM] * 6,
+        out_specs=[ANY] * 11 + [IN_VMEM],
+        scratch_shapes=scratch,
+        compiler_params=pltpu.CompilerParams(
+            collective_id=0, has_side_effects=True, vmem_limit_bytes=VMEM_BYTES
+        ),
+    )(x, g, heads_rows, output_rows, expand_weight, shrink_weight, vecs, key_pos, query_pos, *tables)
+
+
+class Scattered:
+    def __init__(self, links, local, block, cut, unit, via, got, stage, own, loaded):
+        self.links, self.local, self.block, self.cut, self.unit = links, local, block, cut, unit
+        self.via, self.got, self.stage, self.own = via, got, stage, own
+        self.half = unit // 2
+        if loaded:
+            self.loads = [
+                local.start(cut(block(1), self.half, self.half), stage.at[0]),
+                local.start(cut(block(2), 0, self.half), stage.at[1]),
+                local.start(block(0), own),
+            ]
+
+    def first(self):
+        half, cut, far = self.half, self.cut, self.block(3)
+        self.via_x = self.links.send(cut(far, 0, half), self.via.at[0], self.links.x)
+        self.via_y = self.links.send(cut(far, half, half), self.via.at[1], self.links.y)
+
+    def direct(self):
+        half, cut = self.half, self.cut
+        self.x_top = self.links.send(cut(self.block(1), 0, half), cut(self.got.at[0], 0, half), self.links.x)
+        self.y_end = self.links.send(cut(self.block(2), half, half), cut(self.got.at[1], half, half), self.links.y)
+
+    def second(self):
+        half, cut = self.half, self.cut
+        self.local.wait(*self.loads[:2])
+        self.via_x.wait_recv()
+        add_rows(self.stage.at[1], self.stage.at[1], self.via.at[0])
+        self.y_top = self.links.send(self.stage.at[1], cut(self.got.at[1], 0, half), self.links.y)
+        self.via_y.wait_recv()
+        add_rows(self.stage.at[0], self.stage.at[0], self.via.at[1])
+        self.x_end = self.links.send(self.stage.at[0], cut(self.got.at[0], half, half), self.links.x)
+
+    def third(self, total, place):
+        for copy in (self.x_top, self.x_end, self.y_top, self.y_end):
+            copy.wait_recv()
+        self.local.wait(self.loads[2])
+        add_rows(total, self.own, self.got.at[0], self.got.at[1])
+        self.kept = self.local.start(total, place)
+        self.other = self.links.send(total, place, self.links.core)
+
+
+def add_rows(target, *parts):
+    rows, wide = target.shape
+    step = min(rows, 32 if wide > 512 else 256)
+
+    def one(c, carry):
+        at = pl.ds(pl.multiple_of(c * step, step), step)
+        total = parts[0][at, :].astype(FULL)
+        for part in parts[1:]:
+            total = total + part[at, :].astype(FULL)
+        target[at, :] = total.astype(target.dtype)
+        return carry
+
+    lax.fori_loop(0, rows // step, one, 0)
+
+
+class Line:
+    def __init__(self, links, part, low_got, high_got, final, finish):
+        self.links, self.part, self.final, self.finish = links, part, final, finish
+        self.low_got, self.high_got = low_got, high_got
+        self.half = part.shape[0] // 2
+        self.step = self.half // CHUNKS
+        self.first, self.last = links.t == 0, links.t == links.line - 1
+        self.up = {}
+        self.down = {}
+
+    def rows(self, c, low):
+        return pl.ds((0 if low else self.half) + c * self.step, self.step)
+
+    def make(self, c, low, back):
+        rows = self.rows(c, low)
+        got = self.low_got if low else self.high_got
+        source = (self.final if back else self.part).at[rows, :]
+        target = self.final.at[rows, :] if back else got.at[pl.ds(c * self.step, self.step), :]
+        return self.links.prepare(source, target, self.links.left if low != back else self.links.right)
+
+    def toward(self, c, ends):
+        for low in (True, False):
+            key = (c, low)
+            if ends:
+                self.up[key] = self.make(c, low, False)
+            source_end, target_end = (self.last, self.first) if low else (self.first, self.last)
+            copy = self.up[key]
+            if ends:
+                pl.when(source_end)(copy.start)
+                continue
+            rows = self.rows(c, low)
+            got = (self.low_got if low else self.high_got).at[pl.ds(c * self.step, self.step), :]
+
+            def take(copy=copy, rows=rows, got=got):
+                copy.wait_recv()
+                add_rows(self.part.at[rows, :], self.part.at[rows, :], got)
+
+            pl.when(jnp.logical_not(source_end))(take)
+            between = jnp.logical_and(jnp.logical_not(source_end), jnp.logical_not(target_end))
+            pl.when(between)(copy.start)
+
+    def back(self, c):
+        for low in (True, False):
+            copy = self.make(c, low, True)
+            self.down[(c, low)] = copy
+            source_end, target_end = (self.first, self.last) if low else (self.last, self.first)
+            rows = self.rows(c, low)
+
+            def end(copy=copy, rows=rows):
+                self.finish(rows)
+                copy.start()
+
+            def between(copy=copy):
+                copy.wait_recv()
+
+            pl.when(source_end)(end)
+            pl.when(jnp.logical_not(source_end))(between)
+            pl.when(jnp.logical_and(jnp.logical_not(source_end), jnp.logical_not(target_end)))(copy.start)
+
+    def end(self):
+        for (c, low), copy in self.up.items():
+            pl.when(jnp.logical_not(self.first if low else self.last))(copy.wait_send)
+        for (c, low), copy in self.down.items():
+            pl.when(jnp.logical_not(self.last if low else self.first))(copy.wait_send)
+
+
+CHUNKS = 4
+
+
+def scatter_kernel(
+    line_size,
+    we_hbm, ws_hbm, wo_hbm, act_hbm, slope_hbm, n2t_hbm, up_hbm, ctxt_hbm, red_heads, red_out, red_shrink, x_hbm, g_hbm,
+    vecs, sums_in,
+    layer_out, input_grad, heads_grad, output_grad, expand_grad, shrink_grad, got_expand, sums_out,
+    ws, we, wo, act, slope, n2t, up, ctxt, g, part_branch, final_branch, final_up, low_branch, high_branch, low_up, high_up,
+    via_h, got_h, stage_h, own_h, via_o, got_o, stage_o, own_o, via_s, got_s, stage_s, own_s, via_e, got_e,
+    total_rows, total_columns, total_out, grad_rows, sums, sums_got, local_sem, send_sem, recv_sem,
+):
+    links, local = Links(send_sem, recv_sem, line_size), Local(local_sem)
+    tokens, width = g.shape
+    unit = width // 8
+    blocks = range(8)
+    place = [pl.ds(pl.multiple_of(links.block(i) * unit, unit), unit) for i in blocks]
+
+    def here(i):
+        return pl.ds(i * unit, unit)
+
+    first_loads = [local.start(ws_hbm, ws), local.start(act_hbm, act), local.start(ctxt_hbm, ctxt), local.start(wo_hbm, wo)]
+    g_loads = [local.start(g_hbm.at[:, place[i]], g.at[:, here(i)]) for i in blocks]
+    slope_load = local.start(slope_hbm, slope)
+    we_load, up_load, n2t_load = local.start(we_hbm, we), local.start(up_hbm, up), local.start(n2t_hbm, n2t)
+    links.meet()
+
+    shrink = Scattered(links, local, lambda k: red_shrink.at[k], at_columns, unit, via_s, got_s, stage_s, own_s, True)
+    heads = Scattered(links, local, lambda k: red_heads.at[k], at_rows, unit, via_h, got_h, stage_h, own_h, True)
+    output = Scattered(links, local, lambda k: red_out.at[k], at_columns, unit, via_o, got_o, stage_o, own_o, True)
+    shrink.first()
+    heads.first()
+    output.first()
+
+    local.wait(*first_loads)
+    context = ctxt[...].T
+
+    def branch_tile(j, carry):
+        cols = tile_of(j, unit)
+        part_branch[:, cols] = (dot(context, wo[:, cols]) + dot(act[...], ws[:, cols])).astype(LOW)
+        return carry
+
+    lax.fori_loop(0, 8, branch_tile, 0)
+    x = act
+    x_loads = [local.start(x_hbm.at[:, place[i]], x.at[:, here(i)]) for i in blocks]
+
+    def finish_branch(rows):
+        def one(c, carry):
+            at = pl.ds(pl.multiple_of(rows.start + c * 16, 16), 16)
+            total = x[at, :].astype(FULL) + part_branch[at, :].astype(FULL) + vecs[1:2, :]
+            final_branch[at, :] = total.astype(LOW)
+            return carry
+
+        lax.fori_loop(0, rows.size // 16, one, 0)
+
+    def finish_up(rows):
+        final_up[rows, :] = up[rows, :]
+
+    line_branch = Line(links, part_branch, low_branch, high_branch, final_branch, finish_branch)
+    line_up = Line(links, up, low_up, high_up, final_up, finish_up)
+    for c in range(CHUNKS):
+        line_branch.toward(c, True)
+
+    local.wait(*g_loads, slope_load)
+    sums[0, :, :] = sums_in[...]
+
+    def hidden_tile(j, carry):
+        cols = tile_of(j, unit)
+        grad = (contract_last(g[...], ws[cols, :]) * slope[:, cols].astype(FULL)).astype(LOW)
+        slope[:, cols] = grad
+        sums[0, 5:6, cols] = jnp.sum(grad.astype(FULL), 0, keepdims=True)
+        return carry
+
+    lax.fori_loop(0, 8, hidden_tile, 0)
+    local.wait(*x_loads, we_load, up_load, n2t_load)
+    shrink.direct()
+    heads.direct()
+    output.direct()
+
+    def up_block(i):
+        cols = here(i)
+        grad = contract_last(slope[...], we[i * unit : (i + 1) * unit, :])
+        value = x[:, cols].astype(FULL)
+        normal = (value - average) * inverse
+        sums[0, 2:3, place[i]] = jnp.sum(grad * normal, 0, keepdims=True)
+        sums[0, 3:4, place[i]] = jnp.sum(grad, 0, keepdims=True)
+        up[:, cols] = (up[:, cols].astype(FULL) + grad * vecs[0:1, cols]).astype(LOW)
+
+    total = jnp.zeros((tokens, 1), FULL)
+    for i in blocks:
+        total = total + jnp.sum(x[:, here(i)].astype(FULL), -1, keepdims=True)
+    average = total * (1.0 / width)
+    total = jnp.zeros((tokens, 1), FULL)
+    for i in blocks:
+        centred = x[:, here(i)].astype(FULL) - average
+        total = total + jnp.sum(centred * centred, -1, keepdims=True)
+    inverse = lax.rsqrt(total * (1.0 / width) + NORM_EPS)
+
+    line_branch.toward(0, False)
+    for i in range(4):
+        up_block(i)
+    line_branch.toward(1, False)
+    for i in range(4, 8):
+        up_block(i)
+    for c in range(CHUNKS):
+        line_up.toward(c, True)
+    line_branch.toward(2, False)
+    shrink.second()
+
+    expand_got = []
+
+    def expand_block(i, target):
+        def one(c, carry):
+            cols = tile_of(c, 512)
+            part = dot(n2t[i * unit : (i + 1) * unit, :], slope[:, cols])
+            if target is we:
+                part = part + target[(i // 2) * unit : (i // 2 + 1) * unit, cols].astype(FULL)
+            target[(i // 2) * unit : (i // 2 + 1) * unit, cols] = part.astype(LOW)
+            return carry
+
+        lax.fori_loop(0, slope.shape[1] // 512, one, 0)
+
+    for k in (3, 1, 2, 0):
+        expand_block(2 * k + 1, ws)
+        rows = pl.ds(k * unit, unit)
+        expand_got.append((k, links.send(ws.at[rows, :], got_expand.at[k], links.core)))
+    line_branch.toward(3, False)
+    heads.second()
+    output.second()
+    loads = []
+    for k, copy in expand_got:
+        copy.wait_recv()
+        loads.append(local.start(got_expand.at[k], we.at[pl.ds(k * unit, unit), :]))
+    line_branch.back(0)
+    for (k, copy), load in zip(expand_got, loads):
+        local.wait(load)
+        expand_block(2 * k, we)
+    expand = Scattered(
+        links, local, lambda k: we.at[pl.ds(k * unit, unit), :], at_rows, unit, via_e, got_e, None, None, False
+    )
+    expand.first()
+    expand.direct()
+
+    hops = []
+
+    def hop(s, peer):
+        hops.append(links.send(sums.at[s], sums_got.at[s], peer))
+
+    def hop_end(s):
+        hops[s].wait_recv()
+        sums[s + 1, :, :] = sums[s, :, :] + sums_got[s, :, :]
+
+    hop(0, links.core)
+    line_up.toward(0, False)
+    line_branch.back(1)
+    hop_end(0)
+    hop(1, links.x)
+    line_up.toward(1, False)
+    line_branch.back(2)
+    hop_end(1)
+    hop(2, links.y)
+    shrink.third(total_columns, shrink_grad.at[:, pl.ds(pl.multiple_of(links.r * unit, unit), unit)])
+    line_up.toward(2, False)
+    line_branch.back(3)
+    hop_end(2)
+    hop(3, links.pair)
+    for i in blocks:
+        local.start(final_branch.at[:, here(i)], layer_out.at[:, place[i]])
+    line_up.toward(3, False)
+    line_up.back(0)
+    output.third(total_out, output_grad.at[:, pl.ds(pl.multiple_of(links.r * unit, unit), unit)])
+    hop_end(3)
+    hop(4, links.across)
+    heads.third(total_rows.at[:, pl.ds(0, own_h.shape[1])], heads_grad.at[pl.ds(pl.multiple_of(links.r * unit, unit), unit), :])
+    line_up.back(1)
+    expand.via_x.wait_recv()
+    top, end = pl.ds(2 * unit, unit // 2), pl.ds(unit + unit // 2, unit // 2)
+    add_rows(we.at[top, :], we.at[top, :], via_e.at[0])
+    expand.y_top = links.send(we.at[top, :], got_e.at[1, pl.ds(0, unit // 2), :], links.y)
+    expand.via_y.wait_recv()
+    add_rows(we.at[end, :], we.at[end, :], via_e.at[1])
+    expand.x_end = links.send(we.at[end, :], got_e.at[0, pl.ds(unit // 2, unit // 2), :], links.x)
+    hop_end(4)
+    sums_out[0:4, :] = sums[5, 0:4, :]
+    sums_out[4:8, :] = sums[3, 4:8, :]
+    line_up.back(2)
+    line_up.back(3)
+
+    out_copies = {}
+    step = grad_rows.shape[1]
+    for c in range(tokens // step):
+        slot = c % 2
+        if c >= 2:
+            local.wait(*out_copies[c - 2])
+        rows = pl.ds(c * step, step)
+        value = x[rows, :].astype(FULL)
+        centred = value - jnp.mean(value, -1, keepdims=True)
+        scale = lax.rsqrt(jnp.mean(centred * centred, -1, keepdims=True) + NORM_EPS)
+        normal = centred * scale
+        upstream = final_up[rows, :].astype(FULL)
+        inner = upstream - jnp.mean(upstream, -1, keepdims=True)
+        inner = inner - normal * jnp.mean(upstream * normal, -1, keepdims=True)
+        grad_rows[slot, :, :] = g[rows, :].astype(FULL) + inner * scale
+        out_copies[c] = [
+            local.start(grad_rows.at[slot, :, here(i)], input_grad.at[rows, place[i]]) for i in blocks
+        ]
+
+    for copy in (expand.x_top, expand.x_end, expand.y_top, expand.y_end):
+        copy.wait_recv()
+    heads.other.wait_send()
+    local.wait(heads.kept)
+    add_rows(total_rows, we.at[pl.ds(0, unit), :], got_e.at[0], got_e.at[1])
+    spot = expand_grad.at[pl.ds(pl.multiple_of(links.r * unit, unit), unit), :]
+    local.start(total_rows, spot)
+    last = links.send(total_rows, spot, links.core)
+    for copy in (shrink.other, output.other, heads.other, last):
+        copy.wait_recv()
+    links.sent = [copy for copy in links.sent if copy is not heads.other]
+    links.end()
+    line_branch.end()
+    line_up.end()
+    local.end()
+
+
+def scatter_call(line_size, arrays, x, g, vecs, sums):
+    tokens, width = x.shape
+    expand_full, shrink_full, output_full, act, slope, n2t, up, ctxt, red_heads, red_out, red_shrink = arrays
+    unit = width // 8
+    units, heads_wide, out_wide = act.shape[1], red_heads.shape[2], ctxt.shape[0]
+    low = lambda *shape: pltpu.VMEM(shape, LOW)
+    full = lambda *shape: pltpu.VMEM(shape, FULL)
+    half = unit // 2
+    outs = [
+        jax.ShapeDtypeStruct((tokens, width), LOW),
+        jax.ShapeDtypeStruct((tokens, width), FULL),
+        jax.ShapeDtypeStruct((2 * unit, heads_wide), FULL),
+        jax.ShapeDtypeStruct((out_wide, 2 * unit), FULL),
+        jax.ShapeDtypeStruct((2 * unit, units), FULL),
+        jax.ShapeDtypeStruct((units, 2 * unit), FULL),
+        jax.ShapeDtypeStruct((4, unit, units), LOW),
+        jax.ShapeDtypeStruct((8, width), FULL),
+    ]
+    scratch = [
+        low(units, width),
+        low(width, units),
+        low(out_wide, width),
+        low(tokens, units),
+        low(tokens, units),
+        low(width, tokens),
+        low(tokens, width),
+        low(out_wide, tokens),
+        low(tokens, width),
+        low(tokens, width),
+        low(tokens, width),
+        low(tokens, width),
+        *[low(tokens // 2, width)] * 4,
+        low(2, half, heads_wide), low(2, unit, heads_wide), low(2, half, heads_wide), low(unit, heads_wide),
+        low(2, out_wide, half), low(2, out_wide, unit), low(2, out_wide, half), low(out_wide, unit),
+        low(2, units, half), low(2, units, unit), low(2, units, half), low(units, unit),
+        low(2, half, units), low(2, unit, units),
+        full(unit, units),
+        full(units, unit),
+        full(out_wide, unit),
+        full(2, 32, width),
+        full(6, 8, width),
+        full(5, 8, width),
+        pltpu.SemaphoreType.DMA((224,)),
+        pltpu.SemaphoreType.DMA((COPIES,)),
+        pltpu.SemaphoreType.DMA((COPIES,)),
+    ]
+    return pl.pallas_call(
+        functools.partial(scatter_kernel, line_size),
+        out_shape=outs,
+        in_specs=[ANY] * 13 + [IN_VMEM] * 2,
+        out_specs=[ANY] * 7 + [IN_VMEM],
+        scratch_shapes=scratch,
+        compiler_params=pltpu.CompilerParams(
+            collective_id=1, has_side_effects=True, vmem_limit_bytes=VMEM_BYTES
+        ),
+    )(expand_full, shrink_full, output_full, act, slope, n2t, up, ctxt, red_heads, red_out, red_shrink, x, g, vecs, sums)
+
+
+def square_local(
+    layer_input,
+    block_order,
+    first_gain,
+    first_bias,
+    second_gain,
+    second_bias,
+    heads_weight,
+    heads_bias,
+    output_weight,
+    output_bias,
+    expand_weight,
+    expand_bias,
+    shrink_weight,
+    shrink_bias,
+    cotangent,
+):
+    tokens = layer_input.shape[1]
+    width = layer_input.shape[2]
+    replica, fsdp = lax.axis_index("replica"), lax.axis_index("fsdp")
+    r_bit, x_bit, y_bit = replica == 1, fsdp % 2 == 1, fsdp // 2 == 1
+
+    def turned(array, axis):
+        return turn(array, axis, r_bit, x_bit, y_bit)
+
+    heads_rows = heads_weight.reshape(heads_weight.shape[0], -1)
+    output_rows = output_weight.reshape(-1, output_weight.shape[2])
+    wide = heads_rows.shape[1]
+    gain_one, shift_one, gain_two, shift_two = (
+        turned(vec.astype(FULL), 0) for vec in (first_gain, first_bias, second_gain, second_bias)
+    )
+    vecs = jnp.stack(
+        [
+            gain_one,
+            shift_one,
+            gain_two,
+            shift_two,
+            expand_bias.astype(FULL),
+            jnp.pad(heads_bias.reshape(-1).astype(FULL), (0, width - wide)),
+            jnp.zeros((width,), FULL),
+            jnp.zeros((width,), FULL),
+        ]
+    )
+    order_row = block_order[0]
+    slots = fsdp ^ jnp.array([0, 2, 1, 3], jnp.int32)
+    order_here = order_row[slots]
+    offsets = jnp.arange(tokens, dtype=jnp.int32)
+    key_pos = (order_here[:, None] * tokens + offsets[None]).reshape(-1)
+    query_pos = key_pos[: 2 * tokens]
+    cosine, sine_part = rotary_tables(query_pos, ROT)
+    still = jnp.zeros((2 * tokens, 128 - ROT), FULL)
+    left, right = jnp.split(sine_part, 2, 1)
+    tables = (
+        jnp.concatenate([cosine, still + 1.0], 1),
+        jnp.concatenate([-left, jnp.zeros_like(right), still], 1),
+        jnp.concatenate([jnp.zeros_like(left), right, still], 1),
+    )
+    *gathered, sums = gather_call(
+        layer_input[0], cotangent[0], heads_rows, output_rows, expand_weight, shrink_weight,
+        vecs, key_pos[:, None], query_pos[None, :], tables,
+    )
+
+    second = jnp.stack([gain_two, turned(output_bias.astype(FULL) + shrink_bias.astype(FULL), 0)])
+    layer_output, input_grad, heads_grad, output_grad, expand_weight_grad, shrink_weight_grad, _, sums = scatter_call(
+        lax.axis_size("tensor"),
+        gathered,
+        layer_input[0],
+        cotangent[0],
+        jnp.pad(second, ((0, 6), (0, 0))),
+        sums,
+    )
+    return (
+        layer_output[None],
+        input_grad[None],
+        sums[0],
+        sums[1],
+        sums[2],
+        sums[3],
+        heads_grad.reshape(heads_weight.shape),
+        sums[6, :wide].reshape(heads_bias.shape),
+        output_grad.reshape(output_weight.shape),
+        sums[4],
+        expand_weight_grad,
+        sums[5],
+        shrink_weight_grad,
+        sums[4],
+    )
+
+
+def ring_local(
     layer_input,
     block_order,
     first_gain,
@@ -250,6 +1261,7 @@
         P(),
         P("replica", "fsdp", None),
     )
+    local = square_local if mesh.shape["fsdp"] == 4 and mesh.shape["replica"] == 2 and mesh.shape["tensor"] == 4 else ring_local
     return jax.shard_map(
         local,
         mesh=mesh,

time: 1490 us -> 609 us (0.41)
  waiting for transfers between devices: 1250 us -> 0 us
  Pallas kernels: 0 us -> 559 us
  matrix products: 119 us -> 0 us
  blocking collectives: 28.7 us -> 0 us
  other arithmetic: 31.3 us -> 6.83 us
    pallas_call x0 -> x2, Pallas kernels: none -> 559 us  [the longest x1 382 us: scatter_call(): pl.pallas_call(functools.partial(scatter_kernel, line_size), out_shape=ou...]
    reduce_scatter x6 -> x0, waiting for transfers between devices: 527 us -> none  [the longest x1 157 us: local(): lax.psum_scatter(shrink_weight_grad, 'fsdp', scatter_dimension=1, tiled=T...]
    psum x2 -> x0, waiting for transfers between devices: 437 us -> none  [the longest x1 430 us: local(): branch = lax.psum(branch_part, 'tensor')]
    all_gather x6 -> x0, waiting for transfers between devices: 279 us -> none  [the longest x1 71.3 us: local(): lax.all_gather(shrink_weight, 'fsdp', axis=1, tiled=True)]
    dot_general x26 -> x0, matrix products: 119 us -> none  [the longest x8 33.7 us: contract_last(): lax.dot_general(left_op, right_op, (((1,), (1,)), ((), ())), preferred_el...]
    psum x1 -> x0, blocking collectives: 28.7 us -> none  [local(): lax.psum((first_gain_grad, first_bias_grad, second_gain_grad, second_bias...]
    reduce_sum x10 -> x0, other arithmetic: 19.7 us -> none  [the longest x2 8.23 us: layer_norm(): return centred * lax.rsqrt(spread_sq + NORM_EPS) * gain_vec + shift_vec]
  transfers between devices with their start and end apart: 14 -> 0, of which waited for: 14 -> 0; matrix products, arithmetic and copies ran while one was open for 11% -> 0% of each run, Pallas kernels for 0% -> 0%
where the time goes in v2:
time: 609 us; the launch traced here: 600 us
  Pallas kernels  559 us (92%)
  local copies, waits for them, and re-layouts  32.1 us (5%)
  other arithmetic  6.83 us (1%)
    pallas_call x1, Pallas kernels, scatter_call(): pl.pallas_call(functools.partial(scatter_kernel, line_size), out_shape=ou...  382 us
    pallas_call x1, Pallas kernels, gather_call(): pl.pallas_call(functools.partial(gather_kernel, hd ** (-0.5)), out_shape=...  178 us
    unnamed x29, local copies, waits for them, and re-layouts  17.1 us

profile of v2, /device:TPU:0, one launch (start us, length us, event | category | flops | bytes accessed | tf_op | source)
XLA Modules:
  0.0 599.6 jit_solution(945337635515770149)
XLA Ops:
  0.6 0.0 copy-start
  0.7 0.6 copy-done
  1.3 0.7 compare_select_fusion
  2.0 0.1 pad.19.clone
  2.1 0.6 gather_fusion
  2.7 0.7 convert_element_type.29
  3.4 0.7 reshape.126
  4.1 0.1 rev.50
  4.3 0.7 reshape.128
  5.0 0.7 reshape.130
  5.7 0.1 rev.56
  5.9 0.1 rev.53
  6.0 0.7 reshape.132
  6.7 0.7 convert_add_fusion
  7.5 0.1 rev.62
  7.6 0.1 rev.59
  7.8 0.7 stack.28
  8.5 0.1 iota_add_fusion
  8.6 0.6 copy.34
  9.2 0.7 stack.26.vecs
  9.9 0.6 select_maximum_fusion.vecs
  10.5 0.2 broadcast_multiply_fusion
  10.7 2.2 fusion
  13.0 0.8 concatenate.13.cosine
  13.8 0.0 copy-start.6
  13.8 0.2 fusion.3
  14.0 1.3 maximum_maximum_fusion.1
  15.4 1.3 copy.33
  16.7 0.0 copy-done.6
  16.7 1.4 copy.31
  18.1 177.7 %shard_map.263 = (bf16[2048,2048]{1,0:T(8,128)(2,1)}, bf16[2048,2048]{1,0:T(8,128)(2,1)}, bf16[512,2048]{1,0:T(8,128)(2,1)}, bf16[512,2048]{1,0:T(8,128)(2,1)}, ...) custom-call(bf16[512,2048]{1,0:T(8,128)(2,1)} %bitcast.30, ...), custom_call_target="tpu_custom_call" | custom-call | tf_op jit(solution)/shard_map/pallas_call | solution.py:560
  195.8 381.6 %shard_map.264 = (bf16[512,2048]{1,0:T(8,128)(2,1)}, f32[512,2048]{1,0:T(8,128)}, f32[512,1536]{1,0:T(8,128)}, f32[512,512]{1,0:T(8,128)}, f32[512,2048]{1,0:T(8...) custom-call(bf16[2048,2048]{1,0:T(8,128)(2,1)} %get-tuple-element.33.we_hbm, ...), custom_call_target="tpu_custom_call" | custom-call | tf_op jit(solution)/shard_map/pallas_call | solution.py:964
  577.4 0.8 slice_reduce_fusion
  578.2 1.9 fusion.4
  580.1 0.0 copy-start.8
  580.2 0.6 reshape_squeeze.3
  580.8 0.0 copy-start.5
  580.8 5.3 reshape.123
  586.1 0.0 copy-done.8
  586.1 0.0 copy-start.4
  586.1 0.6 copy.42
  586.7 0.0 copy-done.5
  586.7 1.3 copy.43
  588.0 1.0 copy-done.4
  589.0 0.0 copy-start.7
  589.0 0.0 copy-start.3
  589.0 2.1 copy.44
  591.2 0.0 copy-done.7
  591.2 1.0 copy.45
  592.1 1.3 copy-done.3
  593.4 0.0 copy-start.2
  593.4 0.0 copy-start.1
  593.4 2.1 copy.46
  595.6 1.6 copy-done.2
  597.1 2.0 copy.47
  599.1 0.0 copy-done.1
  (29 shorter events, 0.3 us)
Async XLA Ops:
  0.6 0.7 copy-start
  13.8 2.9 copy-start.6
  580.1 5.9 copy-start.8
  580.8 5.9 copy-start.5
  586.1 3.0 copy-start.4
  589.0 2.1 copy-start.7
  589.0 4.4 copy-start.3
  593.4 3.7 copy-start.2
  593.4 5.7 copy-start.1

commit v3 on v0

--- a/solution.py
+++ b/solution.py
@@ -1,6 +1,11 @@
+import functools
+import math
+
 import jax
 import jax.numpy as jnp
 from jax import lax
+from jax.experimental import pallas as pl
+from jax.experimental.pallas import tpu as pltpu
 from jax.sharding import PartitionSpec as P
 
 ROT = 64
@@ -51,7 +56,1087 @@
     return exponent / jnp.sum(exponent, -1, keepdims=True)
 
 
-def local(
+LOW = jnp.bfloat16
+FULL = jnp.float32
+
+
+MESH = pl.DeviceIdType.MESH
+ANY = pl.BlockSpec(memory_space=pl.ANY)
+IN_VMEM = pl.BlockSpec(memory_space=pltpu.VMEM)
+VMEM_BYTES = 63 * 2**20
+COPIES = 224
+
+
+class Sent:
+    def __init__(self, links, k, source, target, peer):
+        self.links, self.k, self.source, self.target, self.peer = links, k, source, target, peer
+
+    def copy(self):
+        return self.links.copy_at(self.k, self.source, self.target, self.peer)
+
+    def start(self):
+        self.copy().start()
+
+    def wait_recv(self):
+        self.copy().wait_recv()
+
+    def wait_send(self):
+        self.copy().wait_send()
+
+
+class Links:
+    def __init__(self, send_sem, recv_sem, line=0):
+        self.send_sem, self.recv_sem, self.sent, self.count = send_sem, recv_sem, [], 0
+        self.r, self.f, self.t = (lax.axis_index(name) for name in ("replica", "fsdp", "tensor"))
+        self.xb, self.yb = lax.rem(self.f, 2), lax.div(self.f, 2)
+        self.x = (self.r, self.f + 1 - 2 * self.xb, self.t)
+        self.y = (self.r, lax.rem(self.f + 2, 4), self.t)
+        self.core = (1 - self.r, self.f, self.t)
+        self.peers = [self.x, self.y, self.core]
+        if line:
+            self.line = line
+            self.left, self.right, self.across = (
+                (self.r, self.f, lax.rem(self.t + step, line)) for step in (line - 1, 1, 2)
+            )
+            self.pair = (self.r, self.f, self.t + 1 - 2 * lax.rem(self.t, 2))
+            self.far = (self.r, 3 - self.f, self.t)
+            self.mirror = (self.r, self.f, line - 1 - self.t)
+            self.peers += [self.far, self.left, self.right, self.across]
+
+    def meet(self):
+        barrier = pltpu.get_barrier_semaphore()
+        for peer in self.peers:
+            pl.semaphore_signal(barrier, inc=1, device_id=peer, device_id_type=MESH)
+        pl.semaphore_wait(barrier, len(self.peers))
+
+    def prepare(self, source, target, peer):
+        self.count += 1
+        return Sent(self, self.count - 1, source, target, peer)
+
+    def send(self, source, target, peer):
+        copy = self.prepare(source, target, peer)
+        copy.start()
+        self.sent.append(copy)
+        return copy
+
+    def series(self, count):
+        k = self.count
+        self.count += count
+        return k
+
+    def copy_at(self, k, source, target, peer):
+        return pltpu.make_async_remote_copy(
+            src_ref=source,
+            dst_ref=target,
+            send_sem=self.send_sem.at[k],
+            recv_sem=self.recv_sem.at[k],
+            device_id=peer,
+            device_id_type=MESH,
+        )
+
+    def sent_out(self, copy):
+        copy.wait_send()
+        self.sent = [other for other in self.sent if other is not copy]
+
+    def end(self):
+        for copy in self.sent:
+            copy.wait_send()
+
+    def block(self, i):
+        place = 0
+        for size, bit in ((4, self.yb), (2, self.xb), (1, self.r)):
+            mine = lax.rem(lax.div(i, size), 2) if isinstance(i, jax.Array) else i // size % 2
+            place = place + size * (mine + bit - 2 * mine * bit)
+        return place
+
+
+class Local:
+    def __init__(self, sem):
+        self.sem, self.count, self.open = sem, 0, []
+
+    def start(self, source, target):
+        copy = pltpu.make_async_copy(source, target, self.sem.at[self.count])
+        self.count += 1
+        copy.start()
+        self.open.append(copy)
+        return copy
+
+    def wait(self, *copies):
+        for copy in copies:
+            copy.wait()
+            self.open = [other for other in self.open if other is not copy]
+
+    def end(self):
+        self.wait(*list(self.open))
+
+
+def at_rows(ref, start, size):
+    return ref.at[pl.ds(start, size), :]
+
+
+def at_columns(ref, start, size):
+    return ref.at[:, pl.ds(start, size)]
+
+
+class Gathered:
+    def __init__(self, links, local, shard, full, cut, unit, copied=True):
+        self.links, self.local, self.full, self.cut = links, local, full, cut
+        self.shard, self.unit, self.half = shard, unit, unit // 2
+        self.starts = [pl.multiple_of(links.r * unit + start, self.half) for start in (0, self.half)]
+        self.bases = [pl.multiple_of(base * unit, unit) for base in (links.r, 1 - links.r)]
+        self.copies = [local.start(self.here(i), self.at(i)) for i in range(2)] if copied else []
+        self.from_x, self.from_y = {}, {}
+
+    def here(self, i):
+        return self.cut(self.shard, self.bases[i], self.unit)
+
+    def mine(self, lower):
+        return self.cut(self.shard, self.starts[lower], self.half)
+
+    def at(self, block, start=0, size=None):
+        return self.cut(self.full, block * self.unit + start, self.unit if size is None else size)
+
+    def to_x(self, lower):
+        source, target = self.mine(lower), self.at(2, self.half * lower, self.half)
+        self.from_x[lower] = self.links.send(source, target, self.links.x)
+
+    def to_y(self, lower):
+        source, target = self.mine(lower), self.at(4, self.half * lower, self.half)
+        self.from_y[lower] = self.links.send(source, target, self.links.y)
+
+    def first(self):
+        self.to_x(False)
+        self.to_y(True)
+
+    def rest(self):
+        self.to_x(True)
+        self.to_y(False)
+
+    def pass_y(self):
+        half = self.half
+        self.from_x[False].wait_recv()
+        self.far_top = self.links.send(self.at(2, 0, half), self.at(6, 0, half), self.links.y)
+
+    def pass_x(self):
+        half = self.half
+        self.from_y[True].wait_recv()
+        self.far_end = self.links.send(self.at(4, half, half), self.at(6, half, half), self.links.x)
+
+    def relay(self):
+        self.pass_y()
+        self.pass_x()
+
+    def share(self):
+        self.from_y[False].wait_recv()
+        self.core_y = self.links.send(self.at(4), self.at(5), self.links.core)
+        self.from_x[True].wait_recv()
+        self.core_x = self.links.send(self.at(2), self.at(3), self.links.core)
+
+    def share_far(self):
+        self.far_top.wait_recv()
+        self.far_end.wait_recv()
+        self.core_far = self.links.send(self.at(6), self.at(7), self.links.core)
+
+    def passed(self):
+        for copy in (self.far_top, self.far_end, self.core_x, self.core_y, self.core_far):
+            self.links.sent_out(copy)
+
+    def whole(self):
+        self.local.wait(*self.copies)
+        for copy in (self.core_x, self.core_y, self.core_far):
+            copy.wait_recv()
+
+
+def odd(j):
+    return j % 2 if isinstance(j, int) else lax.rem(j, 2)
+
+
+def tile_of(j, size):
+    return pl.ds(pl.multiple_of(j * size, size), size)
+
+
+def dot(left, right):
+    return jnp.dot(left, right, preferred_element_type=FULL)
+
+
+def spin(values_in, cosine, sine):
+    head = values_in[:, :128]
+    lane = lax.broadcasted_iota(jnp.int32, head.shape, 1)
+    swapped = jnp.where(lane < ROT // 2, pltpu.roll(head, 96, 1), pltpu.roll(head, 32, 1))
+    return jnp.concatenate([head * cosine + swapped * sine, values_in[:, 128:]], -1)
+
+
+class Scattered:
+    def __init__(self, links, local, blocks, cut, unit, via, got, stage=None, own=None):
+        self.links, self.local, self.blocks, self.cut, self.unit = links, local, blocks, cut, unit
+        self.via, self.got = [via.at[n] for n in range(2)], [got.at[n] for n in range(2)]
+        self.stage, self.own = stage, own
+        self.half, self.loads = unit // 2, []
+
+    def load(self):
+        self.loads = [
+            self.local.start(self.cut(self.blocks[1], self.half, self.half), self.stage[0]),
+            self.local.start(self.cut(self.blocks[2], 0, self.half), self.stage[1]),
+            self.local.start(self.blocks[0], self.own),
+        ]
+
+    def first(self):
+        half, cut, far = self.half, self.cut, self.blocks[3]
+        self.via_x = self.links.send(cut(far, 0, half), self.via[0], self.links.x)
+        self.via_y = self.links.send(cut(far, half, half), self.via[1], self.links.y)
+
+    def direct(self):
+        half, cut = self.half, self.cut
+        self.x_top = self.links.send(cut(self.blocks[1], 0, half), cut(self.got[0], 0, half), self.links.x)
+        self.y_end = self.links.send(cut(self.blocks[2], half, half), cut(self.got[1], half, half), self.links.y)
+
+    def second(self):
+        half, cut = self.half, self.cut
+        self.local.wait(*self.loads[:2])
+        self.via_x.wait_recv()
+        add_rows(self.stage[1], self.stage[1], self.via[0])
+        self.y_top = self.links.send(self.stage[1], cut(self.got[1], 0, half), self.links.y)
+        self.via_y.wait_recv()
+        add_rows(self.stage[0], self.stage[0], self.via[1])
+        self.x_end = self.links.send(self.stage[0], cut(self.got[0], half, half), self.links.x)
+
+    def third(self, slots, place, step, between=lambda: None):
+        for copy in (self.x_top, self.x_end, self.y_top, self.y_end):
+            copy.wait_recv()
+        if self.loads:
+            self.local.wait(self.loads[2])
+        self.other = []
+        for start in range(0, self.own.shape[0], step):
+            between()
+            rows = pl.ds(start, step)
+            at, total = slots.take()
+            add_rows(total, self.own.at[rows, :], self.got[0].at[rows, :], self.got[1].at[rows, :])
+            kept = self.local.start(total, place.at[rows, :])
+            other = self.links.send(total, place.at[rows, :], self.links.core)
+            self.other.append(other)
+
+            def done(kept=kept, other=other):
+                self.local.wait(kept)
+                self.links.sent_out(other)
+
+            slots.busy[at] = done
+
+
+def add_rows(target, *parts):
+    rows, wide = target.shape
+    step = min(rows, 32 if wide > 512 else 256)
+
+    def one(c, carry):
+        at = pl.ds(pl.multiple_of(c * step, step), step)
+        total = parts[0][at, :].astype(FULL)
+        for part in parts[1:]:
+            total = total + part[at, :].astype(FULL)
+        target[at, :] = total.astype(target.dtype)
+        return carry
+
+    lax.fori_loop(0, rows // step, one, 0)
+
+
+class Line:
+    def __init__(self, links, part, got, final, chunks, cut, finish):
+        self.links, self.part, self.got, self.final, self.cut, self.finish = links, part, got, final, cut, finish
+        self.chunks = chunks
+        self.outer = jnp.logical_or(links.t == 0, links.t == links.line - 1)
+        self.middle = jnp.logical_not(self.outer)
+        self.inward = [self.make(c, part, final, links.pair) for c in range(chunks)]
+        self.across = [self.make(c, part, got, links.mirror) for c in range(chunks)]
+        self.outward = [self.make(c, final, final, links.pair) for c in range(chunks)]
+
+    def make(self, c, source, target, peer):
+        return self.links.prepare(self.cut(source, c), self.cut(target, c), peer)
+
+    def start(self, *chunks):
+        @pl.when(self.outer)
+        def _():
+            for c in chunks:
+                self.inward[c].start()
+
+    def first(self, c):
+        @pl.when(self.middle)
+        def _():
+            self.inward[c].wait_recv()
+            part = self.cut(self.part, c)
+            add_rows(part, part, self.cut(self.final, c))
+            self.across[c].start()
+
+    def second(self, c):
+        @pl.when(self.middle)
+        def _():
+            self.across[c].wait_recv()
+            self.finish(c)
+            self.outward[c].start()
+
+    def third(self, c):
+        @pl.when(self.outer)
+        def _():
+            self.outward[c].wait_recv()
+
+    def end(self):
+        @pl.when(self.outer)
+        def _():
+            for copy in self.inward:
+                copy.wait_send()
+
+        @pl.when(self.middle)
+        def _():
+            for copy in self.across + self.outward:
+                copy.wait_send()
+
+
+class Slots:
+    def __init__(self, *refs):
+        self.refs, self.busy, self.count = refs, {}, 0
+
+    def take(self):
+        at = self.count % len(self.refs)
+        self.count += 1
+        if at in self.busy:
+            self.busy.pop(at)()
+        return at, self.refs[at]
+
+    def end(self):
+        for wait in self.busy.values():
+            wait()
+        self.busy = {}
+
+
+def block_kernel(
+    score_scale, line_size,
+    x_hbm, g_hbm, wh_hbm, wo_hbm, we_own, ws_own, raw, order,
+    layer_out, input_grad, heads_grad, output_grad, expand_grad, shrink_grad, we, ws, n2t_hbm, got_core_s, got_core_o,
+    got_core_h, got_core_e, red_s, red_o, red_h, sums_out,
+    x, g, up, n1, nt, stat, wh, wo, qkv, dctx, ctxt, pg, kvg_got, got_branch, final_branch, got_up, final_up,
+    via_h, got_h, via_o, got_o, via_s, got_s, via_e, got_e, vecs, sums, sums_got, gains, gains_got,
+    loop_sem, block_sem, local_sem, send_sem, recv_sem,
+):
+    links, local = Links(send_sem, recv_sem, line_size), Local(local_sem)
+    tokens, width = x.shape
+    units, heads_wide, out_wide = we.shape[1], wh.shape[1], wo.shape[0]
+    hd = dctx.shape[1]
+    unit = width // 8
+    blocks = range(8)
+    room_s = qkv
+    place = [pl.ds(pl.multiple_of(links.block(i) * unit, unit), unit) for i in blocks]
+
+    def here(i):
+        return pl.ds(i * unit, unit)
+
+    rest_rows = pl.ds(2 * unit, width - 2 * unit)
+
+    def tile(j):
+        return pl.ds(j * unit if isinstance(j, int) else pl.multiple_of(j * unit, unit), unit)
+
+    def placed(i):
+        return pl.ds(pl.multiple_of(links.block(i) * unit, unit), unit)
+
+    def stream(start, end, load, body):
+        def copies(j):
+            pairs = load(j, odd(j))
+            return [pltpu.make_async_copy(*pair, loop_sem.at[n, odd(j)]) for n, pair in enumerate(pairs)]
+
+        for copy in copies(start):
+            copy.start()
+
+        def one(j, carry):
+            @pl.when(j + 1 < end)
+            def _():
+                for copy in copies(j + 1):
+                    copy.start()
+
+            for copy in copies(j):
+                copy.wait()
+            body(j, odd(j))
+            return carry
+
+        lax.fori_loop(start, end, one, 0)
+
+    x_in, g_in = [], []
+    for i in blocks:
+        cols = pl.ds(pl.multiple_of(links.block(i) * unit, unit), unit)
+        x_in.append(local.start(x_hbm.at[:, cols], x.at[:, pl.ds(i * unit, unit)]))
+        g_in.append(local.start(g_hbm.at[:, cols], g.at[:, pl.ds(i * unit, unit)]))
+    links.meet()
+    heads_in = Gathered(links, local, wh_hbm, wh, at_rows, unit)
+    output_in = Gathered(links, local, wo_hbm, wo, at_columns, unit)
+    expand = Gathered(links, local, we_own, we, at_rows, unit)
+    weight = Gathered(links, local, ws_own, ws, at_columns, unit, False)
+    heads_in.first()
+    heads_in.rest()
+
+    turns = (3, 1, 2, 0)
+
+    def turn_of(n):
+        return jnp.where(n == 0, 3, jnp.where(n == 3, 0, n))
+
+    class Reduced:
+        def __init__(self, room, got, block):
+            self.room, self.got, self.block = room, got, block
+            self.gots = [got.at[k] for k in range(4)]
+
+        def to_core(self):
+            first = links.series(4)
+
+            def one(n, carry):
+                k = turn_of(n)
+                self.block(2 * k + 1, self.room(n), False)
+                links.copy_at(first + n, self.room(n), self.got.at[k], links.core).start()
+                return carry
+
+            lax.fori_loop(0, 4, one, 0)
+            self.copies = [Sent(links, first + n, self.room(n), self.gots[turns[n]], links.core) for n in range(4)]
+
+        def fetch(self):
+            for n in range(4):
+                self.copies[n].wait_send()
+                self.copies[n].wait_recv()
+                pltpu.make_async_copy(self.got.at[turns[n]], self.room(n), block_sem.at[n]).start()
+
+        def add(self, red):
+            def one(n, carry):
+                k = turn_of(n)
+                pltpu.make_async_copy(self.got.at[k], self.room(n), block_sem.at[n]).wait()
+                self.block(2 * k, self.room(n), True)
+                if red is not None:
+                    pltpu.make_async_copy(self.room(n), red.at[k], block_sem.at[4 + n]).start()
+                return carry
+
+            lax.fori_loop(0, 4, one, 0)
+            if red is not None:
+                for n in range(4):
+                    pltpu.make_async_copy(self.room(n), red.at[turns[n]], block_sem.at[4 + n]).wait()
+
+    def product(left, right, ref, add):
+        part = dot(left, right)
+        if add:
+            part = part + ref[...].astype(FULL)
+        ref[...] = part.astype(LOW)
+
+    def heads_block(i, ref, add):
+        product(nt[tile(i), :], pg[...], ref, add)
+
+    heads_sum = Reduced(lambda n: wh.at[tile(n), :], got_core_h, heads_block)
+    own_h = at_rows(wh, 4 * unit, unit)
+    stage_h = (at_rows(wh, 5 * unit, unit // 2), at_rows(wh, 5 * unit + unit // 2, unit // 2))
+    heads = Scattered(links, local, [red_h.at[k] for k in range(4)], at_rows, unit, via_h, got_h, stage_h, own_h)
+    shrink = Scattered(links, local, [red_s.at[k] for k in range(4)], at_columns, unit, via_s, got_s)
+    output = Scattered(links, local, [red_o.at[k] for k in range(4)], at_columns, unit, via_o, got_o)
+
+    def up_part(i, grad, first):
+        cols, spot = tile(i), placed(i)
+        normal = (x[:, cols].astype(FULL) - stat[:, 0:1]) * stat[:, 128:129]
+        row = 0 if first else 2
+        sums[0, row : row + 1, spot] = jnp.sum(grad * normal, 0, keepdims=True)
+        sums[0, row + 1 : row + 2, spot] = jnp.sum(grad, 0, keepdims=True)
+        scaled = grad * (vecs[0:1, cols] if first else vecs[2:3, cols])
+        n1[:, cols] = (scaled if first else n1[:, cols].astype(FULL) + scaled).astype(LOW)
+
+    def attend(qkv_away, dctx_away, ctxt_all, pgq, pg_away, kvg_away, cosine, sines, dk, dv, stage):
+        for i in blocks:
+            cols = pl.ds(pl.multiple_of(links.block(i) * unit, unit), unit)
+            vecs[0:4, i * unit : (i + 1) * unit] = raw[0:4, cols]
+            vecs[4:5, i * unit : (i + 1) * unit] = raw[6:7, cols] + raw[7:8, cols]
+        local.wait(*x_in)
+
+        def norm_rows(c, carry):
+            rows = tile_of(c, 64)
+            value = x[rows, :].astype(FULL)
+            average = jnp.mean(value, -1, keepdims=True)
+            centred = value - average
+            inverse = lax.rsqrt(jnp.mean(centred * centred, -1, keepdims=True) + NORM_EPS)
+            normal = centred * inverse
+            both = [jnp.broadcast_to(part, (64, 128)) for part in (average, inverse)]
+            stat[rows, :] = jnp.concatenate(both, -1)
+            n1[rows, :] = (normal * vecs[0:1, :] + vecs[1:2, :]).astype(LOW)
+            up[rows, :] = (normal * vecs[2:3, :] + vecs[3:4, :]).astype(LOW)
+            return carry
+
+        lax.fori_loop(0, tokens // 64, norm_rows, 0)
+        bases = [
+            order[0, (links.yb if step < 2 else 1 - links.yb) * 2 + (links.xb if step % 2 == 0 else 1 - links.xb)]
+            * tokens
+            for step in (0, 2, 1, 3)
+        ]
+
+        def table_rows(c, carry):
+            rows = tile_of(c, 64)
+            lane = lax.broadcasted_iota(jnp.int32, (64, 128), 1)
+            row = lax.broadcasted_iota(jnp.int32, (64, 128), 0) + c * 64
+            spot = row + jnp.where(row < tokens, bases[0], bases[1] - tokens)
+            pace = jnp.exp(lax.rem(lane, ROT // 2).astype(FULL) * (-2.0 / ROT * math.log(10000.0)))
+            angle = spot.astype(FULL) * pace
+            sine = jnp.sin(angle)
+            cosine[rows, :] = jnp.where(lane < ROT, jnp.cos(angle), 1.0)
+            sines[rows, :] = jnp.where(lane < ROT // 2, -sine, jnp.where(lane < ROT, sine, 0.0))
+            return carry
+
+        lax.fori_loop(0, 2 * tokens // 64, table_rows, 0)
+        heads_in.relay()
+        output_in.first()
+        output_in.rest()
+
+        def turned_copy(j):
+            slot = odd(j)
+            return pltpu.make_async_copy(stage.at[slot], n2t_hbm.at[tile_of(j, unit), :], loop_sem.at[0, slot])
+
+        def turn_tiles(j, carry):
+            cols = tile_of(j, unit)
+            nt[cols, :] = n1[:, cols].T
+
+            @pl.when(j >= 2)
+            def _():
+                turned_copy(j - 2).wait()
+
+            stage[odd(j), :, :] = up[:, cols].T
+            turned_copy(j).start()
+            return carry
+
+        lax.fori_loop(0, 8, turn_tiles, 0)
+        for j in (6, 7):
+            turned_copy(j).wait()
+        sums[0, :, :] = jnp.zeros(sums.shape[1:], FULL)
+        local.wait(*g_in)
+        for i in blocks:
+            cols = pl.ds(pl.multiple_of(links.block(i) * unit, unit), unit)
+            sums[0, 4:5, cols] = jnp.sum(g[:, i * unit : (i + 1) * unit].astype(FULL), 0, keepdims=True)
+        heads_in.share()
+        heads_in.share_far()
+        heads_in.whole()
+        output_in.relay()
+
+        own, away = links.yb * 3 * hd, (1 - links.yb) * 3 * hd
+
+        def project(c, start, target):
+            cols = pl.ds(pl.multiple_of(start + c * hd, hd), hd)
+            value = dot(n1[...], wh[:, cols]) + raw[5:6, cols]
+            if c < 2:
+                value = spin(value, cosine[:tokens, :], sines[:tokens, :])
+            target[c, :tokens, :] = value.astype(LOW)
+
+        def place_of(c, part):
+            return qkv.at[c, pl.ds(part * tokens, tokens), :]
+
+        from_y, from_x, from_far = {}, {}, {}
+        for c in (1, 2, 0):
+            project(c, away, qkv_away)
+            from_y[c] = links.send(qkv_away.at[c], place_of(c, 1), links.y)
+        for c in (1, 2):
+            project(c, own, qkv)
+            from_x[c] = links.send(place_of(c, 0), place_of(c, 2), links.x)
+        from_y[1].wait_recv()
+        from_far[1] = links.send(place_of(1, 1), place_of(1, 3), links.x)
+        project(0, own, qkv)
+        output_in.share()
+        output_in.share_far()
+        from_y[2].wait_recv()
+        from_far[2] = links.send(place_of(2, 1), place_of(2, 3), links.x)
+        output_in.whole()
+        rows_own = pl.ds(pl.multiple_of(links.yb * hd, hd), hd)
+        rows_away = pl.ds(pl.multiple_of((1 - links.yb) * hd, hd), hd)
+        dctx_away[...] = contract_last(g[...], wo[rows_away, :]).astype(LOW)
+        dctx_from_y = links.send(dctx_away, dctx.at[pl.ds(tokens, tokens), :], links.y)
+        dctx[:tokens, :] = contract_last(g[...], wo[rows_own, :]).astype(LOW)
+        expand.first()
+        expand.to_y(False)
+        for copy in (from_y[0], dctx_from_y, *from_x.values(), *from_far.values()):
+            copy.wait_recv()
+
+        def attention(kt, vt, prob, wgt, prob_low, grad_low):
+            keys = qkv.shape[1]
+            step = tokens
+            lag = lax.broadcasted_iota(jnp.int32, (step, hd), 0) - lax.broadcasted_iota(jnp.int32, (step, hd), 1)
+            parts = [pl.ds(i * step, step) for i in range(keys // step)]
+            for part in parts:
+                kt[:, part] = qkv[1, part, :].T
+                vt[:, part] = qkv[2, part, :].T
+            dk[...] = jnp.zeros_like(dk)
+            dv[...] = jnp.zeros_like(dv)
+
+            def one(b, carry):
+                rows = tile_of(b, hd)
+                query, grad = qkv[0, rows, :], dctx[rows, :]
+                ahead = jnp.where(b < tokens // hd, bases[0], bases[1] - tokens) + b * hd
+                top = jnp.full((1, hd), MASKED, FULL)
+                for i, part in enumerate(parts):
+                    scores = contract_last(qkv[1, part, :], query) * score_scale
+                    scores = jnp.where(lag <= ahead - bases[i], scores, MASKED)
+                    prob[part, :] = scores
+                    top = jnp.maximum(top, jnp.max(scores, 0, keepdims=True))
+                total = jnp.zeros((1, hd), FULL)
+                for part in parts:
+                    exponent = jnp.exp(prob[part, :] - top)
+                    prob[part, :] = exponent
+                    total = total + jnp.sum(exponent, 0, keepdims=True)
+                share = 1.0 / total
+                inner = jnp.zeros((1, hd), FULL)
+                for part in parts:
+                    weight = contract_last(qkv[2, part, :], grad)
+                    chance = prob[part, :] * share
+                    prob[part, :] = chance
+                    prob_low[part, :] = chance.astype(LOW)
+                    wgt[part, :] = weight
+                    inner = inner + jnp.sum(chance * weight, 0, keepdims=True)
+                for part in parts:
+                    grad_low[part, :] = (prob[part, :] * (wgt[part, :] - inner)).astype(LOW)
+                ctxt_all[:, rows] = dot(vt[...], prob_low[...]).astype(LOW)
+                query_grad = dot(kt[...], grad_low[...]) * score_scale
+                for part in parts:
+                    dv[part, :] += dot(prob_low[part, :], grad)
+                    dk[part, :] += dot(grad_low[part, :], query)
+                turned_grad = spin(query_grad.T, cosine[rows, :], -sines[rows, :])
+                pgq[rows, :] = turned_grad.astype(LOW)
+                return carry
+
+            lax.fori_loop(0, 2 * tokens // hd, one, 0)
+            ctxt[rows_own, :] = ctxt_all[:, :tokens]
+            pg[:, pl.ds(pl.multiple_of(own, hd), hd)] = pgq[:tokens, :]
+            for i, total in enumerate((dk, dv)):
+                kvg_away[i, :, :] = total[2 * tokens :, :].astype(LOW)
+
+        keys = qkv.shape[1]
+        pl.run_scoped(
+            attention,
+            pltpu.VMEM((hd, keys), LOW),
+            pltpu.VMEM((hd, keys), LOW),
+            pltpu.VMEM((keys, hd), FULL),
+            pltpu.VMEM((keys, hd), FULL),
+            pltpu.VMEM((keys, hd), LOW),
+            pltpu.VMEM((keys, hd), LOW),
+        )
+
+        def head_columns(ref, start, i):
+            return ref.at[:, pl.ds(pl.multiple_of(start + i * hd, hd), hd)]
+
+        def send_grad(i):
+            source = pgq.at[pl.ds(tokens, tokens), :] if i == 0 else head_columns(pg_away, 0, i - 1)
+            return links.send(source, head_columns(pg, own, i), links.y)
+
+        kvg_from_x = {i: links.send(kvg_away.at[i], kvg_got.at[i], links.x) for i in (1, 0)}
+        pg_from_y = [send_grad(0)]
+        ctx_from_y = links.send(ctxt_all.at[:, pl.ds(tokens, tokens)], ctxt.at[rows_own, :], links.y)
+        expand.pass_x()
+        expand.to_x(True)
+
+        for i in (1, 0):
+            kvg_from_x[i].wait_recv()
+            for away_rows, target in ((True, pg_away), (False, pg)):
+                rows = pl.ds(tokens if away_rows else 0, tokens)
+                total = (dk, dv)[i][rows, :] + kvg_got[i, rows, :].astype(FULL)
+                if i == 0:
+                    total = spin(total * score_scale, cosine[rows, :], -sines[rows, :])
+                head_columns(target, 0 if away_rows else own, i if away_rows else 1 + i)[...] = total.astype(LOW)
+                if away_rows:
+                    pg_from_y.append(send_grad(1 + i))
+        expand.pass_y()
+        weight.first()
+        weight.rest()
+        ctx_from_y.wait_recv()
+        for copy in pg_from_y:
+            copy.wait_recv()
+
+        def first_block(i, carry):
+            up_part(i, contract_last(pg[...], wh[tile(i), :]), True)
+            return carry
+
+        lax.fori_loop(0, 8, first_block, 0)
+        sums[0, 6:7, :heads_wide] = jnp.sum(pg[...].astype(FULL), 0, keepdims=True)
+        heads_in.passed()
+        heads_sum.to_core()
+        expand.share()
+        expand.share_far()
+        expand.whole()
+        for copy in (*from_y.values(), *from_x.values(), *from_far.values(), dctx_from_y, *kvg_from_x.values(), *pg_from_y, ctx_from_y):
+            links.sent_out(copy)
+
+    low, full = (functools.partial(lambda kind, *shape: pltpu.VMEM(shape, kind), kind) for kind in (LOW, FULL))
+    pl.run_scoped(
+        attend,
+        low(3, tokens, hd),
+        low(tokens, hd),
+        low(hd, 2 * tokens),
+        low(2 * tokens, hd),
+        low(tokens, 2 * hd),
+        low(2, 2 * tokens, hd),
+        full(2 * tokens, 128),
+        full(2 * tokens, 128),
+        full(4 * tokens, hd),
+        full(4 * tokens, hd),
+        low(2, unit, tokens),
+    )
+
+    def update(act, actt, slope, ctx, room_o, stage_o, own_o, room_e, total_rows, total_columns, grad_rows):
+        def forward(j, slot):
+            cols = tile(j)
+            value = dot(up[...], room_s[slot]) + raw[4:5, cols]
+            normal_share = 0.5 * (1.0 + lax.erf(value * (0.5**0.5)))
+            low_act = (value * normal_share).astype(LOW)
+            act[:, cols] = low_act
+            actt[cols, :] = low_act.T
+            density = jnp.exp(value * value * -0.5) * 0.3989422804014327
+            slope[:, cols] = (normal_share + value * density).astype(LOW)
+
+        stream(0, 8, lambda j, slot: [(we.at[:, tile(j)], room_s.at[slot])], forward)
+        weight.relay()
+        ctx[...] = ctxt[...].T
+
+        rows_out = grad_rows.shape[1]
+
+        def columns_cut(ref, c):
+            return ref.at[:, here(c)]
+
+        def rows_cut(ref, c):
+            return ref.at[pl.ds(c * rows_out, rows_out), :]
+
+        def finish_branch(c):
+            cols = here(c)
+
+            def one(part, carry):
+                at = tile_of(part, 128)
+                total = up[at, cols].astype(FULL) + got_branch[at, cols].astype(FULL)
+                final_branch[at, cols] = (x[at, cols].astype(FULL) + total + vecs[4:5, cols]).astype(LOW)
+                return carry
+
+            lax.fori_loop(0, tokens // 128, one, 0)
+
+        def finish_up(c):
+            add_rows(rows_cut(final_up, c), rows_cut(n1, c), rows_cut(got_up, c))
+
+        line_branch = Line(links, up, got_branch, final_branch, 8, columns_cut, finish_branch)
+        line_up = Line(links, n1, got_up, final_up, tokens // rows_out, rows_cut, finish_up)
+
+        def branch_blocks(chunks, block, source):
+            def one(n, slot):
+                cols = tile(block(n))
+                up[:, cols] = (dot(ctx[...], wo[:, cols]) + dot(act[...], room_s[slot])).astype(LOW)
+                for at, chunk in enumerate(chunks):
+                    pl.when(n == at)(functools.partial(line_branch.start, chunk))
+
+            stream(0, len(chunks), lambda n, slot: [(source(n), room_s.at[slot])], one)
+
+        steps = [(line_branch, c) for c in (0, 1, 2, 4, 3, 5, 6, 7)] + [(line_up, c) for c in range(line_up.chunks)]
+        out_copies = []
+
+        def input_rows(c):
+            slot = len(out_copies) % 2
+            if len(out_copies) >= 2:
+                local.wait(*out_copies[-2])
+            rows = pl.ds(c * rows_out, rows_out)
+            value = x[rows, :].astype(FULL)
+            centred = value - jnp.mean(value, -1, keepdims=True)
+            scale = lax.rsqrt(jnp.mean(centred * centred, -1, keepdims=True) + NORM_EPS)
+            normal = centred * scale
+            upstream = final_up[rows, :].astype(FULL)
+            inner = upstream - jnp.mean(upstream, -1, keepdims=True)
+            inner = inner - normal * jnp.mean(upstream * normal, -1, keepdims=True)
+            grad_rows[slot, :, :] = g[rows, :].astype(FULL) + inner * scale
+            out_copies.append(
+                [local.start(grad_rows.at[slot, :, here(i)], input_grad.at[rows, place[i]]) for i in blocks]
+            )
+
+        def serve(count):
+            for _ in range(count):
+                at = serve.done
+                if at < len(steps):
+                    steps[at][0].first(steps[at][1])
+                if 2 <= at < len(steps) + 2:
+                    steps[at - 2][0].second(steps[at - 2][1])
+                if at >= 4:
+                    line, c = steps[at - 4]
+                    line.third(c)
+                    if line is line_up:
+                        input_rows(c)
+                    else:
+                        local.start(final_branch.at[:, here(c)], layer_out.at[:, place[c]])
+                serve.done += 1
+
+        serve.done = 0
+        branch_blocks((0, 1), lambda n: n, lambda n: at_columns(ws_own, pl.multiple_of((links.r + n - 2 * links.r * n) * unit, unit), unit))
+
+        def shrink_block(i, ref, add):
+            product(actt[...], g[:, tile(i)], ref, add)
+
+        def output_block(i, ref, add):
+            product(ctxt[...], g[:, tile(i)], ref, add)
+
+        def expand_block(i, ref, add):
+            product(nt[tile(i), :], slope[...], ref, add)
+
+        shrink.stage = (actt.at[:, pl.ds(unit, unit // 2)], actt.at[:, pl.ds(unit + unit // 2, unit // 2)])
+        shrink.own = actt.at[:, pl.ds(0, unit)]
+        output.stage, output.own = (stage_o.at[0], stage_o.at[1]), own_o
+        shrink_sum = Reduced(lambda n: room_s.at[n], got_core_s, shrink_block)
+        output_sum = Reduced(lambda n: room_o.at[n], got_core_o, output_block)
+        expand_sum = Reduced(lambda n: room_e.at[n], got_core_e, expand_block)
+        heads_sum.fetch()
+        heads_sum.add(red_h)
+        heads.first()
+        heads.direct()
+        heads.load()
+        n2t_load = local.start(n2t_hbm, nt)
+        weight.share()
+        serve(1)
+        weight.core_y.wait_recv()
+        weight.core_x.wait_recv()
+        ahead = lambda n: 2 * n + 2 - 3 * (n // 2 if isinstance(n, int) else lax.div(n, 2))
+        branch_blocks((2, 4, 3, 5), ahead, lambda n: ws.at[:, tile(ahead(n))])
+        serve(1)
+        shrink_sum.to_core()
+        weight.share_far()
+        shrink_sum.fetch()
+        shrink_sum.add(red_s)
+        shrink.first()
+        shrink.direct()
+        shrink.load()
+        serve(1)
+        weight.core_far.wait_recv()
+        branch_blocks((6, 7), lambda n: n + 6, lambda n: ws.at[:, tile(n + 6)])
+        serve(1)
+
+        def hidden_tile(j, slot):
+            cols = tile(j)
+            grad = (contract_last(g[...], room_e[slot]) * slope[:, cols].astype(FULL)).astype(LOW)
+            slope[:, cols] = grad
+            sums[0, 5:6, cols] = jnp.sum(grad.astype(FULL), 0, keepdims=True)
+
+        def shrink_rows(j, slot):
+            rows = tile(j)
+            pairs = [(weight.here(i).at[rows, :], room_e.at[slot, :, here(i)]) for i in range(2)]
+            return pairs + [(ws.at[rows, rest_rows], room_e.at[slot, :, rest_rows])]
+
+        stream(0, 4, shrink_rows, hidden_tile)
+        serve(1)
+        stream(4, 8, shrink_rows, hidden_tile)
+        serve(1)
+
+        def second_block(i, slot):
+            up_part(i, contract_last(slope[...], room_e[slot]), False)
+
+        expand_rows = lambda i, slot: [(we.at[tile(i), :], room_e.at[slot])]
+        stream(0, 4, expand_rows, second_block)
+        serve(1)
+        stream(4, 8, expand_rows, second_block)
+        line_up.start(*range(line_up.chunks))
+        serve(1)
+
+        def share(s, peers):
+            return [links.send(sums.at[s], sums_got.at[4 * s + k], peer) for k, peer in enumerate(peers)]
+
+        def shared(s, copies):
+            for copy in copies:
+                copy.wait_recv()
+            total = sums[s, :, :] + sums_got[4 * s, :, :]
+            if len(copies) > 1:
+                total = total + (sums_got[4 * s + 1, :, :] + sums_got[4 * s + 2, :, :])
+            sums[s + 1, :, :] = total
+
+        def share_line(s, peer):
+            return links.send(gains.at[s], gains_got.at[s], peer)
+
+        def shared_line(s, copy):
+            copy.wait_recv()
+            gains[s + 1, :, :] = gains[s, :, :] + gains_got[s, :, :]
+
+        first_share = share(0, [links.core])
+        output_sum.to_core()
+        shared(0, first_share)
+        second_share = share(1, [links.x, links.y, links.far])
+        output_sum.fetch()
+        output_sum.add(red_o)
+        output.first()
+        output.direct()
+        output.load()
+
+        local.wait(n2t_load)
+        expand_sum.to_core()
+        serve(1)
+        shrink.second()
+        serve(1)
+        expand_sum.fetch()
+        serve(1)
+        expand_sum.add(None)
+        red = {k: room_e.at[turns.index(k)] for k in range(4)}
+        expand = Scattered(links, local, [red[k] for k in range(4)], at_rows, unit, via_e, got_e, None, red[0])
+        expand.first()
+        expand.direct()
+        serve(2)
+        half_rows = pl.ds(pl.multiple_of(links.r * unit, unit), unit)
+        column_slots = Slots(total_columns.at[0], total_columns.at[1])
+        serve(2)
+        shrink.third(column_slots, shrink_grad.at[:, half_rows], total_columns.shape[1])
+        serve(1)
+        shared(1, second_share)
+        for row in range(4):
+            for side in range(2):
+                at = 2 * row + side
+                gains[0, at : at + 1, :] = sums[2, row : row + 1, side * (width // 2) : (side + 1) * (width // 2)]
+        pair_share = share_line(0, links.pair)
+        serve(3)
+
+        expand.via_x.wait_recv()
+        top, end = red[2].at[pl.ds(0, unit // 2), :], red[1].at[pl.ds(unit // 2, unit // 2), :]
+        add_rows(top, top, via_e.at[0])
+        expand.y_top = links.send(top, got_e.at[1, pl.ds(0, unit // 2), :], links.y)
+        expand.via_y.wait_recv()
+        add_rows(end, end, via_e.at[1])
+        expand.x_end = links.send(end, got_e.at[0, pl.ds(unit // 2, unit // 2), :], links.x)
+        heads.second()
+        output.second()
+        serve(len(steps) - 1 - serve.done)
+        shared_line(0, pair_share)
+        across_share = share_line(1, links.across)
+        serve(2)
+        expand_slots = Slots(total_rows.at[0], total_rows.at[1])
+        expand.third(expand_slots, expand_grad.at[half_rows, :], total_rows.shape[1])
+        serve(len(steps) + 4 - serve.done)
+        expand_slots.end()
+        total_slots = Slots(*[total_rows.at[n, :, pl.ds(0, heads_wide)] for n in range(2)])
+        heads.third(total_slots, heads_grad.at[half_rows, :], total_rows.shape[1])
+        output.third(column_slots, output_grad.at[:, half_rows], total_columns.shape[1])
+        total_slots.end()
+        column_slots.end()
+        shared_line(1, across_share)
+        for row in range(4):
+            for side in range(2):
+                at = 2 * row + side
+                sums_out[row : row + 1, side * (width // 2) : (side + 1) * (width // 2)] = gains[2, at : at + 1, :]
+        sums_out[4:8, :] = sums[2, 4:8, :]
+        for copy in (*shrink.other, *output.other, *heads.other, *expand.other):
+            copy.wait_recv()
+        assert links.count <= COPIES
+        links.end()
+        line_branch.end()
+        line_up.end()
+        local.end()
+
+
+    pl.run_scoped(
+        update,
+        low(tokens, units),
+        low(units, tokens),
+        low(tokens, units),
+        low(tokens, out_wide),
+        low(4, out_wide, unit),
+        low(2, out_wide, unit // 2),
+        low(out_wide, unit),
+        low(4, unit, units),
+        full(2, unit // 4, units),
+        full(2, out_wide, unit),
+        full(2, 32, width),
+    )
+
+
+def block_call(line_size, x, g, heads_rows, output_rows, expand_weight, shrink_weight, raw, order):
+    tokens, width = x.shape
+    heads_wide, out_wide, units = heads_rows.shape[1], output_rows.shape[0], expand_weight.shape[1]
+    hd, unit, half = heads_wide // 6, width // 8, width // 16
+    low = lambda *shape: pltpu.VMEM(shape, LOW)
+    full = lambda *shape: pltpu.VMEM(shape, FULL)
+    work = lambda *shape: jax.ShapeDtypeStruct(shape, LOW)
+    outs = [
+        work(tokens, width),
+        jax.ShapeDtypeStruct((tokens, width), FULL),
+        jax.ShapeDtypeStruct((2 * unit, heads_wide), FULL),
+        jax.ShapeDtypeStruct((out_wide, 2 * unit), FULL),
+        jax.ShapeDtypeStruct((2 * unit, units), FULL),
+        jax.ShapeDtypeStruct((units, 2 * unit), FULL),
+        work(width, units),
+        work(units, width),
+        work(width, tokens),
+        work(4, units, unit),
+        work(4, out_wide, unit),
+        work(4, unit, heads_wide),
+        work(4, unit, units),
+        work(4, units, unit),
+        work(4, out_wide, unit),
+        work(4, unit, heads_wide),
+        jax.ShapeDtypeStruct((8, width), FULL),
+    ]
+    scratch = [
+        *[low(tokens, width)] * 4, low(width, tokens), full(tokens, 256),
+        low(width, heads_wide), low(out_wide, width), low(4, 4 * tokens, hd), low(2 * tokens, hd),
+        low(out_wide, tokens), low(tokens, heads_wide), low(2, 2 * tokens, hd),
+        *[low(tokens, width)] * 4,
+        low(2, half, heads_wide), low(2, unit, heads_wide),
+        low(2, out_wide, half), low(2, out_wide, unit),
+        low(2, units, half), low(2, units, unit),
+        low(2, half, units), low(2, unit, units),
+        full(8, width), full(3, 8, width), full(7, 8, width), full(3, 8, width // 2), full(2, 8, width // 2),
+        pltpu.SemaphoreType.DMA((3, 2)),
+        pltpu.SemaphoreType.DMA((8,)),
+        pltpu.SemaphoreType.DMA((320,)),
+        pltpu.SemaphoreType.DMA((COPIES,)),
+        pltpu.SemaphoreType.DMA((COPIES,)),
+    ]
+    return pl.pallas_call(
+        functools.partial(block_kernel, hd**-0.5, line_size),
+        out_shape=outs,
+        in_specs=[ANY] * 6 + [IN_VMEM, pl.BlockSpec(memory_space=pltpu.SMEM)],
+        out_specs=[ANY] * 16 + [IN_VMEM],
+        scratch_shapes=scratch,
+        compiler_params=pltpu.CompilerParams(
+            collective_id=0, has_side_effects=True, vmem_limit_bytes=VMEM_BYTES
+        ),
+    )(x, g, heads_rows, output_rows, expand_weight, shrink_weight, raw, order)
+
+
+def square_local(
+    layer_input,
+    block_order,
+    first_gain,
+    first_bias,
+    second_gain,
+    second_bias,
+    heads_weight,
+    heads_bias,
+    output_weight,
+    output_bias,
+    expand_weight,
+    expand_bias,
+    shrink_weight,
+    shrink_bias,
+    cotangent,
+):
+    width = layer_input.shape[2]
+    heads_rows = heads_weight.reshape(heads_weight.shape[0], -1)
+    output_rows = output_weight.reshape(-1, output_weight.shape[2])
+    wide = heads_rows.shape[1]
+    pieces = [first_gain, first_bias, second_gain, second_bias, expand_bias, heads_bias.reshape(-1)]
+    pieces += [jnp.zeros((width - wide,), LOW), output_bias, shrink_bias]
+    raw = jnp.concatenate([piece.astype(FULL) for piece in pieces]).reshape(8, width)
+    layer_output, input_grad, heads_grad, output_grad, expand_weight_grad, shrink_weight_grad, *_, sums = block_call(
+        lax.axis_size("tensor"),
+        layer_input[0],
+        cotangent[0],
+        heads_rows,
+        output_rows,
+        expand_weight,
+        shrink_weight,
+        raw,
+        block_order,
+    )
+    return (
+        layer_output[None],
+        input_grad[None],
+        sums[0],
+        sums[1],
+        sums[2],
+        sums[3],
+        heads_grad.reshape(heads_weight.shape),
+        sums[6, :wide].reshape(heads_bias.shape),
+        output_grad.reshape(output_weight.shape),
+        sums[4],
+        expand_weight_grad,
+        sums[5],
+        shrink_weight_grad,
+        sums[4],
+    )
+
+
+def ring_local(
     layer_input,
     block_order,
     first_gain,
@@ -250,6 +1335,7 @@
         P(),
         P("replica", "fsdp", None),
     )
+    local = square_local if mesh.shape["fsdp"] == 4 and mesh.shape["replica"] == 2 and mesh.shape["tensor"] == 4 else ring_local
     return jax.shard_map(
         local,
         mesh=mesh,

time: 1490 us -> 309 us (0.21)
  waiting for transfers between devices: 1250 us -> 0 us
  Pallas kernels: 0 us -> 277 us
  matrix products: 119 us -> 0 us
  blocking collectives: 28.7 us -> 0 us
  other arithmetic: 31.3 us -> 4.82 us
  local copies, waits for them, and re-layouts: 42.4 us -> 25.7 us
    reduce_scatter x6 -> x0, waiting for transfers between devices: 527 us -> none  [the longest x1 157 us: local(): lax.psum_scatter(shrink_weight_grad, 'fsdp', scatter_dimension=1, tiled=T...]
    psum x2 -> x0, waiting for transfers between devices: 437 us -> none  [the longest x1 430 us: local(): branch = lax.psum(branch_part, 'tensor')]
    all_gather x6 -> x0, waiting for transfers between devices: 279 us -> none  [the longest x1 71.3 us: local(): lax.all_gather(shrink_weight, 'fsdp', axis=1, tiled=True)]
    pallas_call x0 -> x1, Pallas kernels: none -> 277 us  [block_call(): pl.pallas_call(functools.partial(block_kernel, hd ** (-0.5), line_size),...]
    dot_general x26 -> x0, matrix products: 119 us -> none  [the longest x8 33.7 us: contract_last(): lax.dot_general(left_op, right_op, (((1,), (1,)), ((), ())), preferred_el...]
    psum x1 -> x0, blocking collectives: 28.7 us -> none  [local(): lax.psum((first_gain_grad, first_bias_grad, second_gain_grad, second_bias...]
    reduce_sum x10 -> x0, other arithmetic: 19.7 us -> none  [the longest x2 8.23 us: layer_norm(): return centred * lax.rsqrt(spread_sq + NORM_EPS) * gain_vec + shift_vec]
  transfers between devices with their start and end apart: 14 -> 0, of which waited for: 14 -> 0; matrix products, arithmetic and copies ran while one was open for 11% -> 0% of each run, Pallas kernels for 0% -> 0%
where the time goes in v3:
time: 309 us; the launch traced here: 308 us
  Pallas kernels  277 us (90%)
  local copies, waits for them, and re-layouts  25.7 us (8%)
  other arithmetic  4.82 us (2%)
    pallas_call x1, Pallas kernels, block_call(): pl.pallas_call(functools.partial(block_kernel, hd ** (-0.5), line_size),...  277 us
    unnamed x21, local copies, waits for them, and re-layouts  15.9 us

profile of v3, /device:TPU:0, one launch (start us, length us, event | category | flops | bytes accessed | tf_op | source)
XLA Modules:
  0.0 308.2 jit_solution(7578027179190303923)
XLA Ops:
  0.6 0.7 reshape.51
  1.3 0.7 convert_dynamic-update-slice_fusion.6
  2.0 0.7 convert_dynamic-update-slice_fusion.5
  2.7 0.7 convert_dynamic-update-slice_fusion.4
  3.4 0.7 convert_dynamic-update-slice_fusion.3
  4.1 0.7 convert_dynamic-update-slice_fusion.2
  4.8 0.7 convert_dynamic-update-slice_fusion.1
  5.5 0.7 convert_dynamic-update-slice_fusion
  6.2 0.6 reshape.48.raw
  6.8 2.8 copy.29
  9.6 277.0 %shard_map.254 = (bf16[512,2048]{1,0:T(8,128)(2,1)}, f32[512,2048]{1,0:T(8,128)}, f32[512,1536]{1,0:T(8,128)}, f32[512,512]{1,0:T(8,128)}, f32[512,2048]{1,0:T(8...) custom-call(bf16[512,2048]{1,0:T(8,128)(2,1)} %bitcast.17, ...), custom_call_target="tpu_custom_call" | custom-call | tf_op jit(solution)/shard_map/pallas_call | solution.py:1074
  286.7 0.8 slice_reduce_fusion
  287.5 1.7 fusion
  289.2 0.0 copy-start.5
  289.2 0.6 reshape_squeeze.3
  289.8 0.0 copy-start.3
  289.8 5.3 %reshape.49 = f32[512,2,768]{2,1,0:T(2,128)} reshape(f32[512,1536]{1,0:T(8,128)} %get-tuple-element.24) | data formatting | bytes 6291456 | tf_op jit(solution)/shard_map/reshape | solution.py:1128
  295.1 0.0 copy-done.5
  295.1 0.0 copy-start.2
  295.1 0.6 copy.44
  295.7 0.0 copy-done.3
  295.7 1.3 copy.45
  297.1 1.0 copy-done.2
  298.1 0.0 copy-start.4
  298.1 0.0 copy-start.1
  298.1 2.1 copy.46
  300.2 0.0 copy-done.4
  300.2 1.0 copy.47
  301.2 1.3 copy-done.1
  302.5 0.0 copy-start
  302.5 2.1 copy.48
  304.6 1.6 copy-done
  306.2 2.0 copy.49
  (2 shorter events, 0.0 us)
Async XLA Ops:
  289.2 5.9 %copy-start.5 = (f32[1,2048]{1,0:T(1,128)}, f32[1,2048]{1,0:T(1,128)S(1)}, u32[]{:S(2)}) copy-start(f32[1,2048]{1,0:T(1,128)S(1)} %get-tuple-element.29) | copy-start | bytes 24580
  289.8 5.9 %copy-start.3 = (bf16[512,2048]{1,0:T(8,128)(2,1)S(1)}, bf16[512,2048]{1,0:T(8,128)(2,1)}, u32[]{:S(2)}) copy-start(bf16[512,2048]{1,0:T(8,128)(2,1)} %get-tuple-element.21) | copy-start | bytes 6291460
  295.1 3.0 copy-start.2
  298.1 2.1 copy-start.4
  298.1 4.4 %copy-start.1 = (f32[512,2048]{1,0:T(8,128)S(1)}, f32[512,2048]{1,0:T(8,128)}, u32[]{:S(2)}) copy-start(f32[512,2048]{1,0:T(8,128)} %get-tuple-element.86) | copy-start | bytes 12582916
  302.5 3.7 %copy-start = (f32[2048,512]{1,0:T(8,128)S(1)}, f32[2048,512]{1,0:T(8,128)}, u32[]{:S(2)}) copy-start(f32[2048,512]{1,0:T(8,128)} %get-tuple-element.88) | copy-start | bytes 12582916

commit v4 on v3

--- a/solution.py
+++ b/solution.py
@@ -407,11 +407,12 @@
 
 def block_kernel(
     score_scale, line_size,
-    x_hbm, g_hbm, wh_hbm, wo_hbm, we_own, ws_own, raw, order,
+    x_hbm, g_hbm, wh_hbm, wo_hbm, we_own, ws_own, gain_one, shift_one, gain_two, shift_two, units_bias, heads_bias,
+    bias_one, bias_two, order,
     layer_out, input_grad, heads_grad, output_grad, expand_grad, shrink_grad, we, ws, n2t_hbm, got_core_s, got_core_o,
     got_core_h, got_core_e, red_s, red_o, red_h, sums_out,
     x, g, up, n1, nt, stat, wh, wo, qkv, dctx, ctxt, pg, kvg_got, got_branch, final_branch, got_up, final_up,
-    via_h, got_h, via_o, got_o, via_s, got_s, via_e, got_e, vecs, sums, sums_got, gains, gains_got,
+    via_h, got_h, via_o, got_o, via_s, got_s, via_e, got_e, raw, vecs, sums, sums_got, gains, gains_got,
     loop_sem, block_sem, local_sem, send_sem, recv_sem,
 ):
     links, local = Links(send_sem, recv_sem, line_size), Local(local_sem)
@@ -468,6 +469,15 @@
     heads_in.first()
     heads_in.rest()
 
+    def row(ref):
+        return ref[...].astype(FULL).reshape(1, -1)
+
+    for i, vec in enumerate((gain_one, shift_one, gain_two, shift_two, units_bias)):
+        raw[i : i + 1, :] = row(vec)
+    raw[6:7, :] = row(bias_one) + row(bias_two)
+    head_rows = heads_bias[...].astype(FULL)
+    raw[5:6, : 3 * hd], raw[7:8, : 3 * hd] = head_rows[0:1, :], head_rows[1:2, :]
+
     turns = (3, 1, 2, 0)
 
     def turn_of(n):
@@ -539,7 +549,7 @@
         for i in blocks:
             cols = pl.ds(pl.multiple_of(links.block(i) * unit, unit), unit)
             vecs[0:4, i * unit : (i + 1) * unit] = raw[0:4, cols]
-            vecs[4:5, i * unit : (i + 1) * unit] = raw[6:7, cols] + raw[7:8, cols]
+            vecs[4:5, i * unit : (i + 1) * unit] = raw[6:7, cols]
         local.wait(*x_in)
 
         def norm_rows(c, carry):
@@ -608,11 +618,12 @@
         heads_in.whole()
         output_in.relay()
 
-        own, away = links.yb * 3 * hd, (1 - links.yb) * 3 * hd
-
-        def project(c, start, target):
-            cols = pl.ds(pl.multiple_of(start + c * hd, hd), hd)
-            value = dot(n1[...], wh[:, cols]) + raw[5:6, cols]
+        own = links.yb * 3 * hd
+
+        def project(c, head, target):
+            cols = pl.ds(pl.multiple_of(head * 3 * hd + c * hd, hd), hd)
+            bias = jnp.where(head == 0, raw[5:6, c * hd : (c + 1) * hd], raw[7:8, c * hd : (c + 1) * hd])
+            value = dot(n1[...], wh[:, cols]) + bias
             if c < 2:
                 value = spin(value, cosine[:tokens, :], sines[:tokens, :])
             target[c, :tokens, :] = value.astype(LOW)
@@ -622,14 +633,14 @@
 
         from_y, from_x, from_far = {}, {}, {}
         for c in (1, 2, 0):
-            project(c, away, qkv_away)
+            project(c, 1 - links.yb, qkv_away)
             from_y[c] = links.send(qkv_away.at[c], place_of(c, 1), links.y)
         for c in (1, 2):
-            project(c, own, qkv)
+            project(c, links.yb, qkv)
             from_x[c] = links.send(place_of(c, 0), place_of(c, 2), links.x)
         from_y[1].wait_recv()
         from_far[1] = links.send(place_of(1, 1), place_of(1, 3), links.x)
-        project(0, own, qkv)
+        project(0, links.yb, qkv)
         output_in.share()
         output_in.share_far()
         from_y[2].wait_recv()
@@ -1029,7 +1040,7 @@
     )
 
 
-def block_call(line_size, x, g, heads_rows, output_rows, expand_weight, shrink_weight, raw, order):
+def block_call(line_size, x, g, heads_rows, output_rows, expand_weight, shrink_weight, vectors, order):
     tokens, width = x.shape
     heads_wide, out_wide, units = heads_rows.shape[1], output_rows.shape[0], expand_weight.shape[1]
     hd, unit, half = heads_wide // 6, width // 8, width // 16
@@ -1064,7 +1075,7 @@
         low(2, out_wide, half), low(2, out_wide, unit),
         low(2, units, half), low(2, units, unit),
         low(2, half, units), low(2, unit, units),
-        full(8, width), full(3, 8, width), full(7, 8, width), full(3, 8, width // 2), full(2, 8, width // 2),
+        full(8, width), full(8, width), full(3, 8, width), full(7, 8, width), full(3, 8, width // 2), full(2, 8, width // 2),
         pltpu.SemaphoreType.DMA((3, 2)),
         pltpu.SemaphoreType.DMA((8,)),
         pltpu.SemaphoreType.DMA((320,)),
@@ -1074,13 +1085,13 @@
     return pl.pallas_call(
         functools.partial(block_kernel, hd**-0.5, line_size),
         out_shape=outs,
-        in_specs=[ANY] * 6 + [IN_VMEM, pl.BlockSpec(memory_space=pltpu.SMEM)],
+        in_specs=[ANY] * 6 + [IN_VMEM] * 8 + [pl.BlockSpec(memory_space=pltpu.SMEM)],
         out_specs=[ANY] * 16 + [IN_VMEM],
         scratch_shapes=scratch,
         compiler_params=pltpu.CompilerParams(
             collective_id=0, has_side_effects=True, vmem_limit_bytes=VMEM_BYTES
         ),
-    )(x, g, heads_rows, output_rows, expand_weight, shrink_weight, raw, order)
+    )(x, g, heads_rows, output_rows, expand_weight, shrink_weight, *vectors, order)
 
 
 def square_local(
@@ -1100,14 +1111,10 @@
     shrink_bias,
     cotangent,
 ):
-    width = layer_input.shape[2]
     heads_rows = heads_weight.reshape(heads_weight.shape[0], -1)
     output_rows = output_weight.reshape(-1, output_weight.shape[2])
-    wide = heads_rows.shape[1]
-    pieces = [first_gain, first_bias, second_gain, second_bias, expand_bias, heads_bias.reshape(-1)]
-    pieces += [jnp.zeros((width - wide,), LOW), output_bias, shrink_bias]
-    raw = jnp.concatenate([piece.astype(FULL) for piece in pieces]).reshape(8, width)
-    layer_output, input_grad, heads_grad, output_grad, expand_weight_grad, shrink_weight_grad, *_, sums = block_call(
+    vectors = (first_gain, first_bias, second_gain, second_bias, expand_bias, heads_bias, output_bias, shrink_bias)
+    *results, sums = block_call(
         lax.axis_size("tensor"),
         layer_input[0],
         cotangent[0],
@@ -1115,25 +1122,75 @@
         output_rows,
         expand_weight,
         shrink_weight,
-        raw,
+        vectors,
         block_order,
     )
+    results = store_call(results[:6], sums, heads_weight.shape)
+    layer_output, input_grad, heads_grad, output_grad, expand_grad, shrink_grad = results[:6]
+    first_gain_grad, first_bias_grad, second_gain_grad, second_bias_grad = (vec.reshape(-1) for vec in results[6:10])
+    output_bias_grad, expand_bias_grad, shrink_bias_grad = (vec.reshape(-1) for vec in results[10:13])
     return (
         layer_output[None],
         input_grad[None],
-        sums[0],
-        sums[1],
-        sums[2],
-        sums[3],
-        heads_grad.reshape(heads_weight.shape),
-        sums[6, :wide].reshape(heads_bias.shape),
+        first_gain_grad,
+        first_bias_grad,
+        second_gain_grad,
+        second_bias_grad,
+        heads_grad,
+        results[13],
         output_grad.reshape(output_weight.shape),
-        sums[4],
-        expand_weight_grad,
-        sums[5],
-        shrink_weight_grad,
-        sums[4],
-    )
+        output_bias_grad,
+        expand_grad,
+        expand_bias_grad,
+        shrink_grad,
+        shrink_bias_grad,
+    )
+
+
+def store_kernel(*refs):
+    *full_in, sums = refs[:7]
+    full_out, rows_out, heads_bias_out = refs[7:13], refs[13:20], refs[20]
+    for source, target in zip(full_in, full_out):
+        if len(target.shape) == len(source.shape):
+            target[...] = source[...]
+        else:
+            wide = target.shape[2]
+            for head in range(target.shape[1]):
+                target[:, head, :] = source[:, head * wide : (head + 1) * wide]
+
+    @pl.when(pl.program_id(0) == 0)
+    def _():
+        for row, target in zip((0, 1, 2, 3, 4, 5, 4), rows_out):
+            target[...] = sums[row : row + 1, :]
+        wide = heads_bias_out.shape[1]
+        for head in range(heads_bias_out.shape[0]):
+            heads_bias_out[head : head + 1, :] = sums[6:7, head * wide : (head + 1) * wide]
+
+
+def store_call(results, sums, heads_shape):
+    steps = 2
+    width = sums.shape[1]
+
+    def cut(shape):
+        zeros = (0,) * (len(shape) - 1)
+        return pl.BlockSpec((shape[0] // steps,) + tuple(shape[1:]), lambda i: (i, *zeros))
+
+    def whole(shape):
+        return pl.BlockSpec(tuple(shape), lambda i: (0,) * len(shape))
+
+    kept = [result.shape for result in results]
+    kept[2] = heads_shape
+    rows, heads_bias = (1, width), heads_shape[1:]
+    outs = [jax.ShapeDtypeStruct(shape, result.dtype) for shape, result in zip(kept, results)]
+    outs += [jax.ShapeDtypeStruct(rows, FULL)] * 7 + [jax.ShapeDtypeStruct(heads_bias, FULL)]
+    return pl.pallas_call(
+        store_kernel,
+        grid=(steps,),
+        out_shape=outs,
+        in_specs=[cut(result.shape) for result in results] + [whole(sums.shape)],
+        out_specs=[cut(shape) for shape in kept] + [whole(rows)] * 7 + [whole(heads_bias)],
+        compiler_params=pltpu.CompilerParams(vmem_limit_bytes=VMEM_BYTES),
+    )(*results, sums)
 
 
 def ring_local(

time: 309 us -> 293 us (0.948)
  local copies, waits for them, and re-layouts: 25.7 us -> 2.81 us
  Pallas kernels: 277 us -> 289 us
  other arithmetic: 4.82 us -> 0 us
    unnamed x21 -> x1, local copies, waits for them, and re-layouts: 15.9 us -> 2.81 us
    pallas_call x0 -> x1, Pallas kernels: none -> 11.7 us  [store_call(): pl.pallas_call(store_kernel, grid=(steps,), out_shape=outs, in_specs=[cut...]
    reshape x2 -> x0, local copies, waits for them, and re-layouts: 5.95 us -> none  [the longest x1 5.3 us: square_local(): heads_grad.reshape(heads_weight.shape)]
    unnamed x6 -> x0, other arithmetic: 4.13 us -> none
where the time goes in v4:
time: 293 us; the launch traced here: 292 us
  Pallas kernels  289 us (99%)
    pallas_call x1, Pallas kernels, block_call(): pl.pallas_call(functools.partial(block_kernel, hd ** (-0.5), line_size),...  277 us
    pallas_call x1, Pallas kernels, store_call(): pl.pallas_call(store_kernel, grid=(steps,), out_shape=outs, in_specs=[cut...  11.7 us

profile of v4, /device:TPU:0, one launch (start us, length us, event | category | flops | bytes accessed | tf_op | source)
XLA Modules:
  0.0 292.2 jit_solution(8415527199030996023)
XLA Ops:
  0.6 2.8 copy.29
  3.5 276.8 %shard_map.254 = (bf16[512,2048]{1,0:T(8,128)(2,1)}, f32[512,2048]{1,0:T(8,128)}, f32[512,1536]{1,0:T(8,128)}, f32[512,512]{1,0:T(8,128)}, f32[512,2048]{1,0:T(8...) custom-call(bf16[512,2048]{1,0:T(8,128)(2,1)} %bitcast.16, ...), custom_call_target="tpu_custom_call" | custom-call | tf_op jit(solution)/shard_map/pallas_call | solution.py:1085
  280.3 11.7 %shard_map.255 = (bf16[512,2048]{1,0:T(8,128)(2,1)}, f32[512,2048]{1,0:T(8,128)}, f32[512,2,768]{2,1,0:T(2,128)}, f32[512,512]{1,0:T(8,128)}, f32[512,2048]{1,0:...) custom-call(bf16[512,2048]{1,0:T(8,128)(2,1)} %get-tuple-element.35., ...), custom_call_target="tpu_custom_call" | custom-call | tf_op jit(solution)/shard_map/pallas_call | solution.py:1186

commit v5 on v4

--- a/solution.py
+++ b/solution.py
@@ -64,7 +64,8 @@
 ANY = pl.BlockSpec(memory_space=pl.ANY)
 IN_VMEM = pl.BlockSpec(memory_space=pltpu.VMEM)
 VMEM_BYTES = 63 * 2**20
-COPIES = 224
+COPIES = 157
+LOCALS = 34
 
 
 class Sent:
@@ -152,22 +153,26 @@
 
 class Local:
     def __init__(self, sem):
-        self.sem, self.count, self.open = sem, 0, []
+        self.sem, self.count, self.open, self.free = sem, 0, [], []
 
     def start(self, source, target):
-        copy = pltpu.make_async_copy(source, target, self.sem.at[self.count])
-        self.count += 1
+        if not self.free:
+            self.free.append(self.count)
+            self.count += 1
+        k = self.free.pop(0)
+        copy = pltpu.make_async_copy(source, target, self.sem.at[k])
         copy.start()
-        self.open.append(copy)
+        self.open.append((copy, k))
         return copy
 
     def wait(self, *copies):
         for copy in copies:
             copy.wait()
-            self.open = [other for other in self.open if other is not copy]
+            self.free += [k for other, k in self.open if other is copy]
+            self.open = [pair for pair in self.open if pair[0] is not copy]
 
     def end(self):
-        self.wait(*list(self.open))
+        self.wait(*[copy for copy, _ in self.open])
 
 
 def at_rows(ref, start, size):
@@ -345,7 +350,9 @@
         self.middle = jnp.logical_not(self.outer)
         self.inward = [self.make(c, part, final, links.pair) for c in range(chunks)]
         self.across = [self.make(c, part, got, links.mirror) for c in range(chunks)]
-        self.outward = [self.make(c, final, final, links.pair) for c in range(chunks)]
+        self.outward = [
+            Sent(links, self.inward[c].k, cut(final, c), cut(final, c), links.pair) for c in range(chunks)
+        ]
 
     def make(self, c, source, target, peer):
         return self.links.prepare(self.cut(source, c), self.cut(target, c), peer)
@@ -632,12 +639,12 @@
             return qkv.at[c, pl.ds(part * tokens, tokens), :]
 
         from_y, from_x, from_far = {}, {}, {}
+        for c in (1, 2):
+            project(c, links.yb, qkv)
+            from_x[c] = links.send(place_of(c, 0), place_of(c, 2), links.x)
         for c in (1, 2, 0):
             project(c, 1 - links.yb, qkv_away)
             from_y[c] = links.send(qkv_away.at[c], place_of(c, 1), links.y)
-        for c in (1, 2):
-            project(c, links.yb, qkv)
-            from_x[c] = links.send(place_of(c, 0), place_of(c, 2), links.x)
         from_y[1].wait_recv()
         from_far[1] = links.send(place_of(1, 1), place_of(1, 3), links.x)
         project(0, links.yb, qkv)
@@ -843,7 +850,7 @@
             upstream = final_up[rows, :].astype(FULL)
             inner = upstream - jnp.mean(upstream, -1, keepdims=True)
             inner = inner - normal * jnp.mean(upstream * normal, -1, keepdims=True)
-            grad_rows[slot, :, :] = g[rows, :].astype(FULL) + inner * scale
+            grad_rows[slot, :, :] = (g[rows, :].astype(FULL) + inner * scale).astype(LOW)
             out_copies.append(
                 [local.start(grad_rows.at[slot, :, here(i)], input_grad.at[rows, place[i]]) for i in blocks]
             )
@@ -975,7 +982,7 @@
         expand.direct()
         serve(2)
         half_rows = pl.ds(pl.multiple_of(links.r * unit, unit), unit)
-        column_slots = Slots(total_columns.at[0], total_columns.at[1])
+        column_slots = Slots(*[total_columns.at[n] for n in range(4)])
         serve(2)
         shrink.third(column_slots, shrink_grad.at[:, half_rows], total_columns.shape[1])
         serve(1)
@@ -1000,11 +1007,11 @@
         shared_line(0, pair_share)
         across_share = share_line(1, links.across)
         serve(2)
-        expand_slots = Slots(total_rows.at[0], total_rows.at[1])
+        expand_slots = Slots(*[total_rows.at[n] for n in range(4)])
         expand.third(expand_slots, expand_grad.at[half_rows, :], total_rows.shape[1])
         serve(len(steps) + 4 - serve.done)
         expand_slots.end()
-        total_slots = Slots(*[total_rows.at[n, :, pl.ds(0, heads_wide)] for n in range(2)])
+        total_slots = Slots(*[total_rows.at[n, :, pl.ds(0, heads_wide)] for n in range(4)])
         heads.third(total_slots, heads_grad.at[half_rows, :], total_rows.shape[1])
         output.third(column_slots, output_grad.at[:, half_rows], total_columns.shape[1])
         total_slots.end()
@@ -1017,7 +1024,7 @@
         sums_out[4:8, :] = sums[2, 4:8, :]
         for copy in (*shrink.other, *output.other, *heads.other, *expand.other):
             copy.wait_recv()
-        assert links.count <= COPIES
+        assert links.count <= COPIES and local.count <= LOCALS
         links.end()
         line_branch.end()
         line_up.end()
@@ -1034,9 +1041,9 @@
         low(2, out_wide, unit // 2),
         low(out_wide, unit),
         low(4, unit, units),
-        full(2, unit // 4, units),
-        full(2, out_wide, unit),
-        full(2, 32, width),
+        low(4, unit // 4, units),
+        low(4, out_wide, unit),
+        low(2, 32, width),
     )
 
 
@@ -1049,11 +1056,11 @@
     work = lambda *shape: jax.ShapeDtypeStruct(shape, LOW)
     outs = [
         work(tokens, width),
-        jax.ShapeDtypeStruct((tokens, width), FULL),
-        jax.ShapeDtypeStruct((2 * unit, heads_wide), FULL),
-        jax.ShapeDtypeStruct((out_wide, 2 * unit), FULL),
-        jax.ShapeDtypeStruct((2 * unit, units), FULL),
-        jax.ShapeDtypeStruct((units, 2 * unit), FULL),
+        work(tokens, width),
+        work(2 * unit, heads_wide),
+        work(out_wide, 2 * unit),
+        work(2 * unit, units),
+        work(units, 2 * unit),
         work(width, units),
         work(units, width),
         work(width, tokens),
@@ -1078,7 +1085,7 @@
         full(8, width), full(8, width), full(3, 8, width), full(7, 8, width), full(3, 8, width // 2), full(2, 8, width // 2),
         pltpu.SemaphoreType.DMA((3, 2)),
         pltpu.SemaphoreType.DMA((8,)),
-        pltpu.SemaphoreType.DMA((320,)),
+        pltpu.SemaphoreType.DMA((LOCALS,)),
         pltpu.SemaphoreType.DMA((COPIES,)),
         pltpu.SemaphoreType.DMA((COPIES,)),
     ]
@@ -1152,11 +1159,11 @@
     full_out, rows_out, heads_bias_out = refs[7:13], refs[13:20], refs[20]
     for source, target in zip(full_in, full_out):
         if len(target.shape) == len(source.shape):
-            target[...] = source[...]
+            target[...] = source[...].astype(target.dtype)
         else:
             wide = target.shape[2]
             for head in range(target.shape[1]):
-                target[:, head, :] = source[:, head * wide : (head + 1) * wide]
+                target[:, head, :] = source[:, head * wide : (head + 1) * wide].astype(target.dtype)
 
     @pl.when(pl.program_id(0) == 0)
     def _():
@@ -1181,7 +1188,7 @@
     kept = [result.shape for result in results]
     kept[2] = heads_shape
     rows, heads_bias = (1, width), heads_shape[1:]
-    outs = [jax.ShapeDtypeStruct(shape, result.dtype) for shape, result in zip(kept, results)]
+    outs = [jax.ShapeDtypeStruct(shape, FULL if i else LOW) for i, shape in enumerate(kept)]
     outs += [jax.ShapeDtypeStruct(rows, FULL)] * 7 + [jax.ShapeDtypeStruct(heads_bias, FULL)]
     return pl.pallas_call(
         store_kernel,

time: 293 us -> 285 us (0.973)
  Pallas kernels: 289 us -> 280 us
    pallas_call x1, Pallas kernels: 277 us -> 270 us  [block_call(): pl.pallas_call(functools.partial(block_kernel, hd ** (-0.5), line_size),...]
where the time goes in v5:
time: 285 us; the launch traced here: 284 us
  Pallas kernels  280 us (98%)
    pallas_call x1, Pallas kernels, block_call(): pl.pallas_call(functools.partial(block_kernel, hd ** (-0.5), line_size),...  270 us
    pallas_call x1, Pallas kernels, store_call(): pl.pallas_call(store_kernel, grid=(steps,), out_shape=outs, in_specs=[cut...  10.5 us

profile of v5, /device:TPU:0, one launch (start us, length us, event | category | flops | bytes accessed | tf_op | source)
XLA Modules:
  0.0 284.1 jit_solution(10595602268901905953)
XLA Ops:
  0.6 2.8 copy.29
  3.5 270.0 %shard_map.254 = (bf16[512,2048]{1,0:T(8,128)(2,1)}, bf16[512,2048]{1,0:T(8,128)(2,1)}, bf16[512,1536]{1,0:T(8,128)(2,1)}, bf16[512,512]{1,0:T(8,128)(2,1)}, bf1...) custom-call(bf16[512,2048]{1,0:T(8,128)(2,1)} %bitcast.16, ...), custom_call_target="tpu_custom_call" | custom-call | tf_op jit(solution)/shard_map/pallas_call | solution.py:1092
  273.5 10.5 %shard_map.255 = (bf16[512,2048]{1,0:T(8,128)(2,1)}, f32[512,2048]{1,0:T(8,128)}, f32[512,2,768]{2,1,0:T(2,128)}, f32[512,512]{1,0:T(8,128)}, f32[512,2048]{1,0:...) custom-call(bf16[512,2048]{1,0:T(8,128)(2,1)} %get-tuple-element.35., ...), custom_call_target="tpu_custom_call" | custom-call | tf_op jit(solution)/shard_map/pallas_call | solution.py:1193

commit v6 on v5

--- a/solution.py
+++ b/solution.py
@@ -463,18 +463,18 @@
 
         lax.fori_loop(start, end, one, 0)
 
+    links.meet()
+    heads_in = Gathered(links, local, wh_hbm, wh, at_rows, unit)
+    heads_in.first()
+    heads_in.rest()
     x_in, g_in = [], []
     for i in blocks:
         cols = pl.ds(pl.multiple_of(links.block(i) * unit, unit), unit)
         x_in.append(local.start(x_hbm.at[:, cols], x.at[:, pl.ds(i * unit, unit)]))
         g_in.append(local.start(g_hbm.at[:, cols], g.at[:, pl.ds(i * unit, unit)]))
-    links.meet()
-    heads_in = Gathered(links, local, wh_hbm, wh, at_rows, unit)
     output_in = Gathered(links, local, wo_hbm, wo, at_columns, unit)
     expand = Gathered(links, local, we_own, we, at_rows, unit)
     weight = Gathered(links, local, ws_own, ws, at_columns, unit, False)
-    heads_in.first()
-    heads_in.rest()
 
     def row(ref):
         return ref[...].astype(FULL).reshape(1, -1)
@@ -904,6 +904,7 @@
         serve(1)
         shrink_sum.to_core()
         weight.share_far()
+        serve(1)
         shrink_sum.fetch()
         shrink_sum.add(red_s)
         shrink.first()
@@ -938,7 +939,6 @@
         serve(1)
         stream(4, 8, expand_rows, second_block)
         line_up.start(*range(line_up.chunks))
-        serve(1)
 
         def share(s, peers):
             return [links.send(sums.at[s], sums_got.at[4 * s + k], peer) for k, peer in enumerate(peers)]

time: 285 us -> 284 us (level)
  no operation moved by 1% of the time
where the time goes in v6:
time: 284 us; the launch traced here: 283 us
  Pallas kernels  280 us (99%)
    pallas_call x1, Pallas kernels, block_call(): pl.pallas_call(functools.partial(block_kernel, hd ** (-0.5), line_size),...  269 us
    pallas_call x1, Pallas kernels, store_call(): pl.pallas_call(store_kernel, grid=(steps,), out_shape=outs, in_specs=[cut...  10.5 us

profile of v6, /device:TPU:0, one launch (start us, length us, event | category | flops | bytes accessed | tf_op | source)
XLA Modules:
  0.0 283.2 jit_solution(6730886545569457703)
XLA Ops:
  0.6 2.8 copy.29
  3.5 269.1 %shard_map.254 = (bf16[512,2048]{1,0:T(8,128)(2,1)}, bf16[512,2048]{1,0:T(8,128)(2,1)}, bf16[512,1536]{1,0:T(8,128)(2,1)}, bf16[512,512]{1,0:T(8,128)(2,1)}, bf1...) custom-call(bf16[512,2048]{1,0:T(8,128)(2,1)} %bitcast.16, ...), custom_call_target="tpu_custom_call" | custom-call | tf_op jit(solution)/shard_map/pallas_call | solution.py:1092
  272.6 10.5 %shard_map.255 = (bf16[512,2048]{1,0:T(8,128)(2,1)}, f32[512,2048]{1,0:T(8,128)}, f32[512,2,768]{2,1,0:T(2,128)}, f32[512,512]{1,0:T(8,128)}, f32[512,2048]{1,0:...) custom-call(bf16[512,2048]{1,0:T(8,128)(2,1)} %get-tuple-element.35., ...), custom_call_target="tpu_custom_call" | custom-call | tf_op jit(solution)/shard_map/pallas_call | solution.py:1193

commit v7 on v6

--- a/solution.py
+++ b/solution.py
@@ -419,7 +419,7 @@
     layer_out, input_grad, heads_grad, output_grad, expand_grad, shrink_grad, we, ws, n2t_hbm, got_core_s, got_core_o,
     got_core_h, got_core_e, red_s, red_o, red_h, sums_out,
     x, g, up, n1, nt, stat, wh, wo, qkv, dctx, ctxt, pg, kvg_got, got_branch, final_branch, got_up, final_up,
-    via_h, got_h, via_o, got_o, via_s, got_s, via_e, got_e, raw, vecs, sums, sums_got, gains, gains_got,
+    via_h, got_h, via_o, got_o, via_s, got_s, via_e, got_e, raw, vecs, sums, sums_got, sums_low, gains, gains_got,
     loop_sem, block_sem, local_sem, send_sem, recv_sem,
 ):
     links, local = Links(send_sem, recv_sem, line_size), Local(local_sem)
@@ -961,7 +961,12 @@
         first_share = share(0, [links.core])
         output_sum.to_core()
         shared(0, first_share)
-        second_share = share(1, [links.x, links.y, links.far])
+        halves = [sums[1, :, side * (width // 2) : (side + 1) * (width // 2)] for side in range(2)]
+        sums_low[0, :, :] = jnp.concatenate(halves, 0).astype(LOW)
+        second_share = [
+            links.send(sums_low.at[0], sums_low.at[1 + k], peer)
+            for k, peer in enumerate((links.x, links.y, links.far))
+        ]
         output_sum.fetch()
         output_sum.add(red_o)
         output.first()
@@ -986,7 +991,12 @@
         serve(2)
         shrink.third(column_slots, shrink_grad.at[:, half_rows], total_columns.shape[1])
         serve(1)
-        shared(1, second_share)
+        for copy in second_share:
+            copy.wait_recv()
+        parts = [sums_low[k, :, :].astype(FULL) for k in range(4)]
+        total = (parts[0] + parts[1]) + (parts[2] + parts[3])
+        for side in range(2):
+            sums[2, :, side * (width // 2) : (side + 1) * (width // 2)] = total[8 * side : 8 * side + 8, :]
         for row in range(4):
             for side in range(2):
                 at = 2 * row + side
@@ -1082,7 +1092,7 @@
         low(2, out_wide, half), low(2, out_wide, unit),
         low(2, units, half), low(2, units, unit),
         low(2, half, units), low(2, unit, units),
-        full(8, width), full(8, width), full(3, 8, width), full(7, 8, width), full(3, 8, width // 2), full(2, 8, width // 2),
+        full(8, width), full(8, width), full(3, 8, width), full(1, 8, width), low(4, 16, width // 2), full(3, 8, width // 2), full(2, 8, width // 2),
         pltpu.SemaphoreType.DMA((3, 2)),
         pltpu.SemaphoreType.DMA((8,)),
         pltpu.SemaphoreType.DMA((LOCALS,)),

time: 284 us -> 284 us (level)
  no operation moved by 1% of the time
where the time goes in v7:
time: 284 us; the launch traced here: 283 us
  Pallas kernels  280 us (99%)
    pallas_call x1, Pallas kernels, block_call(): pl.pallas_call(functools.partial(block_kernel, hd ** (-0.5), line_size),...  269 us
    pallas_call x1, Pallas kernels, store_call(): pl.pallas_call(store_kernel, grid=(steps,), out_shape=outs, in_specs=[cut...  10.5 us

profile of v7, /device:TPU:0, one launch (start us, length us, event | category | flops | bytes accessed | tf_op | source)
XLA Modules:
  0.0 283.2 jit_solution(6647727081719739498)
XLA Ops:
  0.6 2.8 copy.29
  3.5 269.1 %shard_map.254 = (bf16[512,2048]{1,0:T(8,128)(2,1)}, bf16[512,2048]{1,0:T(8,128)(2,1)}, bf16[512,1536]{1,0:T(8,128)(2,1)}, bf16[512,512]{1,0:T(8,128)(2,1)}, bf1...) custom-call(bf16[512,2048]{1,0:T(8,128)(2,1)} %bitcast.16, ...), custom_call_target="tpu_custom_call" | custom-call | tf_op jit(solution)/shard_map/pallas_call | solution.py:1102
  272.6 10.5 %shard_map.255 = (bf16[512,2048]{1,0:T(8,128)(2,1)}, f32[512,2048]{1,0:T(8,128)}, f32[512,2,768]{2,1,0:T(2,128)}, f32[512,512]{1,0:T(8,128)}, f32[512,2048]{1,0:...) custom-call(bf16[512,2048]{1,0:T(8,128)(2,1)} %get-tuple-element.35., ...), custom_call_target="tpu_custom_call" | custom-call | tf_op jit(solution)/shard_map/pallas_call | solution.py:1203
